TPU v7x, 256 devices: a whole 4x4x8 slice. The times are simulated.
256 devices in a mesh: row: 8 (over x, z_hi), col: 32 (over y, z_lo, core).
Axes of the slice: x: 4, y: 4, z: 8 (z_hi: 2, z_lo: 4; z = z_hi * 4 + z_lo), core: 2. Of those that a mesh axis runs over, the one named last changes fastest.
Arguments:
- counts: int32 [16384, 32768], P('row', 'col'), may hold values from 0 to 64, as said below
- row_marg: int32 [16384], P('row'), may hold values from 3000 to 299999
- col_marg: int32 [32768], P('col'), may hold values from 3000 to 299999
- log_total: float32 [1], replicated, may hold values from 20 to 22
- row_emb: float32 [16384, 256], P(('row', 'col')), may hold values from -1.5 to 1.5
- row_accum: float32 [16384], P(('row', 'col')), may hold values from 983.04 to 983040
- col_emb: float32 [32768, 256], P(('col', 'row')), may hold values from -1.5 to 1.5
- col_accum: float32 [32768], P(('col', 'row')), may hold values from 491.52 to 491520
Outputs:
- new_row_emb: float32 [16384, 256], P(('row', 'col'))
- new_row_accum: float32 [16384], P(('row', 'col'))
- new_col_emb: float32 [32768, 256], P(('col', 'row'))
- new_col_accum: float32 [32768], P(('col', 'row'))
Inputs may be any that keep to these rules, and one draw needn't show every extreme that they name: About half of the counts are zero; the nonzero ones spread over a range of powers of two.
All inputs are finite; a program needn't handle non-finite values.
Results may differ from a plain program's by a relative error of at most 0.0059.
Values may be sent and summed in bfloat16 or wider, within the bound.
No kernel may reach another device: no remote copies, remote signals or barrier semaphores. Data moves between devices by JAX's collectives and lax.ppermute only.
A program may use at most 64 MiB of HBM per device.

v0:
```python
import jax
import jax.numpy as jnp
from jax import lax
from jax.sharding import PartitionSpec as P

learn_rate = 0.5


def block_slopes(counts, row_vecs, col_vecs, row_marg, col_marg, log_total):
    scores = jnp.dot(row_vecs, col_vecs.T, preferred_element_type=jnp.float32)
    values = counts.astype(jnp.float32)
    shift = (
        log_total[0]
        - jnp.log(row_marg.astype(jnp.float32))[:, None]
        - jnp.log(col_marg.astype(jnp.float32))[None, :]
    )
    present = counts > 0
    target = jnp.log(jnp.where(present, values, 1.0)) + shift
    weight = 0.1 + 0.25 * jnp.sqrt(values)
    slopes = jnp.where(present, weight * (scores - target), jax.nn.sigmoid(scores - shift))
    return slopes.astype(jnp.bfloat16)


def adagrad(embed, accum, grad):
    accum_new = accum + jnp.mean(grad * grad, axis=1)
    return (embed - learn_rate * grad / jnp.sqrt(accum_new)[:, None], accum_new)


def per_device(counts, row_marg, col_marg, log_total, row_emb, row_accum, col_emb, col_accum):
    row_vecs = lax.all_gather(row_emb.astype(jnp.bfloat16), "col", axis=0, tiled=True)
    col_vecs = lax.all_gather(col_emb.astype(jnp.bfloat16), "row", axis=0, tiled=True)
    slopes = block_slopes(counts, row_vecs, col_vecs, row_marg, col_marg, log_total)
    own_rows = row_emb.shape[0]
    own_cols = col_emb.shape[0]
    row_whole = lax.psum(jnp.dot(slopes, col_vecs, preferred_element_type=jnp.float32), "col")
    col_local = lax.dot_general(
        slopes, row_vecs, (((0,), (0,)), ((), ())), preferred_element_type=jnp.float32
    )
    col_whole = lax.psum(col_local, "row")
    row_grad = lax.dynamic_slice_in_dim(row_whole, lax.axis_index("col") * own_rows, own_rows, 0)
    col_grad = lax.dynamic_slice_in_dim(col_whole, lax.axis_index("row") * own_cols, own_cols, 0)
    new_row_emb, new_row_accum = adagrad(row_emb, row_accum, row_grad)
    new_col_emb, new_col_accum = adagrad(col_emb, col_accum, col_grad)
    return (new_row_emb, new_row_accum, new_col_emb, new_col_accum)


def solution(mesh):
    return jax.shard_map(
        per_device,
        mesh=mesh,
        in_specs=(
            P("row", "col"),
            P("row"),
            P("col"),
            P(),
            P(("row", "col"), None),
            P(("row", "col")),
            P(("col", "row"), None),
            P(("col", "row")),
        ),
        out_specs=(
            P(("row", "col"), None),
            P(("row", "col")),
            P(("col", "row"), None),
            P(("col", "row")),
        ),
        check_vma=False,
    )
```

profile of v0, /device:TPU:2, one launch (start us, length us, event | category | flops | bytes accessed | tf_op | source)
XLA Modules:
  0.0 516.9 jit_solution(8052136552310608732)
XLA Ops:
  7.2 0.0 all-gather.2.cloned.1.call-start
  7.2 1.5 convert_element_type.19
  8.7 0.0 all-gather.2.cloned.1.call-update
  8.7 0.0 all-reduce.5.cloned.1.call-start
  8.7 0.9 convert_element_type.20
  10.3 0.7 convert_log_fusion
  11.0 0.7 log_subtract_fusion
  11.7 49.2 %all_gather.7 = bf16[1024,256]{1,0:T(8,128)(2,1)S(1)} all-gather(bf16[128,256]{1,0:T(8,128)(2,1)S(1)} %convert_element_type.20), channel_id=1, replica_groups=mesh['row'=8,'col'=32] {'row'}, dimensions={0}, use_global_device_ids=true | all-gather | bytes 589824 | tf_op jit(solution)/shard_map/all_gather | solution.py:31
  60.9 13.6 %all-gather.2.cloned.1.call-done = bf16[2048,256]{1,0:T(8,128)(2,1)} async-done(((bf16[64,256]{1,0:T(8,128)(2,1)}), bf16[2048,256]{1,0:T(8,128)(2,1)}) %all-gather.2.cloned.1.call-update) | async-done | bytes 1048592 | tf_op jit(solution)/shard_map/all_gather | solution.py:30
  74.5 0.0 copy-start.4
  74.5 13.0 %fusion.3 = bf16[2048,1024]{1,0:T(8,128)(2,1)S(1)} fusion(s32[2048,1024]{1,0:T(8,128)} %param.8, f32[1024]{0:T(1024)S(1)} %convert_log_fusion, f32[2048]{0:T(1024)S(1)} %log_subtract_fusion, bf16[2048,256]{1,0:T(8,128)(2,1)} %all-gather.2.cloned.1.call-done, bf16[1024,256]{1,0:T(8,128)(2,1)S(1)} %all_gather.7), kind=kOutput, calls=%fused_computation.5 | convolution fusion | flops 1105199104 | bytes 14168064 | tf_op jit(solution)/shard_map/dot_general | solution.py:10
  87.5 0.0 copy-start.5
  87.5 1.9 copy-done.5
  89.4 0.0 copy-done.4
  89.4 0.0 copy-start.2
  89.4 0.0 copy-start
  89.4 0.0 copy-start.3
  89.5 0.0 copy-start.1
  89.5 2.3 fusion.11
  91.8 0.0 all-reduce.5.cloned.1.call-update
  91.8 0.0 all-reduce.3.cloned.1.call-start
  91.8 4.8 fusion.10
  96.6 0.0 all-reduce.3.cloned.1.call-update
  96.6 128.0 %all-reduce.5.cloned.1.call-done = f32[1024,256]{1,0:T(8,128)} async-done(((f32[1024,256]{1,0:T(8,128)}), f32[1024,256]{1,0:T(8,128)}) %all-reduce.5.cloned.1.call-update) | async-done | bytes 1048592 | tf_op jit(solution)/shard_map/psum | solution.py:39
  224.6 1.0 multiply_reduce_fusion
  225.6 0.0 copy-done.2
  225.6 0.5 fusion.8
  226.1 0.0 copy-done
  226.1 1.7 divide_subtract_fusion
  227.8 279.6 %all-reduce.3.cloned.1.call-done = f32[2048,256]{1,0:T(8,128)} async-done(((f32[2048,256]{1,0:T(8,128)}), f32[2048,256]{1,0:T(8,128)}) %all-reduce.3.cloned.1.call-update) | async-done | bytes 2097168 | tf_op jit(solution)/shard_map/psum | solution.py:35
  507.4 0.9 multiply_reduce_fusion.1
  508.3 0.0 copy-done.3
  508.3 0.5 fusion.9
  508.8 0.0 copy-done.1
  508.8 1.6 divide_subtract_fusion.1
Async XLA Ops:
  7.2 67.3 %all-gather.2.cloned.1.call-start = ((), (), s32[]{:S(2)}) async-start(), calls=%async_computation | async-start | bytes 1081344 | tf_op jit(solution)/shard_map/all_gather | solution.py:30
  8.7 215.9 %all-reduce.5.cloned.1.call-start = ((), (), s32[]{:S(2)}) async-start(), calls=%async_computation.2 | async-start | bytes 2097152 | tf_op jit(solution)/shard_map/psum | solution.py:39
  74.5 14.9 %copy-start.4 = (bf16[2048,256]{1,0:T(8,128)(2,1)S(1)}, bf16[2048,256]{1,0:T(8,128)(2,1)}, u32[]{:S(2)}) copy-start(bf16[2048,256]{1,0:T(8,128)(2,1)} %all-gather.2.cloned.1.call-done) | copy-start | bytes 3145732
  87.5 1.9 copy-start.5
  89.4 136.2 %copy-start.2 = (f32[128]{0:T(128)S(1)}, f32[128]{0:T(128)}, u32[]{:S(2)}) copy-start(f32[128]{0:T(128)} %param.15) | copy-start | bytes 1540
  89.4 136.7 %copy-start = (f32[128,256]{1,0:T(8,128)S(1)}, f32[128,256]{1,0:T(8,128)}, u32[]{:S(2)}) copy-start(f32[128,256]{1,0:T(8,128)} %param.14) | copy-start | bytes 393220
  89.4 418.9 %copy-start.3 = (f32[64]{0:T(128)S(1)}, f32[64]{0:T(128)}, u32[]{:S(2)}) copy-start(f32[64]{0:T(128)} %param.13) | copy-start | bytes 772
  89.5 419.4 %copy-start.1 = (f32[64,256]{1,0:T(8,128)S(1)}, f32[64,256]{1,0:T(8,128)}, u32[]{:S(2)}) copy-start(f32[64,256]{1,0:T(8,128)} %param.12) | copy-start | bytes 196612
  91.8 415.6 %all-reduce.3.cloned.1.call-start = ((), (), s32[]{:S(2)}) async-start(), calls=%async_computation.1 | async-start | bytes 4194304 | tf_op jit(solution)/shard_map/psum | solution.py:35
Sparse Core Ops, SparseCore 0:
  10.4 64.0 all-gather.1
  91.9 132.6 all-reduce.4
  227.2 280.0 all-reduce.2
where the time goes:
time: 519 us; the launch traced here: 517 us
  waiting for transfers between devices  421 us (81%)
  blocking collectives  49.2 us (9%)
  matrix products  20.1 us (4%)
  between operations  14.5 us (3%)
  other arithmetic  9.97 us (2%)
    psum x1, waiting for transfers between devices, per_device(): lax.psum(jnp.dot(slopes, col_vecs, preferred_element_type=jnp.float32), '...  280 us
    psum x1, waiting for transfers between devices, per_device(): col_whole = lax.psum(col_local, 'row')  128 us
    all_gather x1, blocking collectives, per_device(): lax.all_gather(col_emb.astype(jnp.bfloat16), 'row', axis=0, tiled=True)  49.2 us
    all_gather x1, waiting for transfers between devices, per_device(): lax.all_gather(row_emb.astype(jnp.bfloat16), 'col', axis=0, tiled=True)  13.6 us
    dot_general x1, matrix products, block_slopes(): scores = jnp.dot(row_vecs, col_vecs.T, preferred_element_type=jnp.float32)  13 us
  transfers between devices with their start and end apart: 3, of which 3 were waited for; matrix products, arithmetic and copies ran while one was open for 2% of the time, Pallas kernels for 0%

commit v1 on v0

v1 whole, which is shorter than its diff:
```python
import functools
import jax
import jax.numpy as jnp
from jax import lax
from jax.experimental import pallas as pl
from jax.experimental.pallas import tpu as pltpu
from jax.sharding import PartitionSpec as P

learn_rate = 0.5
LN2 = 0.6931471805599453
D = 256
VM = pl.BlockSpec(memory_space=pltpu.VMEM)


def main_kernel(strip, log_total, c0, c1, c2, c3, row_marg, col_marg,
                r0, r1, r2, r3, r4, r5, r6, r7, k0, k1, k2, k3,
                row_own, row_other, col_own, col_1, col_2, col_3,
                rows, cols, row_log, row_half, col_half, col_acc):
    step = pl.program_id(0)

    @pl.when(step == 0)
    def _():
        for i, piece in enumerate((r0, r1, r2, r3, r4, r5, r6, r7)):
            rows[i] = piece[...]
        for i, piece in enumerate((k0, k1, k2, k3)):
            for j in range(2):
                at = pl.multiple_of(strip[32 + 2 * i + j] * 128, 128)
                cols[pl.ds(at, 128), :] = piece[j * 128:(j + 1) * 128, :]
        row_log[...] = jnp.zeros_like(row_log)
        for i in range(32):
            row_log[i:i + 1, 0:64] = jnp.log(row_marg[pl.ds(strip[i], 1), :].astype(jnp.float32))
        turned = 0.5 * row_log[...].T
        for i in range(32):
            row_half[i // 4, (i % 4) * 64:(i % 4) * 64 + 64, :] = jnp.broadcast_to(turned[0:64, i:i + 1], (64, 128))
        col_half[...] = 0.5 * (jnp.log(col_marg[...].astype(jnp.float32)) - log_total[0])
        col_acc[...] = jnp.zeros_like(col_acc)

    r = rows[step]
    half = r * jnp.bfloat16(0.5)
    shift_r = row_half[step]
    shift_r = jnp.concatenate([shift_r, shift_r], axis=1)
    total = None
    for j in range(4):
        at = slice(j * 256, (j + 1) * 256)
        c = cols[at, :]
        s = lax.dot_general(half, c, (((1,), (1,)), ((), ())), preferred_element_type=jnp.float32)
        x = s + shift_r + col_half[:, at]
        n = jnp.concatenate([ref[:, at] for ref in (c0, c1, c2, c3)], axis=0).astype(jnp.float32)
        present = n > 0.0
        n = jnp.maximum(n, 1.0)
        weight = 0.2 + (0.5 * n) * lax.rsqrt(n)
        far = weight * (x - 0.5 * jnp.log(n))
        near = 0.5 * jnp.tanh(x) + 0.5
        slopes = jnp.where(present, far, near).astype(jnp.bfloat16)
        part = jnp.dot(slopes, c, preferred_element_type=jnp.float32)
        total = part if total is None else total + part
        col_acc[at, :] += lax.dot_general(slopes, r, (((0,), (0,)), ((), ())), preferred_element_type=jnp.float32)

    @pl.when(step < 4)
    def _():
        row_own[...] = total

    @pl.when(step >= 4)
    def _():
        row_other[...] = total.astype(jnp.bfloat16)

    @pl.when(step == 7)
    def _():
        for i, out in enumerate((col_own, col_1, col_2, col_3)):
            for j in range(2):
                at = pl.multiple_of(strip[32 + 2 * i + j] * 128, 128)
                out[j * 128:(j + 1) * 128, :] = col_acc[pl.ds(at, 128), :].astype(out.dtype)


def main_call(strip, log_total, counts, row_marg, col_marg, rows, cols):
    whole = lambda shape: pl.BlockSpec(shape, lambda i, s: (0,) * len(shape))
    f32, bf16 = jnp.float32, jnp.bfloat16
    spec = pltpu.PrefetchScalarGridSpec(
        num_scalar_prefetch=1,
        grid=(8,),
        in_specs=[pl.BlockSpec(memory_space=pltpu.SMEM)]
        + [pl.BlockSpec((64, 1024), functools.partial(lambda k, i, s: (s[4 * i + k], 0), k)) for k in range(4)]
        + [whole((32, 64)), whole((1, 1024))]
        + [whole((256, D))] * 12,
        out_specs=[
            pl.BlockSpec((256, D), lambda i, s: (jnp.minimum(i, 3), 0)),
            pl.BlockSpec((256, D), lambda i, s: (jnp.maximum(i - 4, 0), 0)),
        ] + [whole((256, D))] * 4,
        scratch_shapes=[
            pltpu.VMEM((8, 256, D), bf16),
            pltpu.VMEM((1024, D), bf16),
            pltpu.VMEM((128, 128), f32),
            pltpu.VMEM((8, 256, 128), f32),
            pltpu.VMEM((1, 1024), f32),
            pltpu.VMEM((1024, D), f32),
        ],
    )
    piece = lambda n, t: jax.ShapeDtypeStruct((n, D), t)
    return pl.pallas_call(
        main_kernel,
        grid_spec=spec,
        out_shape=[piece(1024, f32), piece(1024, bf16), piece(256, f32)] + [piece(256, bf16)] * 3,
        compiler_params=pltpu.CompilerParams(vmem_limit_bytes=40 << 20, dimension_semantics=("arbitrary",)),
        cost_estimate=pl.CostEstimate(flops=3 * 2 * 2048 * 1024 * 256, bytes_accessed=12 << 20, transcendentals=6 << 20),
    )(strip, log_total, counts, counts, counts, counts, row_marg, col_marg, *rows, *cols)


def fold_kernel(n, *refs):
    own, got, outs = refs[0], refs[1:1 + n], refs[1 + n:]
    rows = outs[0].shape[0]
    for i, out in enumerate(outs):
        at = slice(i * rows, (i + 1) * rows)
        total = own[at, :]
        for ref in got:
            total = total + ref[at, :].astype(jnp.float32)
        out[...] = total.astype(out.dtype)


def fold(own, got, parts):
    rows = own.shape[0] // parts
    return pl.pallas_call(
        functools.partial(fold_kernel, len(got)),
        in_specs=[VM] * (1 + len(got)),
        out_specs=[VM] * parts,
        out_shape=[jax.ShapeDtypeStruct((rows, D), jnp.float32)]
        + [jax.ShapeDtypeStruct((rows, D), jnp.bfloat16)] * (parts - 1),
        compiler_params=pltpu.CompilerParams(vmem_limit_bytes=16 << 20),
    )(own, *got)


def adagrad_kernel(n, *refs):
    own, got, embed, accum, embed_out, accum_out = refs[0], refs[1:1 + n], *refs[1 + n:]
    rows = own.shape[0]
    grad = own[...]
    for ref in got:
        grad = grad + ref[...].astype(jnp.float32)
    line = jnp.concatenate([accum[...]] * (128 // rows), axis=1)
    column = jnp.broadcast_to(line, (128, 128)).T[0:rows, 0:1]
    new = column + jnp.mean(grad * grad, axis=1, keepdims=True)
    embed_out[...] = embed[...] - learn_rate * grad / jnp.sqrt(new)
    tall = jnp.concatenate([jnp.broadcast_to(new, (rows, 128))] * (128 // rows), axis=0)
    accum_out[...] = tall.T[0:1, 0:rows]


def adagrad(own, got, embed, accum):
    rows = own.shape[0]
    new_embed, new_accum = pl.pallas_call(
        functools.partial(adagrad_kernel, len(got)),
        in_specs=[VM] * (3 + len(got)),
        out_specs=[VM] * 2,
        out_shape=[jax.ShapeDtypeStruct((rows, D), jnp.float32), jax.ShapeDtypeStruct((1, rows), jnp.float32)],
        compiler_params=pltpu.CompilerParams(vmem_limit_bytes=16 << 20),
    )(own, *got, embed, accum.reshape(1, rows))
    return new_embed, new_accum.reshape(rows)


def swap(x, axis, size, flip):
    return lax.ppermute(x, axis, [(i, i ^ flip) for i in range(size)])


def per_device(counts, row_marg, col_marg, log_total, row_emb, row_accum, col_emb, col_accum):
    col_swap = lambda x, flip: swap(x, "col", 32, flip)
    row_swap = lambda x, flip: swap(x, "row", 8, flip)
    me_c, me_r = lax.axis_index("col"), lax.axis_index("row")
    flips = [8 * ky + 2 * kz + kc for kc in range(2) for ky in range(4) for kz in range(4)]
    strip = jnp.concatenate([
        me_c ^ jnp.array(flips, jnp.int32),
        me_r ^ jnp.arange(8, dtype=jnp.int32),
    ])

    col_mine = col_emb.astype(jnp.bfloat16)
    col_pair = jnp.concatenate([col_mine, row_swap(col_mine, 1)], axis=0)
    row_mine = row_emb.astype(jnp.bfloat16)
    row_four = jnp.concatenate([row_mine] + [col_swap(row_mine, 2 * k) for k in (1, 2, 3)], axis=0)
    cols = [col_pair] + [row_swap(col_pair, 2 * k) for k in (1, 2, 3)]
    rows = [row_four] + [col_swap(row_four, 8 * k) for k in (1, 2, 3)]
    rows = rows + [col_swap(x, 1) for x in rows]

    row_own, row_other, col_own, *col_send = main_call(
        strip, log_total, counts, row_marg.reshape(32, 64), col_marg.reshape(1, 1024), rows, cols)

    row_got = col_swap(row_other, 1)
    col_got = [row_swap(x, 2 * k) for k, x in zip((1, 2, 3), col_send)]
    row_own, *row_send = fold(row_own, [row_got], 4)
    row_got = [col_swap(x, 8 * k) for k, x in zip((1, 2, 3), row_send)]
    col_own, col_last = fold(col_own, col_got, 2)
    col_got = [row_swap(col_last, 1)]
    row_own, *row_send = fold(row_own, row_got, 4)
    row_got = [col_swap(x, 2 * k) for k, x in zip((1, 2, 3), row_send)]
    new_col_emb, new_col_accum = adagrad(col_own, col_got, col_emb, col_accum)
    new_row_emb, new_row_accum = adagrad(row_own, row_got, row_emb, row_accum)
    return (new_row_emb, new_row_accum, new_col_emb, new_col_accum)


def solution(mesh):
    return jax.shard_map(
        per_device,
        mesh=mesh,
        in_specs=(
            P("row", "col"),
            P("row"),
            P("col"),
            P(),
            P(("row", "col"), None),
            P(("row", "col")),
            P(("col", "row"), None),
            P(("col", "row")),
        ),
        out_specs=(
            P(("row", "col"), None),
            P(("row", "col")),
            P(("col", "row"), None),
            P(("col", "row")),
        ),
        check_vma=False,
    )
```

time: 519 us -> 73.6 us (0.14)
  waiting for transfers between devices: 421 us -> 11.6 us
  blocking collectives: 49.2 us -> 0 us
  starting transfers between devices: 0.12 us -> 36.6 us
  matrix products: 20.1 us -> 0 us
  Pallas kernels: 0 us -> 15.2 us
  between operations: 14.5 us -> 1.38 us
  other arithmetic: 9.97 us -> 2.52 us
    psum x2 -> x0, waiting for transfers between devices: 408 us -> none  [the longest x1 280 us: per_device(): lax.psum(jnp.dot(slopes, col_vecs, preferred_element_type=jnp.float32), '...]
    all_gather x1 -> x0, blocking collectives: 49.2 us -> none  [per_device(): lax.all_gather(col_emb.astype(jnp.bfloat16), 'row', axis=0, tiled=True)]
    ppermute x0 -> x25, starting transfers between devices: none -> 36.6 us  [swap(): return lax.ppermute(x, axis, [(i, i ^ flip) for i in range(size)])]
    dot_general x3 -> x0, matrix products: 20.1 us -> none  [the longest x1 13 us: block_slopes(): scores = jnp.dot(row_vecs, col_vecs.T, preferred_element_type=jnp.float32)]
    pallas_call x0 -> x6, Pallas kernels: none -> 15.2 us  [the longest x1 13.1 us: main_call(): pl.pallas_call(main_kernel, grid_spec=spec, out_shape=[piece(1024, f32),...]
    all_gather x1 -> x0, waiting for transfers between devices: 13.6 us -> none  [per_device(): lax.all_gather(row_emb.astype(jnp.bfloat16), 'col', axis=0, tiled=True)]
    ppermute x0 -> x25, waiting for transfers between devices: none -> 11.6 us  [swap(): return lax.ppermute(x, axis, [(i, i ^ flip) for i in range(size)])]
  transfers between devices with their start and end apart: 3 -> 25, of which waited for: 3 -> 9; matrix products, arithmetic and copies ran while one was open for 2% -> 3% of each run, Pallas kernels for 0% -> 2%
where the time goes in v1:
time: 73.6 us; the launch traced here: 72.2 us
  starting transfers between devices  36.6 us (50%)
  Pallas kernels  15.2 us (21%)
  waiting for transfers between devices  11.6 us (16%)
  local copies, waits for them, and re-layouts  4.85 us (7%)
  other arithmetic  2.52 us (3%)
  between operations  1.38 us (2%)
    ppermute x25, starting transfers between devices, swap(): return lax.ppermute(x, axis, [(i, i ^ flip) for i in range(size)])  36.6 us
    pallas_call x1, Pallas kernels, main_call(): pl.pallas_call(main_kernel, grid_spec=spec, out_shape=[piece(1024, f32),...  13.1 us
    ppermute x25, waiting for transfers between devices, swap(): return lax.ppermute(x, axis, [(i, i ^ flip) for i in range(size)])  11.6 us
    unnamed x12, local copies, waits for them, and re-layouts  4.08 us
    pallas_call x2, Pallas kernels, adagrad(): pl.pallas_call(functools.partial(adagrad_kernel, len(got)), in_specs=[VM]...  1.8 us
  transfers between devices with their start and end apart: 25, of which 9 were waited for; matrix products, arithmetic and copies ran while one was open for 3% of the time, Pallas kernels for 2%

profile of v1, /device:TPU:2, one launch (start us, length us, event | category | flops | bytes accessed | tf_op | source)
XLA Modules:
  0.0 72.2 jit_solution(3917869394245931209)
XLA Ops:
  0.6 0.8 %convert_element_type.6 = bf16[64,256]{1,0:T(8,128)(2,1)S(1)} convert(f32[64,256]{1,0:T(8,128)} %refs_4_.1) | non-fusion elementwise | flops 16384 | bytes 98304 | tf_op jit(solution)/shard_map/convert_element_type | solution.py:173
  1.5 4.6 %collective-permute-start.2 = (bf16[64,256]{1,0:T(8,128)(2,1)S(1)}, bf16[64,256]{1,0:T(8,128)(2,1)S(1)}, u32[]{:S(2)}, u32[]{:S(2)}) collective-permute-start(bf16[64,256]{1,0:T(8,128)(2,1)S(1)} %convert_element_type.6), channel_id=1, source_target_pairs={{0,6},{1,7},{2,4},{3,5},{4,2},{5,3},{6,0},{7,1},{8,14},{9,15},{10,... | collective-permute-start | bytes 98312 | tf_op jit(solution)/shard_map/ppermute | solution.py:158
  6.1 0.6 collective-permute-start
  6.8 0.9 %convert_element_type.7 = bf16[128,256]{1,0:T(8,128)(2,1)S(1)} convert(f32[128,256]{1,0:T(8,128)} %refs_2_.1) | non-fusion elementwise | flops 32768 | bytes 196608 | tf_op jit(solution)/shard_map/convert_element_type | solution.py:171
  7.7 6.4 %collective-permute-start.10 = (bf16[128,256]{1,0:T(8,128)(2,1)S(1)}, bf16[128,256]{1,0:T(8,128)(2,1)S(1)}, u32[]{:S(2)}, u32[]{:S(2)}) collective-permute-start(bf16[128,256]{1,0:T(8,128)(2,1)S(1)} %convert_element_type.7), channel_id=1, source_target_pairs={{0,32},{32,0},{64,96},{96,64},{128,160},{160,128},{192,224},{224,1... | collective-permute-start | bytes 196616 | tf_op jit(solution)/shard_map/ppermute | solution.py:158
  14.1 0.0 collective-permute-done.1
  14.1 0.0 collective-permute-done
  14.1 0.1 collective-permute-start.6
  14.2 3.1 %collective-permute-start.5 = (bf16[256,256]{1,0:T(8,128)(2,1)S(1)}, bf16[256,256]{1,0:T(8,128)(2,1)S(1)}, u32[]{:S(2)}, u32[]{:S(2)}) collective-permute-start(bf16[256,256]{1,0:T(8,128)(2,1)S(1)} %pad_maximum_fusion.r0), channel_id=1, source_target_pairs={{0,24},{1,25},{2,26},{3,27},{4,28},{5,29},{6,30},{7,31},{8,16},{9,... | collective-permute-start | bytes 393224 | tf_op jit(solution)/shard_map/ppermute | solution.py:158
  17.3 0.6 collective-permute-start.4
  17.9 0.5 collective-permute-start.3
  18.4 1.6 %collective-permute-start.13 = (bf16[256,256]{1,0:T(8,128)(2,1)S(1)}, bf16[256,256]{1,0:T(8,128)(2,1)S(1)}, u32[]{:S(2)}, u32[]{:S(2)}) collective-permute-start(bf16[256,256]{1,0:T(8,128)(2,1)S(1)} %pad_maximum_fusion.1.k0), channel_id=1, source_target_pairs={{0,192},{32,224},{64,128},{96,160},{128,64},{160,96},{192,0},{224,... | collective-permute-start | bytes 393224 | tf_op jit(solution)/shard_map/ppermute | solution.py:158
  20.0 0.7 broadcast_xor_fusion
  20.6 1.1 %collective-permute-start.12 = (bf16[256,256]{1,0:T(8,128)(2,1)S(1)}, bf16[256,256]{1,0:T(8,128)(2,1)S(1)}, u32[]{:S(2)}, u32[]{:S(2)}) collective-permute-start(bf16[256,256]{1,0:T(8,128)(2,1)S(1)} %pad_maximum_fusion.1.k0), channel_id=1, source_target_pairs={{0,128},{32,160},{64,192},{96,224},{128,0},{160,32},{192,64},{224,... | collective-permute-start | bytes 393224 | tf_op jit(solution)/shard_map/ppermute | solution.py:158
  21.7 1.7 %collective-permute-done.5.r3 = bf16[256,256]{1,0:T(8,128)(2,1)S(1)} collective-permute-done((bf16[256,256]{1,0:T(8,128)(2,1)S(1)}, bf16[256,256]{1,0:T(8,128)(2,1)S(1)}, u32[]{:S(2)}, u32[]{:S(2)}) %collective-permute-start.5) | collective-permute-done | bytes 131104 | tf_op jit(solution)/shard_map/ppermute | solution.py:158
  23.4 0.5 collective-permute-start.11
  24.0 1.2 %collective-permute-done.4.r2 = bf16[256,256]{1,0:T(8,128)(2,1)S(1)} collective-permute-done((bf16[256,256]{1,0:T(8,128)(2,1)S(1)}, bf16[256,256]{1,0:T(8,128)(2,1)S(1)}, u32[]{:S(2)}, u32[]{:S(2)}) %collective-permute-start.4) | collective-permute-done | bytes 131104 | tf_op jit(solution)/shard_map/ppermute | solution.py:158
  25.1 0.5 collective-permute-start.8
  25.6 0.1 collective-permute-start.7
  26.4 0.8 %reshape.26.row_marg = s32[32,64]{1,0:T(8,128)S(1)} reshape(s32[2048]{0:T(1024)} %param.10) | data formatting | bytes 16384 | tf_op jit(solution)/shard_map/reshape | solution.py:180
  27.2 0.1 pad_add_fusion.strip
  27.2 0.2 collective-permute-done.12.k2
  27.4 1.6 %collective-permute-done.11.k1 = bf16[256,256]{1,0:T(8,128)(2,1)S(1)} collective-permute-done((bf16[256,256]{1,0:T(8,128)(2,1)S(1)}, bf16[256,256]{1,0:T(8,128)(2,1)S(1)}, u32[]{:S(2)}, u32[]{:S(2)}) %collective-permute-start.11) | collective-permute-done | bytes 131104 | tf_op jit(solution)/shard_map/ppermute | solution.py:158
  29.0 0.0 copy-start
  29.0 3.4 %copy-done = s32[2048,1024]{1,0:T(8,128)S(1)} copy-done((s32[2048,1024]{1,0:T(8,128)S(1)}, s32[2048,1024]{1,0:T(8,128)}, u32[]{:S(2)}) %copy-start) | copy-done | bytes 8388632
  32.4 0.7 copy-done.3
  33.1 13.1 %shard_map.120 = (f32[1024,256]{1,0:T(8,128)S(1)}, bf16[1024,256]{1,0:T(8,128)(2,1)S(1)}, f32[256,256]{1,0:T(8,128)S(1)}, bf16[256,256]{1,0:T(8,128)(2,1)S(1)}, ...) custom-call(s32[40]{0:T(128)S(1)} %pad_add_fusion.strip, f32[1]{0:T(128)S(6)} %copy.13.log_total, ...), custom_call_target="tpu_custom_call" | custom-call | flops 3221225472 | bytes 12582912 | tf_op jit(solution)/shard_map/pallas_call | solution.py:99
  46.2 0.1 collective-permute-start.14
  46.3 0.6 collective-permute-start.21
  46.9 2.4 %collective-permute-start.22 = (bf16[256,256]{1,0:T(8,128)(2,1)S(1)}, bf16[256,256]{1,0:T(8,128)(2,1)S(1)}, u32[]{:S(2)}, u32[]{:S(2)}) collective-permute-start(bf16[256,256]{1,0:T(8,128)(2,1)S(1)} %get-tuple-element.38), channel_id=1, source_target_pairs={{0,128},{32,160},{64,192},{96,224},{128,0},{160,32},{192,64},{224,... | collective-permute-start | bytes 393224 | tf_op jit(solution)/shard_map/ppermute | solution.py:158
  49.3 0.5 collective-permute-start.23
  49.9 0.1 shard_map.121
  50.0 1.6 %collective-permute-start.15 = (bf16[256,256]{1,0:T(8,128)(2,1)S(1)}, bf16[256,256]{1,0:T(8,128)(2,1)S(1)}, u32[]{:S(2)}, u32[]{:S(2)}) collective-permute-start(bf16[256,256]{1,0:T(8,128)(2,1)S(1)} %get-tuple-element.27), channel_id=1, source_target_pairs={{0,8},{1,9},{2,10},{3,11},{4,12},{5,13},{6,14},{7,15},{8,0},{9,1},... | collective-permute-start | bytes 393224 | tf_op jit(solution)/shard_map/ppermute | solution.py:158
  51.6 3.5 %collective-permute-start.16 = (bf16[256,256]{1,0:T(8,128)(2,1)S(1)}, bf16[256,256]{1,0:T(8,128)(2,1)S(1)}, u32[]{:S(2)}, u32[]{:S(2)}) collective-permute-start(bf16[256,256]{1,0:T(8,128)(2,1)S(1)} %get-tuple-element.28), channel_id=1, source_target_pairs={{0,16},{1,17},{2,18},{3,19},{4,20},{5,21},{6,22},{7,23},{8,24},{9,... | collective-permute-start | bytes 393224 | tf_op jit(solution)/shard_map/ppermute | solution.py:158
  55.1 0.8 %collective-permute-start.17 = (bf16[256,256]{1,0:T(8,128)(2,1)S(1)}, bf16[256,256]{1,0:T(8,128)(2,1)S(1)}, u32[]{:S(2)}, u32[]{:S(2)}) collective-permute-start(bf16[256,256]{1,0:T(8,128)(2,1)S(1)} %get-tuple-element.29), channel_id=1, source_target_pairs={{0,24},{1,25},{2,26},{3,27},{4,28},{5,29},{6,30},{7,31},{8,16},{9,... | collective-permute-start | bytes 393224 | tf_op jit(solution)/shard_map/ppermute | solution.py:158
  55.9 0.2 collective-permute-done.22.refs_2_
  56.1 1.4 %collective-permute-done.23.refs_3_ = bf16[256,256]{1,0:T(8,128)(2,1)S(1)} collective-permute-done((bf16[256,256]{1,0:T(8,128)(2,1)S(1)}, bf16[256,256]{1,0:T(8,128)(2,1)S(1)}, u32[]{:S(2)}, u32[]{:S(2)}) %collective-permute-start.23) | collective-permute-done | bytes 131104 | tf_op jit(solution)/shard_map/ppermute | solution.py:158
  57.4 0.1 shard_map.124
  57.5 2.9 %collective-permute-start.24 = (bf16[128,256]{1,0:T(8,128)(2,1)S(1)}, bf16[128,256]{1,0:T(8,128)(2,1)S(1)}, u32[]{:S(2)}, u32[]{:S(2)}) collective-permute-start(bf16[128,256]{1,0:T(8,128)(2,1)S(1)} %get-tuple-element.41), channel_id=1, source_target_pairs={{0,32},{32,0},{64,96},{96,64},{128,160},{160,128},{192,224},{224,1... | collective-permute-start | bytes 196616 | tf_op jit(solution)/shard_map/ppermute | solution.py:158
  60.3 0.6 collective-permute-done.16.refs_2_
  61.0 1.9 %collective-permute-done.17.refs_3_ = bf16[256,256]{1,0:T(8,128)(2,1)S(1)} collective-permute-done((bf16[256,256]{1,0:T(8,128)(2,1)S(1)}, bf16[256,256]{1,0:T(8,128)(2,1)S(1)}, u32[]{:S(2)}, u32[]{:S(2)}) %collective-permute-start.17) | collective-permute-done | bytes 131104 | tf_op jit(solution)/shard_map/ppermute | solution.py:158
  62.9 0.1 shard_map.122
  63.0 0.2 collective-permute-start.18
  63.2 2.4 %collective-permute-start.19 = (bf16[64,256]{1,0:T(8,128)(2,1)S(1)}, bf16[64,256]{1,0:T(8,128)(2,1)S(1)}, u32[]{:S(2)}, u32[]{:S(2)}) collective-permute-start(bf16[64,256]{1,0:T(8,128)(2,1)S(1)} %get-tuple-element.32), channel_id=1, source_target_pairs={{0,4},{1,5},{2,6},{3,7},{4,0},{5,1},{6,2},{7,3},{8,12},{9,13},{10,... | collective-permute-start | bytes 98312 | tf_op jit(solution)/shard_map/ppermute | solution.py:158
  65.5 1.9 %collective-permute-start.20 = (bf16[64,256]{1,0:T(8,128)(2,1)S(1)}, bf16[64,256]{1,0:T(8,128)(2,1)S(1)}, u32[]{:S(2)}, u32[]{:S(2)}) collective-permute-start(bf16[64,256]{1,0:T(8,128)(2,1)S(1)} %get-tuple-element.33), channel_id=1, source_target_pairs={{0,6},{1,7},{2,4},{3,5},{4,2},{5,3},{6,0},{7,1},{8,14},{9,15},{10,... | collective-permute-start | bytes 98312 | tf_op jit(solution)/shard_map/ppermute | solution.py:158
  67.5 0.9 %shard_map.125 = (f32[128,256]{1,0:T(8,128)}, f32[1,128]{1,0:T(1,128)}) custom-call(f32[128,256]{1,0:T(8,128)S(1)} %get-tuple-element.40.refs_0_, bf16[128,256]{1,0:T(8,128)(2,1)S(1)} %collective-permute-done.24.refs_1_, f32[128,256]{1,0:T(8,128)S(1)} %copy-done.1, f32[1,128]{1,0:T(1,128)S(1)} %bitcast.6), custom_call_target="tpu_custom_call" | custom-call | tf_op jit(solution)/shard_map/pallas_call | solution.py:147
  68.4 2.9 %collective-permute-done.20.refs_3_ = bf16[64,256]{1,0:T(8,128)(2,1)S(1)} collective-permute-done((bf16[64,256]{1,0:T(8,128)(2,1)S(1)}, bf16[64,256]{1,0:T(8,128)(2,1)S(1)}, u32[]{:S(2)}, u32[]{:S(2)}) %collective-permute-start.20) | collective-permute-done | bytes 32800 | tf_op jit(solution)/shard_map/ppermute | solution.py:158
  71.3 0.9 %shard_map.123 = (f32[64,256]{1,0:T(8,128)}, f32[1,64]{1,0:T(1,128)}) custom-call(f32[64,256]{1,0:T(8,128)S(1)} %get-tuple-element.30.refs_0_, bf16[64,256]{1,0:T(8,128)(2,1)S(1)} %collective-permute-done.18.refs_1_, bf16[64,256]{1,0:T(8,128)(2,1)S(1)} %collective-permute-done.19.refs_2_, bf16[64,256]{1,0:T(8,128)(2,1)S(1)} %collective-permute-done.20.refs_3_, ...), custom_call_target="tpu_custom_call" | custom-call | tf_op jit(solution)/shard_map/pallas_call | solution.py:147
  (28 shorter events, 0.1 us)
Async XLA Ops:
  1.5 12.6 %collective-permute-start.2 = (bf16[64,256]{1,0:T(8,128)(2,1)S(1)}, bf16[64,256]{1,0:T(8,128)(2,1)S(1)}, u32[]{:S(2)}, u32[]{:S(2)}) collective-permute-start(bf16[64,256]{1,0:T(8,128)(2,1)S(1)} %convert_element_type.6), channel_id=1, source_target_pairs={{0,6},{1,7},{2,4},{3,5},{4,2},{5,3},{6,0},{7,1},{8,14},{9,15},{10,... | collective-permute-start | bytes 98312 | tf_op jit(solution)/shard_map/ppermute | solution.py:158
  6.1 8.0 %collective-permute-start.1 = (bf16[64,256]{1,0:T(8,128)(2,1)S(1)}, bf16[64,256]{1,0:T(8,128)(2,1)S(1)}, u32[]{:S(2)}, u32[]{:S(2)}) collective-permute-start(bf16[64,256]{1,0:T(8,128)(2,1)S(1)} %convert_element_type.6), channel_id=1, source_target_pairs={{0,4},{1,5},{2,6},{3,7},{4,0},{5,1},{6,2},{7,3},{8,12},{9,13},{10,... | collective-permute-start | bytes 98312 | tf_op jit(solution)/shard_map/ppermute | solution.py:158
  6.1 8.0 %collective-permute-start = (bf16[64,256]{1,0:T(8,128)(2,1)S(1)}, bf16[64,256]{1,0:T(8,128)(2,1)S(1)}, u32[]{:S(2)}, u32[]{:S(2)}) collective-permute-start(bf16[64,256]{1,0:T(8,128)(2,1)S(1)} %convert_element_type.6), channel_id=1, source_target_pairs={{0,2},{1,3},{2,0},{3,1},{4,6},{5,7},{6,4},{7,5},{8,10},{9,11},{10,... | collective-permute-start | bytes 98312 | tf_op jit(solution)/shard_map/ppermute | solution.py:158
  7.7 10.7 %collective-permute-start.10 = (bf16[128,256]{1,0:T(8,128)(2,1)S(1)}, bf16[128,256]{1,0:T(8,128)(2,1)S(1)}, u32[]{:S(2)}, u32[]{:S(2)}) collective-permute-start(bf16[128,256]{1,0:T(8,128)(2,1)S(1)} %convert_element_type.7), channel_id=1, source_target_pairs={{0,32},{32,0},{64,96},{96,64},{128,160},{160,128},{192,224},{224,1... | collective-permute-start | bytes 196616 | tf_op jit(solution)/shard_map/ppermute | solution.py:158
  14.1 6.5 %collective-permute-start.6 = (bf16[256,256]{1,0:T(8,128)(2,1)S(1)}, bf16[256,256]{1,0:T(8,128)(2,1)S(1)}, u32[]{:S(2)}, u32[]{:S(2)}) collective-permute-start(bf16[256,256]{1,0:T(8,128)(2,1)S(1)} %pad_maximum_fusion.r0), channel_id=1, source_target_pairs={{0,1},{1,0},{2,3},{3,2},{4,5},{5,4},{6,7},{7,6},{8,9},{9,8},{10,11... | collective-permute-start | bytes 393224 | tf_op jit(solution)/shard_map/ppermute | solution.py:158
  14.2 9.3 %collective-permute-start.5 = (bf16[256,256]{1,0:T(8,128)(2,1)S(1)}, bf16[256,256]{1,0:T(8,128)(2,1)S(1)}, u32[]{:S(2)}, u32[]{:S(2)}) collective-permute-start(bf16[256,256]{1,0:T(8,128)(2,1)S(1)} %pad_maximum_fusion.r0), channel_id=1, source_target_pairs={{0,24},{1,25},{2,26},{3,27},{4,28},{5,29},{6,30},{7,31},{8,16},{9,... | collective-permute-start | bytes 393224 | tf_op jit(solution)/shard_map/ppermute | solution.py:158
  17.3 7.8 %collective-permute-start.4 = (bf16[256,256]{1,0:T(8,128)(2,1)S(1)}, bf16[256,256]{1,0:T(8,128)(2,1)S(1)}, u32[]{:S(2)}, u32[]{:S(2)}) collective-permute-start(bf16[256,256]{1,0:T(8,128)(2,1)S(1)} %pad_maximum_fusion.r0), channel_id=1, source_target_pairs={{0,16},{1,17},{2,18},{3,19},{4,20},{5,21},{6,22},{7,23},{8,24},{9,... | collective-permute-start | bytes 393224 | tf_op jit(solution)/shard_map/ppermute | solution.py:158
  17.9 7.2 %collective-permute-start.3 = (bf16[256,256]{1,0:T(8,128)(2,1)S(1)}, bf16[256,256]{1,0:T(8,128)(2,1)S(1)}, u32[]{:S(2)}, u32[]{:S(2)}) collective-permute-start(bf16[256,256]{1,0:T(8,128)(2,1)S(1)} %pad_maximum_fusion.r0), channel_id=1, source_target_pairs={{0,8},{1,9},{2,10},{3,11},{4,12},{5,13},{6,14},{7,15},{8,0},{9,1},... | collective-permute-start | bytes 393224 | tf_op jit(solution)/shard_map/ppermute | solution.py:158
  18.4 7.3 %collective-permute-start.13 = (bf16[256,256]{1,0:T(8,128)(2,1)S(1)}, bf16[256,256]{1,0:T(8,128)(2,1)S(1)}, u32[]{:S(2)}, u32[]{:S(2)}) collective-permute-start(bf16[256,256]{1,0:T(8,128)(2,1)S(1)} %pad_maximum_fusion.1.k0), channel_id=1, source_target_pairs={{0,192},{32,224},{64,128},{96,160},{128,64},{160,96},{192,0},{224,... | collective-permute-start | bytes 393224 | tf_op jit(solution)/shard_map/ppermute | solution.py:158
  20.6 6.8 %collective-permute-start.12 = (bf16[256,256]{1,0:T(8,128)(2,1)S(1)}, bf16[256,256]{1,0:T(8,128)(2,1)S(1)}, u32[]{:S(2)}, u32[]{:S(2)}) collective-permute-start(bf16[256,256]{1,0:T(8,128)(2,1)S(1)} %pad_maximum_fusion.1.k0), channel_id=1, source_target_pairs={{0,128},{32,160},{64,192},{96,224},{128,0},{160,32},{192,64},{224,... | collective-permute-start | bytes 393224 | tf_op jit(solution)/shard_map/ppermute | solution.py:158
  23.4 5.5 %collective-permute-start.11 = (bf16[256,256]{1,0:T(8,128)(2,1)S(1)}, bf16[256,256]{1,0:T(8,128)(2,1)S(1)}, u32[]{:S(2)}, u32[]{:S(2)}) collective-permute-start(bf16[256,256]{1,0:T(8,128)(2,1)S(1)} %pad_maximum_fusion.1.k0), channel_id=1, source_target_pairs={{0,64},{32,96},{64,0},{96,32},{128,192},{160,224},{192,128},{224,1... | collective-permute-start | bytes 393224 | tf_op jit(solution)/shard_map/ppermute | solution.py:158
  25.1 3.8 %collective-permute-start.9 = (bf16[256,256]{1,0:T(8,128)(2,1)S(1)}, bf16[256,256]{1,0:T(8,128)(2,1)S(1)}, u32[]{:S(2)}, u32[]{:S(2)}) collective-permute-start(bf16[256,256]{1,0:T(8,128)(2,1)S(1)} %collective-permute-done.5.r3), channel_id=1, source_target_pairs={{0,1},{1,0},{2,3},{3,2},{4,5},{5,4},{6,7},{7,6},{8,9},{9,8},{10,11... | collective-permute-start | bytes 393224 | tf_op jit(solution)/shard_map/ppermute | solution.py:158
  25.1 3.8 %collective-permute-start.8 = (bf16[256,256]{1,0:T(8,128)(2,1)S(1)}, bf16[256,256]{1,0:T(8,128)(2,1)S(1)}, u32[]{:S(2)}, u32[]{:S(2)}) collective-permute-start(bf16[256,256]{1,0:T(8,128)(2,1)S(1)} %collective-permute-done.4.r2), channel_id=1, source_target_pairs={{0,1},{1,0},{2,3},{3,2},{4,5},{5,4},{6,7},{7,6},{8,9},{9,8},{10,11... | collective-permute-start | bytes 393224 | tf_op jit(solution)/shard_map/ppermute | solution.py:158
  25.6 3.3 %collective-permute-start.7 = (bf16[256,256]{1,0:T(8,128)(2,1)S(1)}, bf16[256,256]{1,0:T(8,128)(2,1)S(1)}, u32[]{:S(2)}, u32[]{:S(2)}) collective-permute-start(bf16[256,256]{1,0:T(8,128)(2,1)S(1)} %collective-permute-done.3.r1), channel_id=1, source_target_pairs={{0,1},{1,0},{2,3},{3,2},{4,5},{5,4},{6,7},{7,6},{8,9},{9,8},{10,11... | collective-permute-start | bytes 393224 | tf_op jit(solution)/shard_map/ppermute | solution.py:158
  29.0 3.4 %copy-start = (s32[2048,1024]{1,0:T(8,128)S(1)}, s32[2048,1024]{1,0:T(8,128)}, u32[]{:S(2)}) copy-start(s32[2048,1024]{1,0:T(8,128)} %c3.1) | copy-start | bytes 25165828
  32.4 0.7 copy-start.3
  33.1 34.4 %copy-start.1 = (f32[128,256]{1,0:T(8,128)S(1)}, f32[128,256]{1,0:T(8,128)}, u32[]{:S(2)}) copy-start(f32[128,256]{1,0:T(8,128)} %refs_2_.1) | copy-start | bytes 393220
  33.1 34.4 %copy-start.4 = (f32[128]{0:T(128)S(1)}, f32[128]{0:T(128)}, u32[]{:S(2)}) copy-start(f32[128]{0:T(128)} %param.16) | copy-start | bytes 1540
  33.1 38.2 %copy-start.2 = (f32[64,256]{1,0:T(8,128)S(1)}, f32[64,256]{1,0:T(8,128)}, u32[]{:S(2)}) copy-start(f32[64,256]{1,0:T(8,128)} %refs_4_.1) | copy-start | bytes 196612
  33.1 38.2 %copy-start.5 = (f32[64]{0:T(128)S(1)}, f32[64]{0:T(128)}, u32[]{:S(2)}) copy-start(f32[64]{0:T(128)} %param.14) | copy-start | bytes 772
  46.2 3.7 %collective-permute-start.14 = (bf16[1024,256]{1,0:T(8,128)(2,1)S(1)}, bf16[1024,256]{1,0:T(8,128)(2,1)S(1)}, u32[]{:S(2)}, u32[]{:S(2)}) collective-permute-start(bf16[1024,256]{1,0:T(8,128)(2,1)S(1)} %get-tuple-element.25), channel_id=1, source_target_pairs={{0,1},{1,0},{2,3},{3,2},{4,5},{5,4},{6,7},{7,6},{8,9},{9,8},{10,11... | collective-permute-start | bytes 1572872 | tf_op jit(solution)/shard_map/ppermute | solution.py:158
  46.3 8.8 %collective-permute-start.21 = (bf16[256,256]{1,0:T(8,128)(2,1)S(1)}, bf16[256,256]{1,0:T(8,128)(2,1)S(1)}, u32[]{:S(2)}, u32[]{:S(2)}) collective-permute-start(bf16[256,256]{1,0:T(8,128)(2,1)S(1)} %get-tuple-element.37), channel_id=1, source_target_pairs={{0,64},{32,96},{64,0},{96,32},{128,192},{160,224},{192,128},{224,1... | collective-permute-start | bytes 393224 | tf_op jit(solution)/shard_map/ppermute | solution.py:158
  46.9 9.1 %collective-permute-start.22 = (bf16[256,256]{1,0:T(8,128)(2,1)S(1)}, bf16[256,256]{1,0:T(8,128)(2,1)S(1)}, u32[]{:S(2)}, u32[]{:S(2)}) collective-permute-start(bf16[256,256]{1,0:T(8,128)(2,1)S(1)} %get-tuple-element.38), channel_id=1, source_target_pairs={{0,128},{32,160},{64,192},{96,224},{128,0},{160,32},{192,64},{224,... | collective-permute-start | bytes 393224 | tf_op jit(solution)/shard_map/ppermute | solution.py:158
  49.3 8.1 %collective-permute-start.23 = (bf16[256,256]{1,0:T(8,128)(2,1)S(1)}, bf16[256,256]{1,0:T(8,128)(2,1)S(1)}, u32[]{:S(2)}, u32[]{:S(2)}) collective-permute-start(bf16[256,256]{1,0:T(8,128)(2,1)S(1)} %get-tuple-element.39), channel_id=1, source_target_pairs={{0,192},{32,224},{64,128},{96,160},{128,64},{160,96},{192,0},{224,... | collective-permute-start | bytes 393224 | tf_op jit(solution)/shard_map/ppermute | solution.py:158
  50.0 10.3 %collective-permute-start.15 = (bf16[256,256]{1,0:T(8,128)(2,1)S(1)}, bf16[256,256]{1,0:T(8,128)(2,1)S(1)}, u32[]{:S(2)}, u32[]{:S(2)}) collective-permute-start(bf16[256,256]{1,0:T(8,128)(2,1)S(1)} %get-tuple-element.27), channel_id=1, source_target_pairs={{0,8},{1,9},{2,10},{3,11},{4,12},{5,13},{6,14},{7,15},{8,0},{9,1},... | collective-permute-start | bytes 393224 | tf_op jit(solution)/shard_map/ppermute | solution.py:158
  51.6 9.3 %collective-permute-start.16 = (bf16[256,256]{1,0:T(8,128)(2,1)S(1)}, bf16[256,256]{1,0:T(8,128)(2,1)S(1)}, u32[]{:S(2)}, u32[]{:S(2)}) collective-permute-start(bf16[256,256]{1,0:T(8,128)(2,1)S(1)} %get-tuple-element.28), channel_id=1, source_target_pairs={{0,16},{1,17},{2,18},{3,19},{4,20},{5,21},{6,22},{7,23},{8,24},{9,... | collective-permute-start | bytes 393224 | tf_op jit(solution)/shard_map/ppermute | solution.py:158
  55.1 7.8 %collective-permute-start.17 = (bf16[256,256]{1,0:T(8,128)(2,1)S(1)}, bf16[256,256]{1,0:T(8,128)(2,1)S(1)}, u32[]{:S(2)}, u32[]{:S(2)}) collective-permute-start(bf16[256,256]{1,0:T(8,128)(2,1)S(1)} %get-tuple-element.29), channel_id=1, source_target_pairs={{0,24},{1,25},{2,26},{3,27},{4,28},{5,29},{6,30},{7,31},{8,16},{9,... | collective-permute-start | bytes 393224 | tf_op jit(solution)/shard_map/ppermute | solution.py:158
  57.5 10.0 %collective-permute-start.24 = (bf16[128,256]{1,0:T(8,128)(2,1)S(1)}, bf16[128,256]{1,0:T(8,128)(2,1)S(1)}, u32[]{:S(2)}, u32[]{:S(2)}) collective-permute-start(bf16[128,256]{1,0:T(8,128)(2,1)S(1)} %get-tuple-element.41), channel_id=1, source_target_pairs={{0,32},{32,0},{64,96},{96,64},{128,160},{160,128},{192,224},{224,1... | collective-permute-start | bytes 196616 | tf_op jit(solution)/shard_map/ppermute | solution.py:158
  63.0 5.4 %collective-permute-start.18 = (bf16[64,256]{1,0:T(8,128)(2,1)S(1)}, bf16[64,256]{1,0:T(8,128)(2,1)S(1)}, u32[]{:S(2)}, u32[]{:S(2)}) collective-permute-start(bf16[64,256]{1,0:T(8,128)(2,1)S(1)} %get-tuple-element.31), channel_id=1, source_target_pairs={{0,2},{1,3},{2,0},{3,1},{4,6},{5,7},{6,4},{7,5},{8,10},{9,11},{10,... | collective-permute-start | bytes 98312 | tf_op jit(solution)/shard_map/ppermute | solution.py:158
  63.2 5.2 %collective-permute-start.19 = (bf16[64,256]{1,0:T(8,128)(2,1)S(1)}, bf16[64,256]{1,0:T(8,128)(2,1)S(1)}, u32[]{:S(2)}, u32[]{:S(2)}) collective-permute-start(bf16[64,256]{1,0:T(8,128)(2,1)S(1)} %get-tuple-element.32), channel_id=1, source_target_pairs={{0,4},{1,5},{2,6},{3,7},{4,0},{5,1},{6,2},{7,3},{8,12},{9,13},{10,... | collective-permute-start | bytes 98312 | tf_op jit(solution)/shard_map/ppermute | solution.py:158
  65.5 5.7 %collective-permute-start.20 = (bf16[64,256]{1,0:T(8,128)(2,1)S(1)}, bf16[64,256]{1,0:T(8,128)(2,1)S(1)}, u32[]{:S(2)}, u32[]{:S(2)}) collective-permute-start(bf16[64,256]{1,0:T(8,128)(2,1)S(1)} %get-tuple-element.33), channel_id=1, source_target_pairs={{0,6},{1,7},{2,4},{3,5},{4,2},{5,3},{6,0},{7,1},{8,14},{9,15},{10,... | collective-permute-start | bytes 98312 | tf_op jit(solution)/shard_map/ppermute | solution.py:158

commit v2 on v0

v2 whole, which is shorter than its diff:
```python
import functools
import jax
import jax.numpy as jnp
from jax import lax
from jax.experimental import pallas as pl
from jax.experimental.pallas import tpu as pltpu
from jax.sharding import PartitionSpec as P

learn_rate = 0.5
D = 256
f32, bf16 = jnp.float32, jnp.bfloat16
VM = pl.BlockSpec(memory_space=pltpu.VMEM)
SM = pl.BlockSpec(memory_space=pltpu.SMEM)


def call(kernel, outs, ins, in_specs=None, scratch=(), limit=8, cost=None):
    return pl.pallas_call(
        kernel,
        in_specs=in_specs or [VM] * len(ins),
        out_specs=[VM] * len(outs),
        out_shape=[jax.ShapeDtypeStruct(s, t) for s, t in outs],
        scratch_shapes=list(scratch),
        compiler_params=pltpu.CompilerParams(vmem_limit_bytes=limit << 20),
        cost_estimate=cost,
    )(*ins)


def by_core(zero, one):
    core = lax.axis_index("col") % 2
    pl.when(core == 0)(zero)
    pl.when(core == 1)(one)


def first_kernel(row_emb, col_emb, row, col, out, row_buf, col_buf, sem):
    copies = [
        pltpu.make_async_copy(row_emb, row_buf, sem.at[0]),
        pltpu.make_async_copy(col_emb, col_buf, sem.at[1]),
    ]
    for copy in copies:
        copy.start()
    for copy in copies:
        copy.wait()
    row[...] = row_buf[...].astype(bf16)
    col[...] = col_buf[...].astype(bf16)

    def zero():
        out[...] = col_buf[...].astype(bf16)

    def one():
        out[0:64, :] = row_buf[...].astype(bf16)
        out[64:128, :] = jnp.zeros((64, D), bf16)

    by_core(zero, one)


def second_kernel(row, col, got, a, b):
    def zero():
        for out in (a, b):
            out[0:64, :] = row[...]
            out[64:128, :] = got[0:64, :]

    def one():
        a[...] = got[...]
        b[...] = col[...]

    by_core(zero, one)


def third_kernel(token, a, b, g1, g2, g3, out):
    def put(*parts):
        for i, part in enumerate(parts):
            out[i * 128:(i + 1) * 128, :] = part[...]

    by_core(lambda: put(a, g1, g2, g3), lambda: put(a, b, g1, g2))


def tie_kernel(x, *refs):
    refs[-1][...] = x[...]


def tie(x, *after):
    return call(tie_kernel, [(x.shape, x.dtype)], (x, *after))[0]


def slope_parts_kernel(half, after, log_total, row_marg, col_marg, counts, *refs):
    weight, base, token, buf, row_buf, col_buf, sem, row_log, row_half, col_half = refs[after:]
    token[...] = jnp.zeros_like(token)
    me = lax.axis_index("row"), lax.axis_index("col")
    core = me[1] % 2
    group = lambda i: (me[1] // 2) ^ (i + 8 * half)

    def copy(i):
        at = pl.multiple_of(group(i) * 128, 128)
        return pltpu.make_async_copy(counts.at[pl.ds(at, 128), :], buf.at[i], sem.at[i])

    small = [
        pltpu.make_async_copy(row_marg, row_buf, sem.at[8]),
        pltpu.make_async_copy(col_marg, col_buf, sem.at[9]),
    ]
    for one in small:
        one.start()
    for i in range(8):
        copy(i).start()
    row_log[...] = jnp.zeros_like(row_log)
    for one in small:
        one.wait()
    for i in range(8):
        row_log[i:i + 1, :] = jnp.log(row_buf[pl.ds(group(i), 1), :].astype(f32))
    turned = 0.5 * row_log[...].T
    for i in range(8):
        row_half[i] = jnp.broadcast_to(turned[:, i:i + 1], (128, 128))
    col_half[...] = 0.5 * (jnp.log(col_buf[...].astype(f32)) - log_total[0])

    def body(i, carry):
        copy(i).wait()
        first = pl.ds(pl.multiple_of(i * 64 + core * 512, 64), 64)
        second = pl.ds(pl.multiple_of(i * 64 + (1 - core) * 512, 64), 64)
        shift = row_half[i]
        for j in range(8):
            strip = me[0] ^ j
            n = buf[i, :, pl.ds(pl.multiple_of(strip * 128, 128), 128)].astype(f32)
            present = n > 0.0
            n = jnp.maximum(n, 1.0)
            at = slice(j * 128, (j + 1) * 128)
            w = jnp.where(present, 0.2 + (0.5 * n) * lax.rsqrt(n), 0.0)
            b = (shift + col_half[pl.ds(strip, 1), :]) - 0.5 * jnp.log(n)
            weight[first, at] = w[0:64, :]
            weight[second, at] = w[64:128, :]
            base[first, at] = b[0:64, :]
            base[second, at] = b[64:128, :]
        return carry

    lax.fori_loop(0, 8, body, 0)


def slope_parts(half, log_total, row_marg, col_marg, counts, after=()):
    hbm = pl.BlockSpec(memory_space=pltpu.HBM)
    keep = lambda x: pltpu.with_memory_space_constraint(x, pltpu.HBM)
    return call(
        functools.partial(slope_parts_kernel, half, len(after)),
        [((1024, 1024), f32)] * 2 + [((8, 128), f32)],
        (log_total, keep(row_marg.reshape(16, 128)), keep(col_marg.reshape(8, 128)), keep(counts), *after),
        in_specs=[SM, hbm, hbm, hbm] + [VM] * len(after),
        scratch=[
            pltpu.VMEM((8, 128, 1024), jnp.int32),
            pltpu.VMEM((16, 128), jnp.int32),
            pltpu.VMEM((8, 128), jnp.int32),
            pltpu.SemaphoreType.DMA((10,)),
            pltpu.VMEM((128, 128), f32),
            pltpu.VMEM((8, 128, 128), f32),
            pltpu.VMEM((8, 128), f32),
        ],
        limit=8,
        cost=pl.CostEstimate(flops=0, bytes_accessed=10 << 20, transcendentals=2 << 20),
    )


def main_kernel(weight_a, base_a, weight_b, base_b, *refs):
    (mine, got, (row_own, row_other, col_own, col_1, col_2, col_3),
     (rows, cols, row_acc, col_acc)) = refs[0:4], refs[4:8], refs[8:14], refs[14:]

    def gather(row_parts, col_parts, core):
        for i, part in enumerate(row_parts):
            for j in range(4):
                for k in range(2):
                    at = j * 128 + (core ^ k) * 64
                    to = (i // 2) * 1024 + k * 512 + (i % 2) * 256 + j * 64
                    rows[to:to + 64, :] = part[at:at + 64, :]
        for i, part in enumerate(col_parts):
            for j in range(2):
                at = j * 256 + core * 128
                to = i * 256 + j * 128
                cols[to:to + 128, :] = part[at:at + 128, :]

    by_core(lambda: gather(mine, got, 0), lambda: gather(got, mine, 1))
    for j in range(4):
        at = slice(j * 256, (j + 1) * 256)
        c = cols[at, :]
        col = None
        for h, (weight, base) in enumerate(((weight_a, base_a), (weight_b, base_b))):
            here = slice(h * 1024, (h + 1) * 1024)
            r = rows[here, :]
            x = lax.dot_general(r * bf16(0.5), c, (((1,), (1,)), ((), ())), preferred_element_type=f32) + base[:, at]
            w = weight[:, at]
            slopes = jnp.where(w > 0.0, w * x, 0.5 * jnp.tanh(x) + 0.5).astype(bf16)
            part = jnp.dot(slopes, c, preferred_element_type=f32)
            row_acc[here, :] = part if j == 0 else row_acc[here, :] + part
            part = lax.dot_general(slopes, r, (((0,), (0,)), ((), ())), preferred_element_type=f32)
            col = part if col is None else col + part
        (col_own, col_1, col_2, col_3)[j][...] = col.astype(f32 if j == 0 else bf16)
    for h in range(2):
        to = slice(h * 512, (h + 1) * 512)
        row_own[to, :] = row_acc[h * 1024:h * 1024 + 512, :]
        row_other[to, :] = row_acc[h * 1024 + 512:(h + 1) * 1024, :].astype(bf16)


def fold_kernel(n, *refs):
    own, got, outs = refs[0], refs[1:1 + n], refs[1 + n:]
    at = 0
    for out in outs:
        rows = slice(at, at + out.shape[0])
        at += out.shape[0]
        total = own[rows, :]
        for ref in got:
            total = total + ref[rows, :].astype(f32)
        out[...] = total.astype(out.dtype)


def fold(own, got, *parts):
    outs = [((rows, D), bf16 if i else f32) for i, rows in enumerate(parts)]
    return call(functools.partial(fold_kernel, len(got)), outs, (own, *got))


def adagrad_part(grad, embed, accum, embed_out, accum_out):
    rows = embed.shape[0]
    line = jnp.concatenate([accum[...]] * (128 // rows), axis=1)
    column = jnp.broadcast_to(line, (128, 128)).T[0:rows, 0:1]
    new = column + jnp.mean(grad * grad, axis=1, keepdims=True)
    embed_out[...] = embed[...] - learn_rate * grad / jnp.sqrt(new)
    tall = jnp.concatenate([jnp.broadcast_to(new, (rows, 128))] * (128 // rows), axis=0)
    accum_out[...] = tall.T[0:1, 0:rows]


def adagrad_kernel(n, *refs):
    own, got, embed, accum, embed_out, accum_out = refs[0], refs[1:1 + n], *refs[1 + n:]
    grad = own[...]
    for ref in got:
        grad = grad + ref[...].astype(f32)
    adagrad_part(grad, embed, accum, embed_out, accum_out)


def adagrad(own, got, embed, accum):
    rows = own.shape[0]
    new_embed, new_accum = call(
        functools.partial(adagrad_kernel, len(got)),
        [((rows, D), f32), ((1, rows), f32)],
        (own, *got, embed, accum.reshape(1, rows)),
    )
    return new_embed, new_accum.reshape(rows)


def swap(x, axis, size, flip):
    return lax.ppermute(x, axis, [(i, i ^ flip) for i in range(size)])


def hop(x, zero, one):
    pairs = []
    for r in range(8):
        for c in range(32):
            if c % 2 == 0:
                pairs.append((r * 32 + c, r * 32 + (c ^ zero)))
            elif one:
                pairs.append((r * 32 + c, (r ^ one) * 32 + c))
    return lax.ppermute(x, ("row", "col"), pairs)


def per_device(counts, row_marg, col_marg, log_total, row_emb, row_accum, col_emb, col_accum):
    col_swap = lambda x, flip: swap(x, "col", 32, flip)
    row_swap = lambda x, flip: swap(x, "row", 8, flip)
    block = lambda n, t=bf16: ((n, D), t)
    hbm = pl.BlockSpec(memory_space=pltpu.HBM)

    keep = lambda x: pltpu.with_memory_space_constraint(x, pltpu.HBM)
    row, col, out = call(
        first_kernel, [block(64), block(128), block(128)], (keep(row_emb), keep(col_emb)), in_specs=[hbm, hbm],
        scratch=[pltpu.VMEM((64, D), f32), pltpu.VMEM((128, D), f32), pltpu.SemaphoreType.DMA((2,))],
    )
    margs = log_total, row_marg, col_marg, counts
    a, b = call(second_kernel, [block(128)] * 2, (row, col, col_swap(out, 1)))
    near = [hop(a, 2, 1), hop(b, 4, 1), hop(a, 6, 0)]
    weight_a, base_a, token = slope_parts(0, *margs, after=(a,))
    mine = list(call(third_kernel, [block(512)], (token, a, b, *near)))
    mine = mine + [hop(mine[0], 8 * k, 2 * k) for k in (1, 2, 3)]
    weight_b, base_b, token = slope_parts(1, *margs, after=(mine[0],))
    mine = mine[0:1] + [tie(x, token) for x in mine[1:]]
    got = [col_swap(x, 1) for x in mine]

    row_own, row_other, col_own, *col_send = call(
        main_kernel,
        [block(1024, f32), block(1024), block(256, f32)] + [block(256)] * 3,
        (weight_a, base_a, weight_b, base_b, *mine, *got),
        scratch=[pltpu.VMEM((2048, D), bf16), pltpu.VMEM((1024, D), bf16),
                 pltpu.VMEM((2048, D), f32), pltpu.VMEM((1024, D), f32)],
        limit=24,
        cost=pl.CostEstimate(flops=3 << 30, bytes_accessed=16 << 20, transcendentals=2 << 20),
    )

    row_got = col_swap(row_other, 1)
    col_got = [row_swap(x, 2 * k) for k, x in zip((1, 2, 3), col_send)]
    row_own, *row_send = fold(row_own, [row_got], 256, 256, 256, 256)
    row_got = [col_swap(x, 8 * k) for k, x in zip((1, 2, 3), row_send)]
    col_own, col_last = fold(col_own, col_got, 128, 128)
    col_got = [row_swap(col_last, 1)]
    row_own, *row_send = fold(row_own, row_got, 64, 64, 64, 64)
    row_got = [col_swap(x, 2 * k) for k, x in zip((1, 2, 3), row_send)]
    new_col_emb, new_col_accum = adagrad(col_own, col_got, col_emb, col_accum)
    new_row_emb, new_row_accum = adagrad(row_own, row_got, row_emb, row_accum)
    return (new_row_emb, new_row_accum, new_col_emb, new_col_accum)


def solution(mesh):
    return jax.shard_map(
        per_device,
        mesh=mesh,
        in_specs=(
            P("row", "col"),
            P("row"),
            P("col"),
            P(),
            P(("row", "col"), None),
            P(("row", "col")),
            P(("col", "row"), None),
            P(("col", "row")),
        ),
        out_specs=(
            P(("row", "col"), None),
            P(("row", "col")),
            P(("col", "row"), None),
            P(("col", "row")),
        ),
        check_vma=False,
    )
```

time: 519 us -> 63.5 us (0.12)
  waiting for transfers between devices: 421 us -> 14.8 us
  blocking collectives: 49.2 us -> 0 us
  starting transfers between devices: 0.12 us -> 31.3 us
  matrix products: 20.1 us -> 0 us
  Pallas kernels: 0 us -> 14.9 us
  between operations: 14.5 us -> 1.46 us
  other arithmetic: 9.97 us -> 0 us
    psum x2 -> x0, waiting for transfers between devices: 408 us -> none  [the longest x1 280 us: per_device(): lax.psum(jnp.dot(slopes, col_vecs, preferred_element_type=jnp.float32), '...]
    all_gather x1 -> x0, blocking collectives: 49.2 us -> none  [per_device(): lax.all_gather(col_emb.astype(jnp.bfloat16), 'row', axis=0, tiled=True)]
    ppermute x0 -> x22, starting transfers between devices: none -> 31.3 us  [the longest x16 19.3 us: swap(): return lax.ppermute(x, axis, [(i, i ^ flip) for i in range(size)])]
    dot_general x3 -> x0, matrix products: 20.1 us -> none  [the longest x1 13 us: block_slopes(): scores = jnp.dot(row_vecs, col_vecs.T, preferred_element_type=jnp.float32)]
    pallas_call x0 -> x14, Pallas kernels: none -> 14.9 us  [call(): pl.pallas_call(kernel, in_specs=in_specs or [VM] * len(ins), out_specs=[V...]
    ppermute x0 -> x22, waiting for transfers between devices: none -> 14.8 us  [the longest x16 7.94 us: swap(): return lax.ppermute(x, axis, [(i, i ^ flip) for i in range(size)])]
    all_gather x1 -> x0, waiting for transfers between devices: 13.6 us -> none  [per_device(): lax.all_gather(row_emb.astype(jnp.bfloat16), 'col', axis=0, tiled=True)]
  transfers between devices with their start and end apart: 3 -> 22, of which waited for: 3 -> 9; matrix products, arithmetic and copies ran while one was open for 2% -> 0% of each run, Pallas kernels for 0% -> 14%
where the time goes in v2:
time: 63.5 us; the launch traced here: 62.4 us
  starting transfers between devices  31.3 us (49%)
  Pallas kernels  14.9 us (23%)
  waiting for transfers between devices  14.8 us (23%)
  between operations  1.46 us (2%)
    ppermute x16, starting transfers between devices, swap(): return lax.ppermute(x, axis, [(i, i ^ flip) for i in range(size)])  19.3 us
    pallas_call x14, Pallas kernels, call(): pl.pallas_call(kernel, in_specs=in_specs or [VM] * len(ins), out_specs=[V...  14.9 us
    ppermute x6, starting transfers between devices, hop(): return lax.ppermute(x, ('row', 'col'), pairs)  12.1 us
    ppermute x16, waiting for transfers between devices, swap(): return lax.ppermute(x, axis, [(i, i ^ flip) for i in range(size)])  7.94 us
    ppermute x6, waiting for transfers between devices, hop(): return lax.ppermute(x, ('row', 'col'), pairs)  6.82 us
  transfers between devices with their start and end apart: 22, of which 9 were waited for; matrix products, arithmetic and copies ran while one was open for 0% of the time, Pallas kernels for 14%

profile of v2, /device:TPU:2, one launch (start us, length us, event | category | flops | bytes accessed | tf_op | source)
XLA Modules:
  0.0 62.4 jit_solution(16308208084440879705)
XLA Ops:
  0.6 1.0 %shard_map.111 = (bf16[64,256]{1,0:T(8,128)(2,1)S(1)}, bf16[128,256]{1,0:T(8,128)(2,1)S(1)}, bf16[128,256]{1,0:T(8,128)(2,1)S(1)}) custom-call(f32[64,256]{1,0:T(8,128)} %refs_4_.1, f32[128,256]{1,0:T(8,128)} %refs_2_.1), custom_call_target="tpu_custom_call" | custom-call | tf_op jit(solution)/shard_map/pallas_call | solution.py:17
  1.6 0.1 collective-permute-start
  1.7 1.2 %collective-permute-done.got = bf16[128,256]{1,0:T(8,128)(2,1)S(1)} collective-permute-done((bf16[128,256]{1,0:T(8,128)(2,1)S(1)}, bf16[128,256]{1,0:T(8,128)(2,1)S(1)}, u32[]{:S(2)}, u32[]{:S(2)}) %collective-permute-start) | collective-permute-done | bytes 65568 | tf_op jit(solution)/shard_map/ppermute | solution.py:243
  3.0 3.4 %collective-permute-start.2 = (bf16[128,256]{1,0:T(8,128)(2,1)S(1)}, bf16[128,256]{1,0:T(8,128)(2,1)S(1)}, u32[]{:S(2)}, u32[]{:S(2)}) collective-permute-start(bf16[128,256]{1,0:T(8,128)(2,1)S(1)} %get-tuple-element.42.b), channel_id=1, source_target_pairs={{0,4},{1,33},{2,6},{3,35},{4,0},{5,37},{6,2},{7,39},{8,12},{9,41},... | collective-permute-start | bytes 196616 | tf_op jit(solution)/shard_map/ppermute | solution.py:254
  6.3 3.3 %collective-permute-start.3 = (bf16[128,256]{1,0:T(8,128)(2,1)S(1)}, bf16[128,256]{1,0:T(8,128)(2,1)S(1)}, u32[]{:S(2)}, u32[]{:S(2)}) collective-permute-start(bf16[128,256]{1,0:T(8,128)(2,1)S(1)} %get-tuple-element.38.refs_0_.a), channel_id=1, source_target_pairs={{0,6},{2,4},{4,2},{6,0},{8,14},{10,12},{12,10},{14,8},{16,22},{18,... | collective-permute-start | bytes 196616 | tf_op jit(solution)/shard_map/ppermute | solution.py:254
  9.6 0.6 %collective-permute-start.1 = (bf16[128,256]{1,0:T(8,128)(2,1)S(1)}, bf16[128,256]{1,0:T(8,128)(2,1)S(1)}, u32[]{:S(2)}, u32[]{:S(2)}) collective-permute-start(bf16[128,256]{1,0:T(8,128)(2,1)S(1)} %get-tuple-element.38.refs_0_.a), channel_id=1, source_target_pairs={{0,2},{1,33},{2,0},{3,35},{4,6},{5,37},{6,4},{7,39},{8,10},{9,41},... | collective-permute-start | bytes 196616 | tf_op jit(solution)/shard_map/ppermute | solution.py:254
  10.9 3.7 %shard_map.113 = (f32[1024,1024]{1,0:T(8,128)S(1)}, f32[1024,1024]{1,0:T(8,128)S(1)}, f32[8,128]{1,0:T(8,128)S(1)}) custom-call(f32[1]{0:T(128)S(6)} %copy.12.log_total, s32[16,128]{1,0:T(8,128)} %bitcast.8, s32[8,128]{1,0:T(8,128)} %bitcast.10, s32[2048,1024]{1,0:T(8,128)} %counts.3, bf16[128,256]{1,0:T(8,128)(2,1)S(1)} %get-tuple-element.38.refs_0_.a), custom_call_target="tpu_custom_call" | custom-call | bytes 10485760 | tf_op jit(solution)/shard_map/pallas_call | solution.py:17
  14.6 0.0 collective-permute-done.2.g2
  14.6 1.6 %collective-permute-done.1.g1 = bf16[128,256]{1,0:T(8,128)(2,1)S(1)} collective-permute-done((bf16[128,256]{1,0:T(8,128)(2,1)S(1)}, bf16[128,256]{1,0:T(8,128)(2,1)S(1)}, u32[]{:S(2)}, u32[]{:S(2)}) %collective-permute-start.1) | collective-permute-done | bytes 65568 | tf_op jit(solution)/shard_map/ppermute | solution.py:254
  16.3 1.7 %collective-permute-start.4 = (bf16[512,256]{1,0:T(8,128)(2,1)S(1)}, bf16[512,256]{1,0:T(8,128)(2,1)S(1)}, u32[]{:S(2)}, u32[]{:S(2)}) collective-permute-start(bf16[512,256]{1,0:T(8,128)(2,1)S(1)} %shard_map.114.refs_0_), channel_id=1, source_target_pairs={{0,8},{1,65},{2,10},{3,67},{4,12},{5,69},{6,14},{7,71},{8,0},{9,73... | collective-permute-start | bytes 786440 | tf_op jit(solution)/shard_map/ppermute | solution.py:254
  18.0 2.9 %collective-permute-start.5 = (bf16[512,256]{1,0:T(8,128)(2,1)S(1)}, bf16[512,256]{1,0:T(8,128)(2,1)S(1)}, u32[]{:S(2)}, u32[]{:S(2)}) collective-permute-start(bf16[512,256]{1,0:T(8,128)(2,1)S(1)} %shard_map.114.refs_0_), channel_id=1, source_target_pairs={{0,16},{1,129},{2,18},{3,131},{4,20},{5,133},{6,22},{7,135},{8,24}... | collective-permute-start | bytes 786440 | tf_op jit(solution)/shard_map/ppermute | solution.py:254
  20.9 0.2 collective-permute-start.6
  21.1 0.5 collective-permute-start.7
  21.6 3.7 %shard_map.115 = (f32[1024,1024]{1,0:T(8,128)S(1)}, f32[1024,1024]{1,0:T(8,128)S(1)}, f32[8,128]{1,0:T(8,128)S(1)}) custom-call(f32[1]{0:T(128)S(6)} %copy.12.log_total, s32[16,128]{1,0:T(8,128)} %bitcast.9, s32[8,128]{1,0:T(8,128)} %bitcast.11, s32[2048,1024]{1,0:T(8,128)} %counts.3, bf16[512,256]{1,0:T(8,128)(2,1)S(1)} %shard_map.114.refs_0_), custom_call_target="tpu_custom_call" | custom-call | bytes 10485760 | tf_op jit(solution)/shard_map/pallas_call | solution.py:17
  25.3 0.0 collective-permute-done.4.x
  25.3 0.1 collective-permute-start.8
  25.4 2.7 %collective-permute-done.5.x = bf16[512,256]{1,0:T(8,128)(2,1)S(1)} collective-permute-done((bf16[512,256]{1,0:T(8,128)(2,1)S(1)}, bf16[512,256]{1,0:T(8,128)(2,1)S(1)}, u32[]{:S(2)}, u32[]{:S(2)}) %collective-permute-start.5) | collective-permute-done | bytes 262176 | tf_op jit(solution)/shard_map/ppermute | solution.py:254
  28.2 0.2 collective-permute-start.9
  28.3 2.5 %collective-permute-done.6.x = bf16[512,256]{1,0:T(8,128)(2,1)S(1)} collective-permute-done((bf16[512,256]{1,0:T(8,128)(2,1)S(1)}, bf16[512,256]{1,0:T(8,128)(2,1)S(1)}, u32[]{:S(2)}, u32[]{:S(2)}) %collective-permute-start.6) | collective-permute-done | bytes 262176 | tf_op jit(solution)/shard_map/ppermute | solution.py:254
  30.9 0.1 collective-permute-start.10
  31.0 0.0 collective-permute-done.7.refs_4_
  31.0 0.0 collective-permute-done.8.refs_5_
  31.0 1.5 %collective-permute-done.10.refs_7_ = bf16[512,256]{1,0:T(8,128)(2,1)S(1)} collective-permute-done((bf16[512,256]{1,0:T(8,128)(2,1)S(1)}, bf16[512,256]{1,0:T(8,128)(2,1)S(1)}, u32[]{:S(2)}, u32[]{:S(2)}) %collective-permute-start.10) | collective-permute-done | bytes 262176 | tf_op jit(solution)/shard_map/ppermute | solution.py:243
  32.5 4.4 %shard_map.119 = (f32[1024,256]{1,0:T(8,128)S(1)}, bf16[1024,256]{1,0:T(8,128)(2,1)S(1)}, f32[256,256]{1,0:T(8,128)S(1)}, bf16[256,256]{1,0:T(8,128)(2,1)S(1)}, ...) custom-call(f32[1024,1024]{1,0:T(8,128)S(1)} %get-tuple-element.39.weight_a, ...), custom_call_target="tpu_custom_call" | custom-call | flops 3221225472 | bytes 16777216 | tf_op jit(solution)/shard_map/pallas_call | solution.py:17
  36.9 0.2 collective-permute-start.11
  37.1 1.4 %collective-permute-start.18 = (bf16[256,256]{1,0:T(8,128)(2,1)S(1)}, bf16[256,256]{1,0:T(8,128)(2,1)S(1)}, u32[]{:S(2)}, u32[]{:S(2)}) collective-permute-start(bf16[256,256]{1,0:T(8,128)(2,1)S(1)} %get-tuple-element.59), channel_id=1, source_target_pairs={{0,64},{32,96},{64,0},{96,32},{128,192},{160,224},{192,128},{224,1... | collective-permute-start | bytes 393224 | tf_op jit(solution)/shard_map/ppermute | solution.py:243
  38.5 1.7 %collective-permute-start.19 = (bf16[256,256]{1,0:T(8,128)(2,1)S(1)}, bf16[256,256]{1,0:T(8,128)(2,1)S(1)}, u32[]{:S(2)}, u32[]{:S(2)}) collective-permute-start(bf16[256,256]{1,0:T(8,128)(2,1)S(1)} %get-tuple-element.60), channel_id=1, source_target_pairs={{0,128},{32,160},{64,192},{96,224},{128,0},{160,32},{192,64},{224,... | collective-permute-start | bytes 393224 | tf_op jit(solution)/shard_map/ppermute | solution.py:243
  40.2 0.5 collective-permute-start.20
  40.7 0.0 collective-permute-done.11.refs_1_
  40.7 0.1 shard_map.120
  40.8 0.9 %collective-permute-start.12 = (bf16[256,256]{1,0:T(8,128)(2,1)S(1)}, bf16[256,256]{1,0:T(8,128)(2,1)S(1)}, u32[]{:S(2)}, u32[]{:S(2)}) collective-permute-start(bf16[256,256]{1,0:T(8,128)(2,1)S(1)} %get-tuple-element.49), channel_id=1, source_target_pairs={{0,8},{1,9},{2,10},{3,11},{4,12},{5,13},{6,14},{7,15},{8,0},{9,1},... | collective-permute-start | bytes 393224 | tf_op jit(solution)/shard_map/ppermute | solution.py:243
  41.8 2.9 %collective-permute-start.13 = (bf16[256,256]{1,0:T(8,128)(2,1)S(1)}, bf16[256,256]{1,0:T(8,128)(2,1)S(1)}, u32[]{:S(2)}, u32[]{:S(2)}) collective-permute-start(bf16[256,256]{1,0:T(8,128)(2,1)S(1)} %get-tuple-element.50), channel_id=1, source_target_pairs={{0,16},{1,17},{2,18},{3,19},{4,20},{5,21},{6,22},{7,23},{8,24},{9,... | collective-permute-start | bytes 393224 | tf_op jit(solution)/shard_map/ppermute | solution.py:243
  44.7 0.0 collective-permute-done.18.refs_1_
  44.7 1.1 %collective-permute-start.14 = (bf16[256,256]{1,0:T(8,128)(2,1)S(1)}, bf16[256,256]{1,0:T(8,128)(2,1)S(1)}, u32[]{:S(2)}, u32[]{:S(2)}) collective-permute-start(bf16[256,256]{1,0:T(8,128)(2,1)S(1)} %get-tuple-element.51), channel_id=1, source_target_pairs={{0,24},{1,25},{2,26},{3,27},{4,28},{5,29},{6,30},{7,31},{8,16},{9,... | collective-permute-start | bytes 393224 | tf_op jit(solution)/shard_map/ppermute | solution.py:243
  45.8 0.9 %collective-permute-done.19.refs_2_ = bf16[256,256]{1,0:T(8,128)(2,1)S(1)} collective-permute-done((bf16[256,256]{1,0:T(8,128)(2,1)S(1)}, bf16[256,256]{1,0:T(8,128)(2,1)S(1)}, u32[]{:S(2)}, u32[]{:S(2)}) %collective-permute-start.19) | collective-permute-done | bytes 131104 | tf_op jit(solution)/shard_map/ppermute | solution.py:243
  46.7 1.4 %collective-permute-done.20.refs_3_ = bf16[256,256]{1,0:T(8,128)(2,1)S(1)} collective-permute-done((bf16[256,256]{1,0:T(8,128)(2,1)S(1)}, bf16[256,256]{1,0:T(8,128)(2,1)S(1)}, u32[]{:S(2)}, u32[]{:S(2)}) %collective-permute-start.20) | collective-permute-done | bytes 131104 | tf_op jit(solution)/shard_map/ppermute | solution.py:243
  48.1 0.1 shard_map.123
  48.1 5.0 %collective-permute-start.21 = (bf16[128,256]{1,0:T(8,128)(2,1)S(1)}, bf16[128,256]{1,0:T(8,128)(2,1)S(1)}, u32[]{:S(2)}, u32[]{:S(2)}) collective-permute-start(bf16[128,256]{1,0:T(8,128)(2,1)S(1)} %get-tuple-element.63), channel_id=1, source_target_pairs={{0,32},{32,0},{64,96},{96,64},{128,160},{160,128},{192,224},{224,1... | collective-permute-start | bytes 196616 | tf_op jit(solution)/shard_map/ppermute | solution.py:243
  53.2 0.0 collective-permute-done.14.refs_3_
  53.2 0.1 shard_map.121
  53.2 0.9 %collective-permute-start.15 = (bf16[64,256]{1,0:T(8,128)(2,1)S(1)}, bf16[64,256]{1,0:T(8,128)(2,1)S(1)}, u32[]{:S(2)}, u32[]{:S(2)}) collective-permute-start(bf16[64,256]{1,0:T(8,128)(2,1)S(1)} %get-tuple-element.53), channel_id=1, source_target_pairs={{0,2},{1,3},{2,0},{3,1},{4,6},{5,7},{6,4},{7,5},{8,10},{9,11},{10,... | collective-permute-start | bytes 98312 | tf_op jit(solution)/shard_map/ppermute | solution.py:243
  54.2 1.6 %collective-permute-start.16 = (bf16[64,256]{1,0:T(8,128)(2,1)S(1)}, bf16[64,256]{1,0:T(8,128)(2,1)S(1)}, u32[]{:S(2)}, u32[]{:S(2)}) collective-permute-start(bf16[64,256]{1,0:T(8,128)(2,1)S(1)} %get-tuple-element.54), channel_id=1, source_target_pairs={{0,4},{1,5},{2,6},{3,7},{4,0},{5,1},{6,2},{7,3},{8,12},{9,13},{10,... | collective-permute-start | bytes 98312 | tf_op jit(solution)/shard_map/ppermute | solution.py:243
  55.8 1.9 %collective-permute-start.17 = (bf16[64,256]{1,0:T(8,128)(2,1)S(1)}, bf16[64,256]{1,0:T(8,128)(2,1)S(1)}, u32[]{:S(2)}, u32[]{:S(2)}) collective-permute-start(bf16[64,256]{1,0:T(8,128)(2,1)S(1)} %get-tuple-element.55), channel_id=1, source_target_pairs={{0,6},{1,7},{2,4},{3,5},{4,2},{5,3},{6,0},{7,1},{8,14},{9,15},{10,... | collective-permute-start | bytes 98312 | tf_op jit(solution)/shard_map/ppermute | solution.py:243
  57.7 0.0 collective-permute-done.21.refs_1_
  57.7 0.9 %shard_map.124 = (f32[128,256]{1,0:T(8,128)}, f32[1,128]{1,0:T(1,128)}) custom-call(f32[128,256]{1,0:T(8,128)S(1)} %get-tuple-element.62.refs_0_, bf16[128,256]{1,0:T(8,128)(2,1)S(1)} %collective-permute-done.21.refs_1_, f32[128,256]{1,0:T(8,128)S(1)} %copy-done, f32[1,128]{1,0:T(1,128)S(1)} %bitcast.6), custom_call_target="tpu_custom_call" | custom-call | tf_op jit(solution)/shard_map/pallas_call | solution.py:17
  58.6 1.1 %collective-permute-done.16.refs_2_ = bf16[64,256]{1,0:T(8,128)(2,1)S(1)} collective-permute-done((bf16[64,256]{1,0:T(8,128)(2,1)S(1)}, bf16[64,256]{1,0:T(8,128)(2,1)S(1)}, u32[]{:S(2)}, u32[]{:S(2)}) %collective-permute-start.16) | collective-permute-done | bytes 32800 | tf_op jit(solution)/shard_map/ppermute | solution.py:243
  59.7 1.8 %collective-permute-done.17.refs_3_ = bf16[64,256]{1,0:T(8,128)(2,1)S(1)} collective-permute-done((bf16[64,256]{1,0:T(8,128)(2,1)S(1)}, bf16[64,256]{1,0:T(8,128)(2,1)S(1)}, u32[]{:S(2)}, u32[]{:S(2)}) %collective-permute-start.17) | collective-permute-done | bytes 32800 | tf_op jit(solution)/shard_map/ppermute | solution.py:243
  61.5 0.9 %shard_map.122 = (f32[64,256]{1,0:T(8,128)}, f32[1,64]{1,0:T(1,128)}) custom-call(f32[64,256]{1,0:T(8,128)S(1)} %get-tuple-element.52.refs_0_, bf16[64,256]{1,0:T(8,128)(2,1)S(1)} %collective-permute-done.15.refs_1_, bf16[64,256]{1,0:T(8,128)(2,1)S(1)} %collective-permute-done.16.refs_2_, bf16[64,256]{1,0:T(8,128)(2,1)S(1)} %collective-permute-done.17.refs_3_, ...), custom_call_target="tpu_custom_call" | custom-call | tf_op jit(solution)/shard_map/pallas_call | solution.py:17
  (18 shorter events, 0.1 us)
Async XLA Ops:
  1.6 1.3 %collective-permute-start = (bf16[128,256]{1,0:T(8,128)(2,1)S(1)}, bf16[128,256]{1,0:T(8,128)(2,1)S(1)}, u32[]{:S(2)}, u32[]{:S(2)}) collective-permute-start(bf16[128,256]{1,0:T(8,128)(2,1)S(1)} %get-tuple-element.37), channel_id=1, source_target_pairs={{0,1},{1,0},{2,3},{3,2},{4,5},{5,4},{6,7},{7,6},{8,9},{9,8},{10,11... | collective-permute-start | bytes 196616 | tf_op jit(solution)/shard_map/ppermute | solution.py:243
  3.0 11.6 %collective-permute-start.2 = (bf16[128,256]{1,0:T(8,128)(2,1)S(1)}, bf16[128,256]{1,0:T(8,128)(2,1)S(1)}, u32[]{:S(2)}, u32[]{:S(2)}) collective-permute-start(bf16[128,256]{1,0:T(8,128)(2,1)S(1)} %get-tuple-element.42.b), channel_id=1, source_target_pairs={{0,4},{1,33},{2,6},{3,35},{4,0},{5,37},{6,2},{7,39},{8,12},{9,41},... | collective-permute-start | bytes 196616 | tf_op jit(solution)/shard_map/ppermute | solution.py:254
  6.3 8.3 %collective-permute-start.3 = (bf16[128,256]{1,0:T(8,128)(2,1)S(1)}, bf16[128,256]{1,0:T(8,128)(2,1)S(1)}, u32[]{:S(2)}, u32[]{:S(2)}) collective-permute-start(bf16[128,256]{1,0:T(8,128)(2,1)S(1)} %get-tuple-element.38.refs_0_.a), channel_id=1, source_target_pairs={{0,6},{2,4},{4,2},{6,0},{8,14},{10,12},{12,10},{14,8},{16,22},{18,... | collective-permute-start | bytes 196616 | tf_op jit(solution)/shard_map/ppermute | solution.py:254
  9.6 6.7 %collective-permute-start.1 = (bf16[128,256]{1,0:T(8,128)(2,1)S(1)}, bf16[128,256]{1,0:T(8,128)(2,1)S(1)}, u32[]{:S(2)}, u32[]{:S(2)}) collective-permute-start(bf16[128,256]{1,0:T(8,128)(2,1)S(1)} %get-tuple-element.38.refs_0_.a), channel_id=1, source_target_pairs={{0,2},{1,33},{2,0},{3,35},{4,6},{5,37},{6,4},{7,39},{8,10},{9,41},... | collective-permute-start | bytes 196616 | tf_op jit(solution)/shard_map/ppermute | solution.py:254
  16.3 9.0 %collective-permute-start.4 = (bf16[512,256]{1,0:T(8,128)(2,1)S(1)}, bf16[512,256]{1,0:T(8,128)(2,1)S(1)}, u32[]{:S(2)}, u32[]{:S(2)}) collective-permute-start(bf16[512,256]{1,0:T(8,128)(2,1)S(1)} %shard_map.114.refs_0_), channel_id=1, source_target_pairs={{0,8},{1,65},{2,10},{3,67},{4,12},{5,69},{6,14},{7,71},{8,0},{9,73... | collective-permute-start | bytes 786440 | tf_op jit(solution)/shard_map/ppermute | solution.py:254
  18.0 10.2 %collective-permute-start.5 = (bf16[512,256]{1,0:T(8,128)(2,1)S(1)}, bf16[512,256]{1,0:T(8,128)(2,1)S(1)}, u32[]{:S(2)}, u32[]{:S(2)}) collective-permute-start(bf16[512,256]{1,0:T(8,128)(2,1)S(1)} %shard_map.114.refs_0_), channel_id=1, source_target_pairs={{0,16},{1,129},{2,18},{3,131},{4,20},{5,133},{6,22},{7,135},{8,24}... | collective-permute-start | bytes 786440 | tf_op jit(solution)/shard_map/ppermute | solution.py:254
  20.9 10.0 %collective-permute-start.6 = (bf16[512,256]{1,0:T(8,128)(2,1)S(1)}, bf16[512,256]{1,0:T(8,128)(2,1)S(1)}, u32[]{:S(2)}, u32[]{:S(2)}) collective-permute-start(bf16[512,256]{1,0:T(8,128)(2,1)S(1)} %shard_map.114.refs_0_), channel_id=1, source_target_pairs={{0,24},{1,193},{2,26},{3,195},{4,28},{5,197},{6,30},{7,199},{8,16}... | collective-permute-start | bytes 786440 | tf_op jit(solution)/shard_map/ppermute | solution.py:254
  21.1 9.9 %collective-permute-start.7 = (bf16[512,256]{1,0:T(8,128)(2,1)S(1)}, bf16[512,256]{1,0:T(8,128)(2,1)S(1)}, u32[]{:S(2)}, u32[]{:S(2)}) collective-permute-start(bf16[512,256]{1,0:T(8,128)(2,1)S(1)} %shard_map.114.refs_0_), channel_id=1, source_target_pairs={{0,1},{1,0},{2,3},{3,2},{4,5},{5,4},{6,7},{7,6},{8,9},{9,8},{10,11... | collective-permute-start | bytes 786440 | tf_op jit(solution)/shard_map/ppermute | solution.py:243
  25.3 5.6 %collective-permute-start.8 = (bf16[512,256]{1,0:T(8,128)(2,1)S(1)}, bf16[512,256]{1,0:T(8,128)(2,1)S(1)}, u32[]{:S(2)}, u32[]{:S(2)}) collective-permute-start(bf16[512,256]{1,0:T(8,128)(2,1)S(1)} %shard_map.116.refs_1_), channel_id=1, source_target_pairs={{0,1},{1,0},{2,3},{3,2},{4,5},{5,4},{6,7},{7,6},{8,9},{9,8},{10,11... | collective-permute-start | bytes 786440 | tf_op jit(solution)/shard_map/ppermute | solution.py:243
  28.2 2.8 %collective-permute-start.9 = (bf16[512,256]{1,0:T(8,128)(2,1)S(1)}, bf16[512,256]{1,0:T(8,128)(2,1)S(1)}, u32[]{:S(2)}, u32[]{:S(2)}) collective-permute-start(bf16[512,256]{1,0:T(8,128)(2,1)S(1)} %shard_map.117.refs_2_), channel_id=1, source_target_pairs={{0,1},{1,0},{2,3},{3,2},{4,5},{5,4},{6,7},{7,6},{8,9},{9,8},{10,11... | collective-permute-start | bytes 786440 | tf_op jit(solution)/shard_map/ppermute | solution.py:243
  30.9 1.6 %collective-permute-start.10 = (bf16[512,256]{1,0:T(8,128)(2,1)S(1)}, bf16[512,256]{1,0:T(8,128)(2,1)S(1)}, u32[]{:S(2)}, u32[]{:S(2)}) collective-permute-start(bf16[512,256]{1,0:T(8,128)(2,1)S(1)} %shard_map.118.refs_3_), channel_id=1, source_target_pairs={{0,1},{1,0},{2,3},{3,2},{4,5},{5,4},{6,7},{7,6},{8,9},{9,8},{10,11... | collective-permute-start | bytes 786440 | tf_op jit(solution)/shard_map/ppermute | solution.py:243
  32.5 25.2 %copy-start = (f32[128,256]{1,0:T(8,128)S(1)}, f32[128,256]{1,0:T(8,128)}, u32[]{:S(2)}) copy-start(f32[128,256]{1,0:T(8,128)} %refs_2_.1) | copy-start | bytes 393220
  32.5 25.2 %copy-start.2 = (f32[128]{0:T(128)S(1)}, f32[128]{0:T(128)}, u32[]{:S(2)}) copy-start(f32[128]{0:T(128)} %param.15) | copy-start | bytes 1540
  32.5 29.0 %copy-start.1 = (f32[64,256]{1,0:T(8,128)S(1)}, f32[64,256]{1,0:T(8,128)}, u32[]{:S(2)}) copy-start(f32[64,256]{1,0:T(8,128)} %refs_4_.1) | copy-start | bytes 196612
  32.5 29.0 %copy-start.3 = (f32[64]{0:T(128)S(1)}, f32[64]{0:T(128)}, u32[]{:S(2)}) copy-start(f32[64]{0:T(128)} %param.13) | copy-start | bytes 772
  36.9 3.9 %collective-permute-start.11 = (bf16[1024,256]{1,0:T(8,128)(2,1)S(1)}, bf16[1024,256]{1,0:T(8,128)(2,1)S(1)}, u32[]{:S(2)}, u32[]{:S(2)}) collective-permute-start(bf16[1024,256]{1,0:T(8,128)(2,1)S(1)} %get-tuple-element.47), channel_id=1, source_target_pairs={{0,1},{1,0},{2,3},{3,2},{4,5},{5,4},{6,7},{7,6},{8,9},{9,8},{10,11... | collective-permute-start | bytes 1572872 | tf_op jit(solution)/shard_map/ppermute | solution.py:243
  37.1 7.6 %collective-permute-start.18 = (bf16[256,256]{1,0:T(8,128)(2,1)S(1)}, bf16[256,256]{1,0:T(8,128)(2,1)S(1)}, u32[]{:S(2)}, u32[]{:S(2)}) collective-permute-start(bf16[256,256]{1,0:T(8,128)(2,1)S(1)} %get-tuple-element.59), channel_id=1, source_target_pairs={{0,64},{32,96},{64,0},{96,32},{128,192},{160,224},{192,128},{224,1... | collective-permute-start | bytes 393224 | tf_op jit(solution)/shard_map/ppermute | solution.py:243
  38.5 8.2 %collective-permute-start.19 = (bf16[256,256]{1,0:T(8,128)(2,1)S(1)}, bf16[256,256]{1,0:T(8,128)(2,1)S(1)}, u32[]{:S(2)}, u32[]{:S(2)}) collective-permute-start(bf16[256,256]{1,0:T(8,128)(2,1)S(1)} %get-tuple-element.60), channel_id=1, source_target_pairs={{0,128},{32,160},{64,192},{96,224},{128,0},{160,32},{192,64},{224,... | collective-permute-start | bytes 393224 | tf_op jit(solution)/shard_map/ppermute | solution.py:243
  40.2 7.9 %collective-permute-start.20 = (bf16[256,256]{1,0:T(8,128)(2,1)S(1)}, bf16[256,256]{1,0:T(8,128)(2,1)S(1)}, u32[]{:S(2)}, u32[]{:S(2)}) collective-permute-start(bf16[256,256]{1,0:T(8,128)(2,1)S(1)} %get-tuple-element.61), channel_id=1, source_target_pairs={{0,192},{32,224},{64,128},{96,160},{128,64},{160,96},{192,0},{224,... | collective-permute-start | bytes 393224 | tf_op jit(solution)/shard_map/ppermute | solution.py:243
  40.8 12.3 %collective-permute-start.12 = (bf16[256,256]{1,0:T(8,128)(2,1)S(1)}, bf16[256,256]{1,0:T(8,128)(2,1)S(1)}, u32[]{:S(2)}, u32[]{:S(2)}) collective-permute-start(bf16[256,256]{1,0:T(8,128)(2,1)S(1)} %get-tuple-element.49), channel_id=1, source_target_pairs={{0,8},{1,9},{2,10},{3,11},{4,12},{5,13},{6,14},{7,15},{8,0},{9,1},... | collective-permute-start | bytes 393224 | tf_op jit(solution)/shard_map/ppermute | solution.py:243
  41.8 11.4 %collective-permute-start.13 = (bf16[256,256]{1,0:T(8,128)(2,1)S(1)}, bf16[256,256]{1,0:T(8,128)(2,1)S(1)}, u32[]{:S(2)}, u32[]{:S(2)}) collective-permute-start(bf16[256,256]{1,0:T(8,128)(2,1)S(1)} %get-tuple-element.50), channel_id=1, source_target_pairs={{0,16},{1,17},{2,18},{3,19},{4,20},{5,21},{6,22},{7,23},{8,24},{9,... | collective-permute-start | bytes 393224 | tf_op jit(solution)/shard_map/ppermute | solution.py:243
  44.7 8.5 %collective-permute-start.14 = (bf16[256,256]{1,0:T(8,128)(2,1)S(1)}, bf16[256,256]{1,0:T(8,128)(2,1)S(1)}, u32[]{:S(2)}, u32[]{:S(2)}) collective-permute-start(bf16[256,256]{1,0:T(8,128)(2,1)S(1)} %get-tuple-element.51), channel_id=1, source_target_pairs={{0,24},{1,25},{2,26},{3,27},{4,28},{5,29},{6,30},{7,31},{8,16},{9,... | collective-permute-start | bytes 393224 | tf_op jit(solution)/shard_map/ppermute | solution.py:243
  48.1 9.6 %collective-permute-start.21 = (bf16[128,256]{1,0:T(8,128)(2,1)S(1)}, bf16[128,256]{1,0:T(8,128)(2,1)S(1)}, u32[]{:S(2)}, u32[]{:S(2)}) collective-permute-start(bf16[128,256]{1,0:T(8,128)(2,1)S(1)} %get-tuple-element.63), channel_id=1, source_target_pairs={{0,32},{32,0},{64,96},{96,64},{128,160},{160,128},{192,224},{224,1... | collective-permute-start | bytes 196616 | tf_op jit(solution)/shard_map/ppermute | solution.py:243
  53.2 5.4 %collective-permute-start.15 = (bf16[64,256]{1,0:T(8,128)(2,1)S(1)}, bf16[64,256]{1,0:T(8,128)(2,1)S(1)}, u32[]{:S(2)}, u32[]{:S(2)}) collective-permute-start(bf16[64,256]{1,0:T(8,128)(2,1)S(1)} %get-tuple-element.53), channel_id=1, source_target_pairs={{0,2},{1,3},{2,0},{3,1},{4,6},{5,7},{6,4},{7,5},{8,10},{9,11},{10,... | collective-permute-start | bytes 98312 | tf_op jit(solution)/shard_map/ppermute | solution.py:243
  54.2 5.5 %collective-permute-start.16 = (bf16[64,256]{1,0:T(8,128)(2,1)S(1)}, bf16[64,256]{1,0:T(8,128)(2,1)S(1)}, u32[]{:S(2)}, u32[]{:S(2)}) collective-permute-start(bf16[64,256]{1,0:T(8,128)(2,1)S(1)} %get-tuple-element.54), channel_id=1, source_target_pairs={{0,4},{1,5},{2,6},{3,7},{4,0},{5,1},{6,2},{7,3},{8,12},{9,13},{10,... | collective-permute-start | bytes 98312 | tf_op jit(solution)/shard_map/ppermute | solution.py:243
  55.8 5.7 %collective-permute-start.17 = (bf16[64,256]{1,0:T(8,128)(2,1)S(1)}, bf16[64,256]{1,0:T(8,128)(2,1)S(1)}, u32[]{:S(2)}, u32[]{:S(2)}) collective-permute-start(bf16[64,256]{1,0:T(8,128)(2,1)S(1)} %get-tuple-element.55), channel_id=1, source_target_pairs={{0,6},{1,7},{2,4},{3,5},{4,2},{5,3},{6,0},{7,1},{8,14},{9,15},{10,... | collective-permute-start | bytes 98312 | tf_op jit(solution)/shard_map/ppermute | solution.py:243

commit v3 on v2

--- a/solution.py
+++ b/solution.py
@@ -160,13 +160,13 @@
      (rows, cols, row_acc, col_acc)) = refs[0:4], refs[4:8], refs[8:14], refs[14:]
 
     def gather(row_parts, col_parts, core):
-        for i, part in enumerate(row_parts):
+        for i, part in zip((0,) + (2, 1, 3), row_parts):
             for j in range(4):
                 for k in range(2):
                     at = j * 128 + (core ^ k) * 64
                     to = (i // 2) * 1024 + k * 512 + (i % 2) * 256 + j * 64
                     rows[to:to + 64, :] = part[at:at + 64, :]
-        for i, part in enumerate(col_parts):
+        for i, part in zip((0,) + (2, 1, 3), col_parts):
             for j in range(2):
                 at = j * 256 + core * 128
                 to = i * 256 + j * 128
@@ -270,7 +270,7 @@
     near = [hop(a, 2, 1), hop(b, 4, 1), hop(a, 6, 0)]
     weight_a, base_a, token = slope_parts(0, *margs, after=(a,))
     mine = list(call(third_kernel, [block(512)], (token, a, b, *near)))
-    mine = mine + [hop(mine[0], 8 * k, 2 * k) for k in (1, 2, 3)]
+    mine = mine + [hop(mine[0], 8 * k, 2 * k) for k in (2, 1, 3)]
     weight_b, base_b, token = slope_parts(1, *margs, after=(mine[0],))
     mine = mine[0:1] + [tie(x, token) for x in mine[1:]]
     got = [col_swap(x, 1) for x in mine]
@@ -286,13 +286,13 @@
     )
 
     row_got = col_swap(row_other, 1)
-    col_got = [row_swap(x, 2 * k) for k, x in zip((1, 2, 3), col_send)]
+    col_got = [row_swap(col_send[k - 1], 2 * k) for k in (2, 1, 3)]
     row_own, *row_send = fold(row_own, [row_got], 256, 256, 256, 256)
-    row_got = [col_swap(x, 8 * k) for k, x in zip((1, 2, 3), row_send)]
+    row_got = [col_swap(row_send[k - 1], 8 * k) for k in (2, 1, 3)]
     col_own, col_last = fold(col_own, col_got, 128, 128)
     col_got = [row_swap(col_last, 1)]
     row_own, *row_send = fold(row_own, row_got, 64, 64, 64, 64)
-    row_got = [col_swap(x, 2 * k) for k, x in zip((1, 2, 3), row_send)]
+    row_got = [col_swap(row_send[k - 1], 2 * k) for k in (2, 3, 1)]
     new_col_emb, new_col_accum = adagrad(col_own, col_got, col_emb, col_accum)
     new_row_emb, new_row_accum = adagrad(row_own, row_got, row_emb, row_accum)
     return (new_row_emb, new_row_accum, new_col_emb, new_col_accum)

time: 63.5 us -> 58.4 us (0.920); the launches traced: 62.4 us -> 58.2 us
  waiting for transfers between devices: 14.8 us -> 9.1 us
  starting transfers between devices: 31.3 us -> 32.8 us
    ppermute x6, waiting for transfers between devices: 6.82 us -> 3.04 us  [hop(): return lax.ppermute(x, ('row', 'col'), pairs)]
    ppermute x16, starting transfers between devices: 19.3 us -> 21.2 us  [swap(): return lax.ppermute(x, axis, [(i, i ^ flip) for i in range(size)])]
    ppermute x16, waiting for transfers between devices: 7.94 us -> 6.06 us  [swap(): return lax.ppermute(x, axis, [(i, i ^ flip) for i in range(size)])]
  transfers between devices with their start and end apart: 22 -> 22, of which waited for: 9 -> 8; matrix products, arithmetic and copies ran while one was open for 0% -> 0% of each run, Pallas kernels for 14% -> 15%
where the time goes in v3:
time: 58.4 us; the launch traced here: 58.2 us
  starting transfers between devices  32.8 us (56%)
  Pallas kernels  14.8 us (25%)
  waiting for transfers between devices  9.1 us (16%)
  between operations  1.43 us (2%)
    ppermute x16, starting transfers between devices, swap(): return lax.ppermute(x, axis, [(i, i ^ flip) for i in range(size)])  21.2 us
    pallas_call x14, Pallas kernels, call(): pl.pallas_call(kernel, in_specs=in_specs or [VM] * len(ins), out_specs=[V...  14.8 us
    ppermute x6, starting transfers between devices, hop(): return lax.ppermute(x, ('row', 'col'), pairs)  11.6 us
    ppermute x16, waiting for transfers between devices, swap(): return lax.ppermute(x, axis, [(i, i ^ flip) for i in range(size)])  6.06 us
    ppermute x6, waiting for transfers between devices, hop(): return lax.ppermute(x, ('row', 'col'), pairs)  3.04 us
  transfers between devices with their start and end apart: 22, of which 8 were waited for; matrix products, arithmetic and copies ran while one was open for 0% of the time, Pallas kernels for 15%

profile of v3, /device:TPU:2, one launch (start us, length us, event | category | flops | bytes accessed | tf_op | source)
XLA Modules:
  0.0 58.2 jit_solution(7304254647878933355)
XLA Ops:
  0.6 1.0 %shard_map.111 = (bf16[64,256]{1,0:T(8,128)(2,1)S(1)}, bf16[128,256]{1,0:T(8,128)(2,1)S(1)}, bf16[128,256]{1,0:T(8,128)(2,1)S(1)}) custom-call(f32[64,256]{1,0:T(8,128)} %refs_4_.1, f32[128,256]{1,0:T(8,128)} %refs_2_.1), custom_call_target="tpu_custom_call" | custom-call | tf_op jit(solution)/shard_map/pallas_call | solution.py:17
  1.6 0.1 collective-permute-start
  1.7 1.2 %collective-permute-done.got = bf16[128,256]{1,0:T(8,128)(2,1)S(1)} collective-permute-done((bf16[128,256]{1,0:T(8,128)(2,1)S(1)}, bf16[128,256]{1,0:T(8,128)(2,1)S(1)}, u32[]{:S(2)}, u32[]{:S(2)}) %collective-permute-start) | collective-permute-done | bytes 65568 | tf_op jit(solution)/shard_map/ppermute | solution.py:243
  3.0 3.4 %collective-permute-start.2 = (bf16[128,256]{1,0:T(8,128)(2,1)S(1)}, bf16[128,256]{1,0:T(8,128)(2,1)S(1)}, u32[]{:S(2)}, u32[]{:S(2)}) collective-permute-start(bf16[128,256]{1,0:T(8,128)(2,1)S(1)} %get-tuple-element.42.b), channel_id=1, source_target_pairs={{0,4},{1,33},{2,6},{3,35},{4,0},{5,37},{6,2},{7,39},{8,12},{9,41},... | collective-permute-start | bytes 196616 | tf_op jit(solution)/shard_map/ppermute | solution.py:254
  6.3 3.3 %collective-permute-start.3 = (bf16[128,256]{1,0:T(8,128)(2,1)S(1)}, bf16[128,256]{1,0:T(8,128)(2,1)S(1)}, u32[]{:S(2)}, u32[]{:S(2)}) collective-permute-start(bf16[128,256]{1,0:T(8,128)(2,1)S(1)} %get-tuple-element.38.refs_0_.a), channel_id=1, source_target_pairs={{0,6},{2,4},{4,2},{6,0},{8,14},{10,12},{12,10},{14,8},{16,22},{18,... | collective-permute-start | bytes 196616 | tf_op jit(solution)/shard_map/ppermute | solution.py:254
  9.6 0.6 %collective-permute-start.1 = (bf16[128,256]{1,0:T(8,128)(2,1)S(1)}, bf16[128,256]{1,0:T(8,128)(2,1)S(1)}, u32[]{:S(2)}, u32[]{:S(2)}) collective-permute-start(bf16[128,256]{1,0:T(8,128)(2,1)S(1)} %get-tuple-element.38.refs_0_.a), channel_id=1, source_target_pairs={{0,2},{1,33},{2,0},{3,35},{4,6},{5,37},{6,4},{7,39},{8,10},{9,41},... | collective-permute-start | bytes 196616 | tf_op jit(solution)/shard_map/ppermute | solution.py:254
  10.9 3.7 %shard_map.113 = (f32[1024,1024]{1,0:T(8,128)S(1)}, f32[1024,1024]{1,0:T(8,128)S(1)}, f32[8,128]{1,0:T(8,128)S(1)}) custom-call(f32[1]{0:T(128)S(6)} %copy.12.log_total, s32[16,128]{1,0:T(8,128)} %bitcast.8, s32[8,128]{1,0:T(8,128)} %bitcast.10, s32[2048,1024]{1,0:T(8,128)} %counts.3, bf16[128,256]{1,0:T(8,128)(2,1)S(1)} %get-tuple-element.38.refs_0_.a), custom_call_target="tpu_custom_call" | custom-call | bytes 10485760 | tf_op jit(solution)/shard_map/pallas_call | solution.py:17
  14.6 1.6 %collective-permute-done.1.g1 = bf16[128,256]{1,0:T(8,128)(2,1)S(1)} collective-permute-done((bf16[128,256]{1,0:T(8,128)(2,1)S(1)}, bf16[128,256]{1,0:T(8,128)(2,1)S(1)}, u32[]{:S(2)}, u32[]{:S(2)}) %collective-permute-start.1) | collective-permute-done | bytes 65568 | tf_op jit(solution)/shard_map/ppermute | solution.py:254
  16.3 3.3 %collective-permute-start.4 = (bf16[512,256]{1,0:T(8,128)(2,1)S(1)}, bf16[512,256]{1,0:T(8,128)(2,1)S(1)}, u32[]{:S(2)}, u32[]{:S(2)}) collective-permute-start(bf16[512,256]{1,0:T(8,128)(2,1)S(1)} %shard_map.114.refs_0_), channel_id=1, source_target_pairs={{0,16},{1,129},{2,18},{3,131},{4,20},{5,133},{6,22},{7,135},{8,24}... | collective-permute-start | bytes 786440 | tf_op jit(solution)/shard_map/ppermute | solution.py:254
  19.6 0.7 %collective-permute-start.5 = (bf16[512,256]{1,0:T(8,128)(2,1)S(1)}, bf16[512,256]{1,0:T(8,128)(2,1)S(1)}, u32[]{:S(2)}, u32[]{:S(2)}) collective-permute-start(bf16[512,256]{1,0:T(8,128)(2,1)S(1)} %shard_map.114.refs_0_), channel_id=1, source_target_pairs={{0,8},{1,65},{2,10},{3,67},{4,12},{5,69},{6,14},{7,71},{8,0},{9,73... | collective-permute-start | bytes 786440 | tf_op jit(solution)/shard_map/ppermute | solution.py:254
  20.3 0.4 collective-permute-start.6
  20.6 1.5 %collective-permute-start.7 = (bf16[512,256]{1,0:T(8,128)(2,1)S(1)}, bf16[512,256]{1,0:T(8,128)(2,1)S(1)}, u32[]{:S(2)}, u32[]{:S(2)}) collective-permute-start(bf16[512,256]{1,0:T(8,128)(2,1)S(1)} %shard_map.114.refs_0_), channel_id=1, source_target_pairs={{0,1},{1,0},{2,3},{3,2},{4,5},{5,4},{6,7},{7,6},{8,9},{9,8},{10,11... | collective-permute-start | bytes 786440 | tf_op jit(solution)/shard_map/ppermute | solution.py:243
  22.2 3.7 %shard_map.115 = (f32[1024,1024]{1,0:T(8,128)S(1)}, f32[1024,1024]{1,0:T(8,128)S(1)}, f32[8,128]{1,0:T(8,128)S(1)}) custom-call(f32[1]{0:T(128)S(6)} %copy.12.log_total, s32[16,128]{1,0:T(8,128)} %bitcast.9, s32[8,128]{1,0:T(8,128)} %bitcast.11, s32[2048,1024]{1,0:T(8,128)} %counts.3, bf16[512,256]{1,0:T(8,128)(2,1)S(1)} %shard_map.114.refs_0_), custom_call_target="tpu_custom_call" | custom-call | bytes 10485760 | tf_op jit(solution)/shard_map/pallas_call | solution.py:17
  25.9 0.0 collective-permute-done.4.x
  25.9 0.1 collective-permute-start.8
  26.1 1.4 %collective-permute-done.5.x = bf16[512,256]{1,0:T(8,128)(2,1)S(1)} collective-permute-done((bf16[512,256]{1,0:T(8,128)(2,1)S(1)}, bf16[512,256]{1,0:T(8,128)(2,1)S(1)}, u32[]{:S(2)}, u32[]{:S(2)}) %collective-permute-start.5) | collective-permute-done | bytes 262176 | tf_op jit(solution)/shard_map/ppermute | solution.py:254
  27.5 1.2 %collective-permute-start.9 = (bf16[512,256]{1,0:T(8,128)(2,1)S(1)}, bf16[512,256]{1,0:T(8,128)(2,1)S(1)}, u32[]{:S(2)}, u32[]{:S(2)}) collective-permute-start(bf16[512,256]{1,0:T(8,128)(2,1)S(1)} %shard_map.117.refs_2_), channel_id=1, source_target_pairs={{0,1},{1,0},{2,3},{3,2},{4,5},{5,4},{6,7},{7,6},{8,9},{9,8},{10,11... | collective-permute-start | bytes 786440 | tf_op jit(solution)/shard_map/ppermute | solution.py:243
  28.7 0.0 collective-permute-done.6.x
  28.7 0.1 collective-permute-start.10
  28.8 0.0 collective-permute-done.7.refs_4_
  28.8 0.0 collective-permute-done.8.refs_5_
  28.8 1.0 %collective-permute-done.9.refs_6_ = bf16[512,256]{1,0:T(8,128)(2,1)S(1)} collective-permute-done((bf16[512,256]{1,0:T(8,128)(2,1)S(1)}, bf16[512,256]{1,0:T(8,128)(2,1)S(1)}, u32[]{:S(2)}, u32[]{:S(2)}) %collective-permute-start.9) | collective-permute-done | bytes 262176 | tf_op jit(solution)/shard_map/ppermute | solution.py:243
  29.8 0.5 collective-permute-done.10.refs_7_
  30.3 4.4 %shard_map.119 = (f32[1024,256]{1,0:T(8,128)S(1)}, bf16[1024,256]{1,0:T(8,128)(2,1)S(1)}, f32[256,256]{1,0:T(8,128)S(1)}, bf16[256,256]{1,0:T(8,128)(2,1)S(1)}, ...) custom-call(f32[1024,1024]{1,0:T(8,128)S(1)} %get-tuple-element.39.weight_a, ...), custom_call_target="tpu_custom_call" | custom-call | flops 3221225472 | bytes 16777216 | tf_op jit(solution)/shard_map/pallas_call | solution.py:17
  34.7 0.3 collective-permute-start.11
  35.1 1.7 %collective-permute-start.18 = (bf16[256,256]{1,0:T(8,128)(2,1)S(1)}, bf16[256,256]{1,0:T(8,128)(2,1)S(1)}, u32[]{:S(2)}, u32[]{:S(2)}) collective-permute-start(bf16[256,256]{1,0:T(8,128)(2,1)S(1)} %get-tuple-element.59), channel_id=1, source_target_pairs={{0,128},{32,160},{64,192},{96,224},{128,0},{160,32},{192,64},{224,... | collective-permute-start | bytes 393224 | tf_op jit(solution)/shard_map/ppermute | solution.py:243
  36.7 1.4 %collective-permute-start.19 = (bf16[256,256]{1,0:T(8,128)(2,1)S(1)}, bf16[256,256]{1,0:T(8,128)(2,1)S(1)}, u32[]{:S(2)}, u32[]{:S(2)}) collective-permute-start(bf16[256,256]{1,0:T(8,128)(2,1)S(1)} %get-tuple-element.60), channel_id=1, source_target_pairs={{0,64},{32,96},{64,0},{96,32},{128,192},{160,224},{192,128},{224,1... | collective-permute-start | bytes 393224 | tf_op jit(solution)/shard_map/ppermute | solution.py:243
  38.2 1.0 %collective-permute-start.20 = (bf16[256,256]{1,0:T(8,128)(2,1)S(1)}, bf16[256,256]{1,0:T(8,128)(2,1)S(1)}, u32[]{:S(2)}, u32[]{:S(2)}) collective-permute-start(bf16[256,256]{1,0:T(8,128)(2,1)S(1)} %get-tuple-element.61), channel_id=1, source_target_pairs={{0,192},{32,224},{64,128},{96,160},{128,64},{160,96},{192,0},{224,... | collective-permute-start | bytes 393224 | tf_op jit(solution)/shard_map/ppermute | solution.py:243
  39.2 0.0 collective-permute-done.11.refs_1_
  39.2 0.1 shard_map.120
  39.3 3.3 %collective-permute-start.12 = (bf16[256,256]{1,0:T(8,128)(2,1)S(1)}, bf16[256,256]{1,0:T(8,128)(2,1)S(1)}, u32[]{:S(2)}, u32[]{:S(2)}) collective-permute-start(bf16[256,256]{1,0:T(8,128)(2,1)S(1)} %get-tuple-element.49), channel_id=1, source_target_pairs={{0,16},{1,17},{2,18},{3,19},{4,20},{5,21},{6,22},{7,23},{8,24},{9,... | collective-permute-start | bytes 393224 | tf_op jit(solution)/shard_map/ppermute | solution.py:243
  42.5 0.7 %collective-permute-start.13 = (bf16[256,256]{1,0:T(8,128)(2,1)S(1)}, bf16[256,256]{1,0:T(8,128)(2,1)S(1)}, u32[]{:S(2)}, u32[]{:S(2)}) collective-permute-start(bf16[256,256]{1,0:T(8,128)(2,1)S(1)} %get-tuple-element.50), channel_id=1, source_target_pairs={{0,8},{1,9},{2,10},{3,11},{4,12},{5,13},{6,14},{7,15},{8,0},{9,1},... | collective-permute-start | bytes 393224 | tf_op jit(solution)/shard_map/ppermute | solution.py:243
  43.2 0.0 collective-permute-done.18.refs_1_
  43.2 2.7 %collective-permute-start.14 = (bf16[256,256]{1,0:T(8,128)(2,1)S(1)}, bf16[256,256]{1,0:T(8,128)(2,1)S(1)}, u32[]{:S(2)}, u32[]{:S(2)}) collective-permute-start(bf16[256,256]{1,0:T(8,128)(2,1)S(1)} %get-tuple-element.51), channel_id=1, source_target_pairs={{0,24},{1,25},{2,26},{3,27},{4,28},{5,29},{6,30},{7,31},{8,16},{9,... | collective-permute-start | bytes 393224 | tf_op jit(solution)/shard_map/ppermute | solution.py:243
  45.9 0.0 collective-permute-done.19.refs_2_
  45.9 0.0 collective-permute-done.20.refs_3_
  45.9 0.1 shard_map.123
  46.0 3.4 %collective-permute-start.21 = (bf16[128,256]{1,0:T(8,128)(2,1)S(1)}, bf16[128,256]{1,0:T(8,128)(2,1)S(1)}, u32[]{:S(2)}, u32[]{:S(2)}) collective-permute-start(bf16[128,256]{1,0:T(8,128)(2,1)S(1)} %get-tuple-element.63), channel_id=1, source_target_pairs={{0,32},{32,0},{64,96},{96,64},{128,160},{160,128},{192,224},{224,1... | collective-permute-start | bytes 196616 | tf_op jit(solution)/shard_map/ppermute | solution.py:243
  49.4 0.0 collective-permute-done.13.refs_2_
  49.4 0.1 shard_map.121
  49.5 1.8 %collective-permute-start.15 = (bf16[64,256]{1,0:T(8,128)(2,1)S(1)}, bf16[64,256]{1,0:T(8,128)(2,1)S(1)}, u32[]{:S(2)}, u32[]{:S(2)}) collective-permute-start(bf16[64,256]{1,0:T(8,128)(2,1)S(1)} %get-tuple-element.53), channel_id=1, source_target_pairs={{0,4},{1,5},{2,6},{3,7},{4,0},{5,1},{6,2},{7,3},{8,12},{9,13},{10,... | collective-permute-start | bytes 98312 | tf_op jit(solution)/shard_map/ppermute | solution.py:243
  51.4 1.7 %collective-permute-start.16 = (bf16[64,256]{1,0:T(8,128)(2,1)S(1)}, bf16[64,256]{1,0:T(8,128)(2,1)S(1)}, u32[]{:S(2)}, u32[]{:S(2)}) collective-permute-start(bf16[64,256]{1,0:T(8,128)(2,1)S(1)} %get-tuple-element.54), channel_id=1, source_target_pairs={{0,6},{1,7},{2,4},{3,5},{4,2},{5,3},{6,0},{7,1},{8,14},{9,15},{10,... | collective-permute-start | bytes 98312 | tf_op jit(solution)/shard_map/ppermute | solution.py:243
  53.0 0.1 collective-permute-start.17
  53.1 2.4 %collective-permute-done.21.refs_1_ = bf16[128,256]{1,0:T(8,128)(2,1)S(1)} collective-permute-done((bf16[128,256]{1,0:T(8,128)(2,1)S(1)}, bf16[128,256]{1,0:T(8,128)(2,1)S(1)}, u32[]{:S(2)}, u32[]{:S(2)}) %collective-permute-start.21) | collective-permute-done | bytes 65568 | tf_op jit(solution)/shard_map/ppermute | solution.py:243
  55.5 0.9 %shard_map.124 = (f32[128,256]{1,0:T(8,128)}, f32[1,128]{1,0:T(1,128)}) custom-call(f32[128,256]{1,0:T(8,128)S(1)} %get-tuple-element.62.refs_0_, bf16[128,256]{1,0:T(8,128)(2,1)S(1)} %collective-permute-done.21.refs_1_, f32[128,256]{1,0:T(8,128)S(1)} %copy-done, f32[1,128]{1,0:T(1,128)S(1)} %bitcast.6), custom_call_target="tpu_custom_call" | custom-call | tf_op jit(solution)/shard_map/pallas_call | solution.py:17
  56.4 0.8 %collective-permute-done.16.refs_2_ = bf16[64,256]{1,0:T(8,128)(2,1)S(1)} collective-permute-done((bf16[64,256]{1,0:T(8,128)(2,1)S(1)}, bf16[64,256]{1,0:T(8,128)(2,1)S(1)}, u32[]{:S(2)}, u32[]{:S(2)}) %collective-permute-start.16) | collective-permute-done | bytes 32800 | tf_op jit(solution)/shard_map/ppermute | solution.py:243
  57.2 0.1 collective-permute-done.17.refs_3_
  57.3 0.9 %shard_map.122 = (f32[64,256]{1,0:T(8,128)}, f32[1,64]{1,0:T(1,128)}) custom-call(f32[64,256]{1,0:T(8,128)S(1)} %get-tuple-element.52.refs_0_, bf16[64,256]{1,0:T(8,128)(2,1)S(1)} %collective-permute-done.15.refs_1_, bf16[64,256]{1,0:T(8,128)(2,1)S(1)} %collective-permute-done.16.refs_2_, bf16[64,256]{1,0:T(8,128)(2,1)S(1)} %collective-permute-done.17.refs_3_, ...), custom_call_target="tpu_custom_call" | custom-call | tf_op jit(solution)/shard_map/pallas_call | solution.py:17
  (18 shorter events, 0.1 us)
Async XLA Ops:
  1.6 1.3 %collective-permute-start = (bf16[128,256]{1,0:T(8,128)(2,1)S(1)}, bf16[128,256]{1,0:T(8,128)(2,1)S(1)}, u32[]{:S(2)}, u32[]{:S(2)}) collective-permute-start(bf16[128,256]{1,0:T(8,128)(2,1)S(1)} %get-tuple-element.37), channel_id=1, source_target_pairs={{0,1},{1,0},{2,3},{3,2},{4,5},{5,4},{6,7},{7,6},{8,9},{9,8},{10,11... | collective-permute-start | bytes 196616 | tf_op jit(solution)/shard_map/ppermute | solution.py:243
  3.0 11.6 %collective-permute-start.2 = (bf16[128,256]{1,0:T(8,128)(2,1)S(1)}, bf16[128,256]{1,0:T(8,128)(2,1)S(1)}, u32[]{:S(2)}, u32[]{:S(2)}) collective-permute-start(bf16[128,256]{1,0:T(8,128)(2,1)S(1)} %get-tuple-element.42.b), channel_id=1, source_target_pairs={{0,4},{1,33},{2,6},{3,35},{4,0},{5,37},{6,2},{7,39},{8,12},{9,41},... | collective-permute-start | bytes 196616 | tf_op jit(solution)/shard_map/ppermute | solution.py:254
  6.3 8.3 %collective-permute-start.3 = (bf16[128,256]{1,0:T(8,128)(2,1)S(1)}, bf16[128,256]{1,0:T(8,128)(2,1)S(1)}, u32[]{:S(2)}, u32[]{:S(2)}) collective-permute-start(bf16[128,256]{1,0:T(8,128)(2,1)S(1)} %get-tuple-element.38.refs_0_.a), channel_id=1, source_target_pairs={{0,6},{2,4},{4,2},{6,0},{8,14},{10,12},{12,10},{14,8},{16,22},{18,... | collective-permute-start | bytes 196616 | tf_op jit(solution)/shard_map/ppermute | solution.py:254
  9.6 6.7 %collective-permute-start.1 = (bf16[128,256]{1,0:T(8,128)(2,1)S(1)}, bf16[128,256]{1,0:T(8,128)(2,1)S(1)}, u32[]{:S(2)}, u32[]{:S(2)}) collective-permute-start(bf16[128,256]{1,0:T(8,128)(2,1)S(1)} %get-tuple-element.38.refs_0_.a), channel_id=1, source_target_pairs={{0,2},{1,33},{2,0},{3,35},{4,6},{5,37},{6,4},{7,39},{8,10},{9,41},... | collective-permute-start | bytes 196616 | tf_op jit(solution)/shard_map/ppermute | solution.py:254
  16.3 9.6 %collective-permute-start.4 = (bf16[512,256]{1,0:T(8,128)(2,1)S(1)}, bf16[512,256]{1,0:T(8,128)(2,1)S(1)}, u32[]{:S(2)}, u32[]{:S(2)}) collective-permute-start(bf16[512,256]{1,0:T(8,128)(2,1)S(1)} %shard_map.114.refs_0_), channel_id=1, source_target_pairs={{0,16},{1,129},{2,18},{3,131},{4,20},{5,133},{6,22},{7,135},{8,24}... | collective-permute-start | bytes 786440 | tf_op jit(solution)/shard_map/ppermute | solution.py:254
  19.6 7.9 %collective-permute-start.5 = (bf16[512,256]{1,0:T(8,128)(2,1)S(1)}, bf16[512,256]{1,0:T(8,128)(2,1)S(1)}, u32[]{:S(2)}, u32[]{:S(2)}) collective-permute-start(bf16[512,256]{1,0:T(8,128)(2,1)S(1)} %shard_map.114.refs_0_), channel_id=1, source_target_pairs={{0,8},{1,65},{2,10},{3,67},{4,12},{5,69},{6,14},{7,71},{8,0},{9,73... | collective-permute-start | bytes 786440 | tf_op jit(solution)/shard_map/ppermute | solution.py:254
  20.3 8.4 %collective-permute-start.6 = (bf16[512,256]{1,0:T(8,128)(2,1)S(1)}, bf16[512,256]{1,0:T(8,128)(2,1)S(1)}, u32[]{:S(2)}, u32[]{:S(2)}) collective-permute-start(bf16[512,256]{1,0:T(8,128)(2,1)S(1)} %shard_map.114.refs_0_), channel_id=1, source_target_pairs={{0,24},{1,193},{2,26},{3,195},{4,28},{5,197},{6,30},{7,199},{8,16}... | collective-permute-start | bytes 786440 | tf_op jit(solution)/shard_map/ppermute | solution.py:254
  20.6 8.1 %collective-permute-start.7 = (bf16[512,256]{1,0:T(8,128)(2,1)S(1)}, bf16[512,256]{1,0:T(8,128)(2,1)S(1)}, u32[]{:S(2)}, u32[]{:S(2)}) collective-permute-start(bf16[512,256]{1,0:T(8,128)(2,1)S(1)} %shard_map.114.refs_0_), channel_id=1, source_target_pairs={{0,1},{1,0},{2,3},{3,2},{4,5},{5,4},{6,7},{7,6},{8,9},{9,8},{10,11... | collective-permute-start | bytes 786440 | tf_op jit(solution)/shard_map/ppermute | solution.py:243
  25.9 2.9 %collective-permute-start.8 = (bf16[512,256]{1,0:T(8,128)(2,1)S(1)}, bf16[512,256]{1,0:T(8,128)(2,1)S(1)}, u32[]{:S(2)}, u32[]{:S(2)}) collective-permute-start(bf16[512,256]{1,0:T(8,128)(2,1)S(1)} %shard_map.116.refs_1_), channel_id=1, source_target_pairs={{0,1},{1,0},{2,3},{3,2},{4,5},{5,4},{6,7},{7,6},{8,9},{9,8},{10,11... | collective-permute-start | bytes 786440 | tf_op jit(solution)/shard_map/ppermute | solution.py:243
  27.5 2.3 %collective-permute-start.9 = (bf16[512,256]{1,0:T(8,128)(2,1)S(1)}, bf16[512,256]{1,0:T(8,128)(2,1)S(1)}, u32[]{:S(2)}, u32[]{:S(2)}) collective-permute-start(bf16[512,256]{1,0:T(8,128)(2,1)S(1)} %shard_map.117.refs_2_), channel_id=1, source_target_pairs={{0,1},{1,0},{2,3},{3,2},{4,5},{5,4},{6,7},{7,6},{8,9},{9,8},{10,11... | collective-permute-start | bytes 786440 | tf_op jit(solution)/shard_map/ppermute | solution.py:243
  28.7 1.6 %collective-permute-start.10 = (bf16[512,256]{1,0:T(8,128)(2,1)S(1)}, bf16[512,256]{1,0:T(8,128)(2,1)S(1)}, u32[]{:S(2)}, u32[]{:S(2)}) collective-permute-start(bf16[512,256]{1,0:T(8,128)(2,1)S(1)} %shard_map.118.refs_3_), channel_id=1, source_target_pairs={{0,1},{1,0},{2,3},{3,2},{4,5},{5,4},{6,7},{7,6},{8,9},{9,8},{10,11... | collective-permute-start | bytes 786440 | tf_op jit(solution)/shard_map/ppermute | solution.py:243
  30.3 25.2 %copy-start = (f32[128,256]{1,0:T(8,128)S(1)}, f32[128,256]{1,0:T(8,128)}, u32[]{:S(2)}) copy-start(f32[128,256]{1,0:T(8,128)} %refs_2_.1) | copy-start | bytes 393220
  30.3 25.2 %copy-start.2 = (f32[128]{0:T(128)S(1)}, f32[128]{0:T(128)}, u32[]{:S(2)}) copy-start(f32[128]{0:T(128)} %param.15) | copy-start | bytes 1540
  30.3 27.0 %copy-start.1 = (f32[64,256]{1,0:T(8,128)S(1)}, f32[64,256]{1,0:T(8,128)}, u32[]{:S(2)}) copy-start(f32[64,256]{1,0:T(8,128)} %refs_4_.1) | copy-start | bytes 196612
  30.3 27.0 %copy-start.3 = (f32[64]{0:T(128)S(1)}, f32[64]{0:T(128)}, u32[]{:S(2)}) copy-start(f32[64]{0:T(128)} %param.13) | copy-start | bytes 772
  34.7 4.5 %collective-permute-start.11 = (bf16[1024,256]{1,0:T(8,128)(2,1)S(1)}, bf16[1024,256]{1,0:T(8,128)(2,1)S(1)}, u32[]{:S(2)}, u32[]{:S(2)}) collective-permute-start(bf16[1024,256]{1,0:T(8,128)(2,1)S(1)} %get-tuple-element.47), channel_id=1, source_target_pairs={{0,1},{1,0},{2,3},{3,2},{4,5},{5,4},{6,7},{7,6},{8,9},{9,8},{10,11... | collective-permute-start | bytes 1572872 | tf_op jit(solution)/shard_map/ppermute | solution.py:243
  35.1 8.2 %collective-permute-start.18 = (bf16[256,256]{1,0:T(8,128)(2,1)S(1)}, bf16[256,256]{1,0:T(8,128)(2,1)S(1)}, u32[]{:S(2)}, u32[]{:S(2)}) collective-permute-start(bf16[256,256]{1,0:T(8,128)(2,1)S(1)} %get-tuple-element.59), channel_id=1, source_target_pairs={{0,128},{32,160},{64,192},{96,224},{128,0},{160,32},{192,64},{224,... | collective-permute-start | bytes 393224 | tf_op jit(solution)/shard_map/ppermute | solution.py:243
  36.7 9.2 %collective-permute-start.19 = (bf16[256,256]{1,0:T(8,128)(2,1)S(1)}, bf16[256,256]{1,0:T(8,128)(2,1)S(1)}, u32[]{:S(2)}, u32[]{:S(2)}) collective-permute-start(bf16[256,256]{1,0:T(8,128)(2,1)S(1)} %get-tuple-element.60), channel_id=1, source_target_pairs={{0,64},{32,96},{64,0},{96,32},{128,192},{160,224},{192,128},{224,1... | collective-permute-start | bytes 393224 | tf_op jit(solution)/shard_map/ppermute | solution.py:243
  38.2 7.8 %collective-permute-start.20 = (bf16[256,256]{1,0:T(8,128)(2,1)S(1)}, bf16[256,256]{1,0:T(8,128)(2,1)S(1)}, u32[]{:S(2)}, u32[]{:S(2)}) collective-permute-start(bf16[256,256]{1,0:T(8,128)(2,1)S(1)} %get-tuple-element.61), channel_id=1, source_target_pairs={{0,192},{32,224},{64,128},{96,160},{128,64},{160,96},{192,0},{224,... | collective-permute-start | bytes 393224 | tf_op jit(solution)/shard_map/ppermute | solution.py:243
  39.3 10.2 %collective-permute-start.12 = (bf16[256,256]{1,0:T(8,128)(2,1)S(1)}, bf16[256,256]{1,0:T(8,128)(2,1)S(1)}, u32[]{:S(2)}, u32[]{:S(2)}) collective-permute-start(bf16[256,256]{1,0:T(8,128)(2,1)S(1)} %get-tuple-element.49), channel_id=1, source_target_pairs={{0,16},{1,17},{2,18},{3,19},{4,20},{5,21},{6,22},{7,23},{8,24},{9,... | collective-permute-start | bytes 393224 | tf_op jit(solution)/shard_map/ppermute | solution.py:243
  42.5 6.9 %collective-permute-start.13 = (bf16[256,256]{1,0:T(8,128)(2,1)S(1)}, bf16[256,256]{1,0:T(8,128)(2,1)S(1)}, u32[]{:S(2)}, u32[]{:S(2)}) collective-permute-start(bf16[256,256]{1,0:T(8,128)(2,1)S(1)} %get-tuple-element.50), channel_id=1, source_target_pairs={{0,8},{1,9},{2,10},{3,11},{4,12},{5,13},{6,14},{7,15},{8,0},{9,1},... | collective-permute-start | bytes 393224 | tf_op jit(solution)/shard_map/ppermute | solution.py:243
  43.2 6.2 %collective-permute-start.14 = (bf16[256,256]{1,0:T(8,128)(2,1)S(1)}, bf16[256,256]{1,0:T(8,128)(2,1)S(1)}, u32[]{:S(2)}, u32[]{:S(2)}) collective-permute-start(bf16[256,256]{1,0:T(8,128)(2,1)S(1)} %get-tuple-element.51), channel_id=1, source_target_pairs={{0,24},{1,25},{2,26},{3,27},{4,28},{5,29},{6,30},{7,31},{8,16},{9,... | collective-permute-start | bytes 393224 | tf_op jit(solution)/shard_map/ppermute | solution.py:243
  46.0 9.5 %collective-permute-start.21 = (bf16[128,256]{1,0:T(8,128)(2,1)S(1)}, bf16[128,256]{1,0:T(8,128)(2,1)S(1)}, u32[]{:S(2)}, u32[]{:S(2)}) collective-permute-start(bf16[128,256]{1,0:T(8,128)(2,1)S(1)} %get-tuple-element.63), channel_id=1, source_target_pairs={{0,32},{32,0},{64,96},{96,64},{128,160},{160,128},{192,224},{224,1... | collective-permute-start | bytes 196616 | tf_op jit(solution)/shard_map/ppermute | solution.py:243
  49.5 6.9 %collective-permute-start.15 = (bf16[64,256]{1,0:T(8,128)(2,1)S(1)}, bf16[64,256]{1,0:T(8,128)(2,1)S(1)}, u32[]{:S(2)}, u32[]{:S(2)}) collective-permute-start(bf16[64,256]{1,0:T(8,128)(2,1)S(1)} %get-tuple-element.53), channel_id=1, source_target_pairs={{0,4},{1,5},{2,6},{3,7},{4,0},{5,1},{6,2},{7,3},{8,12},{9,13},{10,... | collective-permute-start | bytes 98312 | tf_op jit(solution)/shard_map/ppermute | solution.py:243
  51.4 5.9 %collective-permute-start.16 = (bf16[64,256]{1,0:T(8,128)(2,1)S(1)}, bf16[64,256]{1,0:T(8,128)(2,1)S(1)}, u32[]{:S(2)}, u32[]{:S(2)}) collective-permute-start(bf16[64,256]{1,0:T(8,128)(2,1)S(1)} %get-tuple-element.54), channel_id=1, source_target_pairs={{0,6},{1,7},{2,4},{3,5},{4,2},{5,3},{6,0},{7,1},{8,14},{9,15},{10,... | collective-permute-start | bytes 98312 | tf_op jit(solution)/shard_map/ppermute | solution.py:243
  53.0 4.3 %collective-permute-start.17 = (bf16[64,256]{1,0:T(8,128)(2,1)S(1)}, bf16[64,256]{1,0:T(8,128)(2,1)S(1)}, u32[]{:S(2)}, u32[]{:S(2)}) collective-permute-start(bf16[64,256]{1,0:T(8,128)(2,1)S(1)} %get-tuple-element.55), channel_id=1, source_target_pairs={{0,2},{1,3},{2,0},{3,1},{4,6},{5,7},{6,4},{7,5},{8,10},{9,11},{10,... | collective-permute-start | bytes 98312 | tf_op jit(solution)/shard_map/ppermute | solution.py:243

commit v4 on v3

--- a/solution.py
+++ b/solution.py
@@ -7,6 +7,7 @@
 from jax.sharding import PartitionSpec as P
 
 learn_rate = 0.5
+FIRST = 6
 D = 256
 f32, bf16 = jnp.float32, jnp.bfloat16
 VM = pl.BlockSpec(memory_space=pltpu.VMEM)
@@ -71,7 +72,7 @@
         for i, part in enumerate(parts):
             out[i * 128:(i + 1) * 128, :] = part[...]
 
-    by_core(lambda: put(a, g1, g2, g3), lambda: put(a, b, g1, g2))
+    by_core(lambda: put(a, g1, g2, g3), lambda: put(a, b, g3, g2))
 
 
 def tie_kernel(x, *refs):
@@ -82,39 +83,37 @@
     return call(tie_kernel, [(x.shape, x.dtype)], (x, *after))[0]
 
 
-def slope_parts_kernel(half, after, log_total, row_marg, col_marg, counts, *refs):
+def slope_parts_kernel(low, groups, after, log_total, row_marg, col_marg, counts, *refs):
     weight, base, token, buf, row_buf, col_buf, sem, row_log, row_half, col_half = refs[after:]
     token[...] = jnp.zeros_like(token)
     me = lax.axis_index("row"), lax.axis_index("col")
-    core = me[1] % 2
-    group = lambda i: (me[1] // 2) ^ (i + 8 * half)
+    group = lambda i: (me[1] // 2) ^ (i + low)
 
     def copy(i):
         at = pl.multiple_of(group(i) * 128, 128)
         return pltpu.make_async_copy(counts.at[pl.ds(at, 128), :], buf.at[i], sem.at[i])
 
     small = [
-        pltpu.make_async_copy(row_marg, row_buf, sem.at[8]),
-        pltpu.make_async_copy(col_marg, col_buf, sem.at[9]),
+        pltpu.make_async_copy(row_marg, row_buf, sem.at[groups]),
+        pltpu.make_async_copy(col_marg, col_buf, sem.at[groups + 1]),
     ]
     for one in small:
         one.start()
-    for i in range(8):
+    for i in range(groups):
         copy(i).start()
     row_log[...] = jnp.zeros_like(row_log)
     for one in small:
         one.wait()
-    for i in range(8):
+    for i in range(groups):
         row_log[i:i + 1, :] = jnp.log(row_buf[pl.ds(group(i), 1), :].astype(f32))
     turned = 0.5 * row_log[...].T
-    for i in range(8):
+    for i in range(groups):
         row_half[i] = jnp.broadcast_to(turned[:, i:i + 1], (128, 128))
     col_half[...] = 0.5 * (jnp.log(col_buf[...].astype(f32)) - log_total[0])
 
     def body(i, carry):
         copy(i).wait()
-        first = pl.ds(pl.multiple_of(i * 64 + core * 512, 64), 64)
-        second = pl.ds(pl.multiple_of(i * 64 + (1 - core) * 512, 64), 64)
+        rows = pl.ds(pl.multiple_of(i * 128, 128), 128)
         shift = row_half[i]
         for j in range(8):
             strip = me[0] ^ j
@@ -122,36 +121,32 @@
             present = n > 0.0
             n = jnp.maximum(n, 1.0)
             at = slice(j * 128, (j + 1) * 128)
-            w = jnp.where(present, 0.2 + (0.5 * n) * lax.rsqrt(n), 0.0)
-            b = (shift + col_half[pl.ds(strip, 1), :]) - 0.5 * jnp.log(n)
-            weight[first, at] = w[0:64, :]
-            weight[second, at] = w[64:128, :]
-            base[first, at] = b[0:64, :]
-            base[second, at] = b[64:128, :]
+            weight[rows, at] = jnp.where(present, 0.2 + (0.5 * n) * lax.rsqrt(n), 0.0)
+            base[rows, at] = (shift + col_half[pl.ds(strip, 1), :]) - 0.5 * jnp.log(n)
         return carry
 
-    lax.fori_loop(0, 8, body, 0)
-
-
-def slope_parts(half, log_total, row_marg, col_marg, counts, after=()):
+    lax.fori_loop(0, groups, body, 0)
+
+
+def slope_parts(low, groups, log_total, row_marg, col_marg, counts, after=()):
     hbm = pl.BlockSpec(memory_space=pltpu.HBM)
     keep = lambda x: pltpu.with_memory_space_constraint(x, pltpu.HBM)
     return call(
-        functools.partial(slope_parts_kernel, half, len(after)),
-        [((1024, 1024), f32)] * 2 + [((8, 128), f32)],
+        functools.partial(slope_parts_kernel, low, groups, len(after)),
+        [((128 * groups, 1024), f32)] * 2 + [((8, 128), f32)],
         (log_total, keep(row_marg.reshape(16, 128)), keep(col_marg.reshape(8, 128)), keep(counts), *after),
         in_specs=[SM, hbm, hbm, hbm] + [VM] * len(after),
         scratch=[
-            pltpu.VMEM((8, 128, 1024), jnp.int32),
+            pltpu.VMEM((groups, 128, 1024), jnp.int32),
             pltpu.VMEM((16, 128), jnp.int32),
             pltpu.VMEM((8, 128), jnp.int32),
-            pltpu.SemaphoreType.DMA((10,)),
+            pltpu.SemaphoreType.DMA((groups + 2,)),
             pltpu.VMEM((128, 128), f32),
-            pltpu.VMEM((8, 128, 128), f32),
+            pltpu.VMEM((groups, 128, 128), f32),
             pltpu.VMEM((8, 128), f32),
         ],
-        limit=8,
-        cost=pl.CostEstimate(flops=0, bytes_accessed=10 << 20, transcendentals=2 << 20),
+        limit=10,
+        cost=pl.CostEstimate(flops=0, bytes_accessed=groups * 5 << 18, transcendentals=groups << 18),
     )
 
 
@@ -161,11 +156,7 @@
 
     def gather(row_parts, col_parts, core):
         for i, part in zip((0,) + (2, 1, 3), row_parts):
-            for j in range(4):
-                for k in range(2):
-                    at = j * 128 + (core ^ k) * 64
-                    to = (i // 2) * 1024 + k * 512 + (i % 2) * 256 + j * 64
-                    rows[to:to + 64, :] = part[at:at + 64, :]
+            rows[i * 512:(i + 1) * 512, :] = part[...]
         for i, part in zip((0,) + (2, 1, 3), col_parts):
             for j in range(2):
                 at = j * 256 + core * 128
@@ -178,7 +169,7 @@
         c = cols[at, :]
         col = None
         for h, (weight, base) in enumerate(((weight_a, base_a), (weight_b, base_b))):
-            here = slice(h * 1024, (h + 1) * 1024)
+            here = slice(FIRST * 128 * h, FIRST * 128 + (2048 - FIRST * 128) * h)
             r = rows[here, :]
             x = lax.dot_general(r * bf16(0.5), c, (((1,), (1,)), ((), ())), preferred_element_type=f32) + base[:, at]
             w = weight[:, at]
@@ -188,10 +179,11 @@
             part = lax.dot_general(slopes, r, (((0,), (0,)), ((), ())), preferred_element_type=f32)
             col = part if col is None else col + part
         (col_own, col_1, col_2, col_3)[j][...] = col.astype(f32 if j == 0 else bf16)
-    for h in range(2):
-        to = slice(h * 512, (h + 1) * 512)
-        row_own[to, :] = row_acc[h * 1024:h * 1024 + 512, :]
-        row_other[to, :] = row_acc[h * 1024 + 512:(h + 1) * 1024, :].astype(bf16)
+    core = lax.axis_index("col") % 2
+    for i in range(16):
+        to = slice(i * 64, (i + 1) * 64)
+        row_own[to, :] = row_acc[pl.ds(pl.multiple_of(i * 128 + core * 64, 64), 64), :]
+        row_other[to, :] = row_acc[pl.ds(pl.multiple_of(i * 128 + (1 - core) * 64, 64), 64), :].astype(bf16)
 
 
 def fold_kernel(n, *refs):
@@ -267,11 +259,11 @@
     )
     margs = log_total, row_marg, col_marg, counts
     a, b = call(second_kernel, [block(128)] * 2, (row, col, col_swap(out, 1)))
-    near = [hop(a, 2, 1), hop(b, 4, 1), hop(a, 6, 0)]
-    weight_a, base_a, token = slope_parts(0, *margs, after=(a,))
+    near = [hop(a, 2, 0), hop(b, 4, 1), hop(a, 6, 1)]
+    weight_a, base_a, token = slope_parts(0, FIRST, *margs, after=(a,))
     mine = list(call(third_kernel, [block(512)], (token, a, b, *near)))
     mine = mine + [hop(mine[0], 8 * k, 2 * k) for k in (2, 1, 3)]
-    weight_b, base_b, token = slope_parts(1, *margs, after=(mine[0],))
+    weight_b, base_b, token = slope_parts(FIRST, 16 - FIRST, *margs, after=(mine[0],))
     mine = mine[0:1] + [tie(x, token) for x in mine[1:]]
     got = [col_swap(x, 1) for x in mine]
 

time: 58.4 us -> 57.3 us (0.981)
  waiting for transfers between devices: 9.1 us -> 10.7 us
  starting transfers between devices: 32.8 us -> 31.3 us
  Pallas kernels: 14.8 us -> 13.6 us
    ppermute x6, waiting for transfers between devices: 3.04 us -> 4.81 us  [hop(): return lax.ppermute(x, ('row', 'col'), pairs)]
    ppermute x16, starting transfers between devices: 21.2 us -> 19.8 us  [swap(): return lax.ppermute(x, axis, [(i, i ^ flip) for i in range(size)])]
    pallas_call x14, Pallas kernels: 14.8 us -> 13.6 us  [call(): pl.pallas_call(kernel, in_specs=in_specs or [VM] * len(ins), out_specs=[V...]
  transfers between devices with their start and end apart: 22 -> 22, of which waited for: 8 -> 8; matrix products, arithmetic and copies ran while one was open for 0% -> 0% of each run, Pallas kernels for 15% -> 12%
where the time goes in v4:
time: 57.3 us; the launch traced here: 57 us
  starting transfers between devices  31.3 us (55%)
  Pallas kernels  13.6 us (24%)
  waiting for transfers between devices  10.7 us (19%)
  between operations  1.43 us (2%)
    ppermute x16, starting transfers between devices, swap(): return lax.ppermute(x, axis, [(i, i ^ flip) for i in range(size)])  19.8 us
    pallas_call x14, Pallas kernels, call(): pl.pallas_call(kernel, in_specs=in_specs or [VM] * len(ins), out_specs=[V...  13.6 us
    ppermute x6, starting transfers between devices, hop(): return lax.ppermute(x, ('row', 'col'), pairs)  11.5 us
    ppermute x16, waiting for transfers between devices, swap(): return lax.ppermute(x, axis, [(i, i ^ flip) for i in range(size)])  5.88 us
    ppermute x6, waiting for transfers between devices, hop(): return lax.ppermute(x, ('row', 'col'), pairs)  4.81 us
  transfers between devices with their start and end apart: 22, of which 8 were waited for; matrix products, arithmetic and copies ran while one was open for 0% of the time, Pallas kernels for 12%

profile of v4, /device:TPU:2, one launch (start us, length us, event | category | flops | bytes accessed | tf_op | source)
XLA Modules:
  0.0 57.0 jit_solution(14200986558110512911)
XLA Ops:
  0.6 1.0 %shard_map.111 = (bf16[64,256]{1,0:T(8,128)(2,1)S(1)}, bf16[128,256]{1,0:T(8,128)(2,1)S(1)}, bf16[128,256]{1,0:T(8,128)(2,1)S(1)}) custom-call(f32[64,256]{1,0:T(8,128)} %refs_4_.1, f32[128,256]{1,0:T(8,128)} %refs_2_.1), custom_call_target="tpu_custom_call" | custom-call | tf_op jit(solution)/shard_map/pallas_call | solution.py:18
  1.6 0.1 collective-permute-start
  1.7 1.2 %collective-permute-done.got = bf16[128,256]{1,0:T(8,128)(2,1)S(1)} collective-permute-done((bf16[128,256]{1,0:T(8,128)(2,1)S(1)}, bf16[128,256]{1,0:T(8,128)(2,1)S(1)}, u32[]{:S(2)}, u32[]{:S(2)}) %collective-permute-start) | collective-permute-done | bytes 65568 | tf_op jit(solution)/shard_map/ppermute | solution.py:235
  3.0 3.4 %collective-permute-start.2 = (bf16[128,256]{1,0:T(8,128)(2,1)S(1)}, bf16[128,256]{1,0:T(8,128)(2,1)S(1)}, u32[]{:S(2)}, u32[]{:S(2)}) collective-permute-start(bf16[128,256]{1,0:T(8,128)(2,1)S(1)} %get-tuple-element.42.b), channel_id=1, source_target_pairs={{0,4},{1,33},{2,6},{3,35},{4,0},{5,37},{6,2},{7,39},{8,12},{9,41},... | collective-permute-start | bytes 196616 | tf_op jit(solution)/shard_map/ppermute | solution.py:246
  6.3 1.5 %collective-permute-start.3 = (bf16[128,256]{1,0:T(8,128)(2,1)S(1)}, bf16[128,256]{1,0:T(8,128)(2,1)S(1)}, u32[]{:S(2)}, u32[]{:S(2)}) collective-permute-start(bf16[128,256]{1,0:T(8,128)(2,1)S(1)} %get-tuple-element.38.refs_0_.a), channel_id=1, source_target_pairs={{0,6},{1,33},{2,4},{3,35},{4,2},{5,37},{6,0},{7,39},{8,14},{9,41},... | collective-permute-start | bytes 196616 | tf_op jit(solution)/shard_map/ppermute | solution.py:246
  7.8 2.4 %collective-permute-start.1 = (bf16[128,256]{1,0:T(8,128)(2,1)S(1)}, bf16[128,256]{1,0:T(8,128)(2,1)S(1)}, u32[]{:S(2)}, u32[]{:S(2)}) collective-permute-start(bf16[128,256]{1,0:T(8,128)(2,1)S(1)} %get-tuple-element.38.refs_0_.a), channel_id=1, source_target_pairs={{0,2},{2,0},{4,6},{6,4},{8,10},{10,8},{12,14},{14,12},{16,18},{18,... | collective-permute-start | bytes 196616 | tf_op jit(solution)/shard_map/ppermute | solution.py:246
  10.8 2.5 %shard_map.113 = (f32[768,1024]{1,0:T(8,128)S(1)}, f32[768,1024]{1,0:T(8,128)S(1)}, f32[8,128]{1,0:T(8,128)S(1)}) custom-call(f32[1]{0:T(128)S(6)} %copy.12.log_total, s32[16,128]{1,0:T(8,128)} %bitcast.8, s32[8,128]{1,0:T(8,128)} %bitcast.10, s32[2048,1024]{1,0:T(8,128)} %counts.3, bf16[128,256]{1,0:T(8,128)(2,1)S(1)} %get-tuple-element.38.refs_0_.a), custom_call_target="tpu_custom_call" | custom-call | bytes 7864320 | tf_op jit(solution)/shard_map/pallas_call | solution.py:18
  13.3 0.1 collective-permute-done.3.g3
  13.5 2.6 %collective-permute-done.1.g1 = bf16[128,256]{1,0:T(8,128)(2,1)S(1)} collective-permute-done((bf16[128,256]{1,0:T(8,128)(2,1)S(1)}, bf16[128,256]{1,0:T(8,128)(2,1)S(1)}, u32[]{:S(2)}, u32[]{:S(2)}) %collective-permute-start.1) | collective-permute-done | bytes 65568 | tf_op jit(solution)/shard_map/ppermute | solution.py:246
  16.1 3.3 %collective-permute-start.4 = (bf16[512,256]{1,0:T(8,128)(2,1)S(1)}, bf16[512,256]{1,0:T(8,128)(2,1)S(1)}, u32[]{:S(2)}, u32[]{:S(2)}) collective-permute-start(bf16[512,256]{1,0:T(8,128)(2,1)S(1)} %shard_map.114.refs_0_), channel_id=1, source_target_pairs={{0,16},{1,129},{2,18},{3,131},{4,20},{5,133},{6,22},{7,135},{8,24}... | collective-permute-start | bytes 786440 | tf_op jit(solution)/shard_map/ppermute | solution.py:246
  19.4 0.7 %collective-permute-start.5 = (bf16[512,256]{1,0:T(8,128)(2,1)S(1)}, bf16[512,256]{1,0:T(8,128)(2,1)S(1)}, u32[]{:S(2)}, u32[]{:S(2)}) collective-permute-start(bf16[512,256]{1,0:T(8,128)(2,1)S(1)} %shard_map.114.refs_0_), channel_id=1, source_target_pairs={{0,8},{1,65},{2,10},{3,67},{4,12},{5,69},{6,14},{7,71},{8,0},{9,73... | collective-permute-start | bytes 786440 | tf_op jit(solution)/shard_map/ppermute | solution.py:246
  20.1 0.4 collective-permute-start.6
  20.5 0.9 %collective-permute-start.7 = (bf16[512,256]{1,0:T(8,128)(2,1)S(1)}, bf16[512,256]{1,0:T(8,128)(2,1)S(1)}, u32[]{:S(2)}, u32[]{:S(2)}) collective-permute-start(bf16[512,256]{1,0:T(8,128)(2,1)S(1)} %shard_map.114.refs_0_), channel_id=1, source_target_pairs={{0,1},{1,0},{2,3},{3,2},{4,5},{5,4},{6,7},{7,6},{8,9},{9,8},{10,11... | collective-permute-start | bytes 786440 | tf_op jit(solution)/shard_map/ppermute | solution.py:235
  21.3 3.5 %shard_map.115 = (f32[1280,1024]{1,0:T(8,128)S(1)}, f32[1280,1024]{1,0:T(8,128)S(1)}, f32[8,128]{1,0:T(8,128)S(1)}) custom-call(f32[1]{0:T(128)S(6)} %copy.12.log_total, s32[16,128]{1,0:T(8,128)} %bitcast.9, s32[8,128]{1,0:T(8,128)} %bitcast.11, s32[2048,1024]{1,0:T(8,128)} %counts.3, bf16[512,256]{1,0:T(8,128)(2,1)S(1)} %shard_map.114.refs_0_), custom_call_target="tpu_custom_call" | custom-call | bytes 13107200 | tf_op jit(solution)/shard_map/pallas_call | solution.py:18
  24.9 0.4 collective-permute-start.8
  25.2 2.0 %collective-permute-done.5.x = bf16[512,256]{1,0:T(8,128)(2,1)S(1)} collective-permute-done((bf16[512,256]{1,0:T(8,128)(2,1)S(1)}, bf16[512,256]{1,0:T(8,128)(2,1)S(1)}, u32[]{:S(2)}, u32[]{:S(2)}) %collective-permute-start.5) | collective-permute-done | bytes 262176 | tf_op jit(solution)/shard_map/ppermute | solution.py:246
  27.3 0.6 %collective-permute-start.9 = (bf16[512,256]{1,0:T(8,128)(2,1)S(1)}, bf16[512,256]{1,0:T(8,128)(2,1)S(1)}, u32[]{:S(2)}, u32[]{:S(2)}) collective-permute-start(bf16[512,256]{1,0:T(8,128)(2,1)S(1)} %shard_map.117.refs_2_), channel_id=1, source_target_pairs={{0,1},{1,0},{2,3},{3,2},{4,5},{5,4},{6,7},{7,6},{8,9},{9,8},{10,11... | collective-permute-start | bytes 786440 | tf_op jit(solution)/shard_map/ppermute | solution.py:235
  27.9 0.0 collective-permute-done.6.x
  27.9 0.1 collective-permute-start.10
  28.0 0.0 collective-permute-done.7.refs_4_
  28.0 0.0 collective-permute-done.8.refs_5_
  28.0 1.0 %collective-permute-done.9.refs_6_ = bf16[512,256]{1,0:T(8,128)(2,1)S(1)} collective-permute-done((bf16[512,256]{1,0:T(8,128)(2,1)S(1)}, bf16[512,256]{1,0:T(8,128)(2,1)S(1)}, u32[]{:S(2)}, u32[]{:S(2)}) %collective-permute-start.9) | collective-permute-done | bytes 262176 | tf_op jit(solution)/shard_map/ppermute | solution.py:235
  29.0 0.5 collective-permute-done.10.refs_7_
  29.5 4.6 %shard_map.119 = (f32[1024,256]{1,0:T(8,128)S(1)}, bf16[1024,256]{1,0:T(8,128)(2,1)S(1)}, f32[256,256]{1,0:T(8,128)S(1)}, bf16[256,256]{1,0:T(8,128)(2,1)S(1)}, ...) custom-call(f32[768,1024]{1,0:T(8,128)S(1)} %get-tuple-element.39.weight_a, ...), custom_call_target="tpu_custom_call" | custom-call | flops 3221225472 | bytes 16777216 | tf_op jit(solution)/shard_map/pallas_call | solution.py:18
  34.1 0.3 collective-permute-start.11
  34.4 1.9 %collective-permute-start.18 = (bf16[256,256]{1,0:T(8,128)(2,1)S(1)}, bf16[256,256]{1,0:T(8,128)(2,1)S(1)}, u32[]{:S(2)}, u32[]{:S(2)}) collective-permute-start(bf16[256,256]{1,0:T(8,128)(2,1)S(1)} %get-tuple-element.59), channel_id=1, source_target_pairs={{0,128},{32,160},{64,192},{96,224},{128,0},{160,32},{192,64},{224,... | collective-permute-start | bytes 393224 | tf_op jit(solution)/shard_map/ppermute | solution.py:235
  36.4 1.4 %collective-permute-start.19 = (bf16[256,256]{1,0:T(8,128)(2,1)S(1)}, bf16[256,256]{1,0:T(8,128)(2,1)S(1)}, u32[]{:S(2)}, u32[]{:S(2)}) collective-permute-start(bf16[256,256]{1,0:T(8,128)(2,1)S(1)} %get-tuple-element.60), channel_id=1, source_target_pairs={{0,64},{32,96},{64,0},{96,32},{128,192},{160,224},{192,128},{224,1... | collective-permute-start | bytes 393224 | tf_op jit(solution)/shard_map/ppermute | solution.py:235
  37.8 0.8 %collective-permute-start.20 = (bf16[256,256]{1,0:T(8,128)(2,1)S(1)}, bf16[256,256]{1,0:T(8,128)(2,1)S(1)}, u32[]{:S(2)}, u32[]{:S(2)}) collective-permute-start(bf16[256,256]{1,0:T(8,128)(2,1)S(1)} %get-tuple-element.61), channel_id=1, source_target_pairs={{0,192},{32,224},{64,128},{96,160},{128,64},{160,96},{192,0},{224,... | collective-permute-start | bytes 393224 | tf_op jit(solution)/shard_map/ppermute | solution.py:235
  38.6 0.0 collective-permute-done.11.refs_1_
  38.6 0.1 shard_map.120
  38.6 3.2 %collective-permute-start.12 = (bf16[256,256]{1,0:T(8,128)(2,1)S(1)}, bf16[256,256]{1,0:T(8,128)(2,1)S(1)}, u32[]{:S(2)}, u32[]{:S(2)}) collective-permute-start(bf16[256,256]{1,0:T(8,128)(2,1)S(1)} %get-tuple-element.49), channel_id=1, source_target_pairs={{0,16},{1,17},{2,18},{3,19},{4,20},{5,21},{6,22},{7,23},{8,24},{9,... | collective-permute-start | bytes 393224 | tf_op jit(solution)/shard_map/ppermute | solution.py:235
  41.9 0.7 %collective-permute-start.13 = (bf16[256,256]{1,0:T(8,128)(2,1)S(1)}, bf16[256,256]{1,0:T(8,128)(2,1)S(1)}, u32[]{:S(2)}, u32[]{:S(2)}) collective-permute-start(bf16[256,256]{1,0:T(8,128)(2,1)S(1)} %get-tuple-element.50), channel_id=1, source_target_pairs={{0,8},{1,9},{2,10},{3,11},{4,12},{5,13},{6,14},{7,15},{8,0},{9,1},... | collective-permute-start | bytes 393224 | tf_op jit(solution)/shard_map/ppermute | solution.py:235
  42.5 0.0 collective-permute-done.18.refs_1_
  42.5 2.7 %collective-permute-start.14 = (bf16[256,256]{1,0:T(8,128)(2,1)S(1)}, bf16[256,256]{1,0:T(8,128)(2,1)S(1)}, u32[]{:S(2)}, u32[]{:S(2)}) collective-permute-start(bf16[256,256]{1,0:T(8,128)(2,1)S(1)} %get-tuple-element.51), channel_id=1, source_target_pairs={{0,24},{1,25},{2,26},{3,27},{4,28},{5,29},{6,30},{7,31},{8,16},{9,... | collective-permute-start | bytes 393224 | tf_op jit(solution)/shard_map/ppermute | solution.py:235
  45.2 0.0 collective-permute-done.19.refs_2_
  45.2 0.0 collective-permute-done.20.refs_3_
  45.2 0.1 shard_map.123
  45.3 3.2 %collective-permute-start.21 = (bf16[128,256]{1,0:T(8,128)(2,1)S(1)}, bf16[128,256]{1,0:T(8,128)(2,1)S(1)}, u32[]{:S(2)}, u32[]{:S(2)}) collective-permute-start(bf16[128,256]{1,0:T(8,128)(2,1)S(1)} %get-tuple-element.63), channel_id=1, source_target_pairs={{0,32},{32,0},{64,96},{96,64},{128,160},{160,128},{192,224},{224,1... | collective-permute-start | bytes 196616 | tf_op jit(solution)/shard_map/ppermute | solution.py:235
  48.5 0.0 collective-permute-done.12.refs_1_
  48.5 0.0 collective-permute-done.13.refs_2_
  48.5 0.2 collective-permute-done.14.refs_3_
  48.7 0.1 shard_map.121
  48.8 1.0 %collective-permute-start.15 = (bf16[64,256]{1,0:T(8,128)(2,1)S(1)}, bf16[64,256]{1,0:T(8,128)(2,1)S(1)}, u32[]{:S(2)}, u32[]{:S(2)}) collective-permute-start(bf16[64,256]{1,0:T(8,128)(2,1)S(1)} %get-tuple-element.53), channel_id=1, source_target_pairs={{0,4},{1,5},{2,6},{3,7},{4,0},{5,1},{6,2},{7,3},{8,12},{9,13},{10,... | collective-permute-start | bytes 98312 | tf_op jit(solution)/shard_map/ppermute | solution.py:235
  49.8 2.1 %collective-permute-start.16 = (bf16[64,256]{1,0:T(8,128)(2,1)S(1)}, bf16[64,256]{1,0:T(8,128)(2,1)S(1)}, u32[]{:S(2)}, u32[]{:S(2)}) collective-permute-start(bf16[64,256]{1,0:T(8,128)(2,1)S(1)} %get-tuple-element.54), channel_id=1, source_target_pairs={{0,6},{1,7},{2,4},{3,5},{4,2},{5,3},{6,0},{7,1},{8,14},{9,15},{10,... | collective-permute-start | bytes 98312 | tf_op jit(solution)/shard_map/ppermute | solution.py:235
  51.9 0.4 collective-permute-start.17
  52.4 2.9 %collective-permute-done.21.refs_1_ = bf16[128,256]{1,0:T(8,128)(2,1)S(1)} collective-permute-done((bf16[128,256]{1,0:T(8,128)(2,1)S(1)}, bf16[128,256]{1,0:T(8,128)(2,1)S(1)}, u32[]{:S(2)}, u32[]{:S(2)}) %collective-permute-start.21) | collective-permute-done | bytes 65568 | tf_op jit(solution)/shard_map/ppermute | solution.py:235
  55.2 0.9 %shard_map.124 = (f32[128,256]{1,0:T(8,128)}, f32[1,128]{1,0:T(1,128)}) custom-call(f32[128,256]{1,0:T(8,128)S(1)} %get-tuple-element.62.refs_0_, bf16[128,256]{1,0:T(8,128)(2,1)S(1)} %collective-permute-done.21.refs_1_, f32[128,256]{1,0:T(8,128)S(1)} %copy-done, f32[1,128]{1,0:T(1,128)S(1)} %bitcast.6), custom_call_target="tpu_custom_call" | custom-call | tf_op jit(solution)/shard_map/pallas_call | solution.py:18
  56.1 0.9 %shard_map.122 = (f32[64,256]{1,0:T(8,128)}, f32[1,64]{1,0:T(1,128)}) custom-call(f32[64,256]{1,0:T(8,128)S(1)} %get-tuple-element.52.refs_0_, bf16[64,256]{1,0:T(8,128)(2,1)S(1)} %collective-permute-done.15.refs_1_, bf16[64,256]{1,0:T(8,128)(2,1)S(1)} %collective-permute-done.16.refs_2_, bf16[64,256]{1,0:T(8,128)(2,1)S(1)} %collective-permute-done.17.refs_3_, ...), custom_call_target="tpu_custom_call" | custom-call | tf_op jit(solution)/shard_map/pallas_call | solution.py:18
  (18 shorter events, 0.1 us)
Async XLA Ops:
  1.6 1.3 %collective-permute-start = (bf16[128,256]{1,0:T(8,128)(2,1)S(1)}, bf16[128,256]{1,0:T(8,128)(2,1)S(1)}, u32[]{:S(2)}, u32[]{:S(2)}) collective-permute-start(bf16[128,256]{1,0:T(8,128)(2,1)S(1)} %get-tuple-element.37), channel_id=1, source_target_pairs={{0,1},{1,0},{2,3},{3,2},{4,5},{5,4},{6,7},{7,6},{8,9},{9,8},{10,11... | collective-permute-start | bytes 196616 | tf_op jit(solution)/shard_map/ppermute | solution.py:235
  3.0 10.3 %collective-permute-start.2 = (bf16[128,256]{1,0:T(8,128)(2,1)S(1)}, bf16[128,256]{1,0:T(8,128)(2,1)S(1)}, u32[]{:S(2)}, u32[]{:S(2)}) collective-permute-start(bf16[128,256]{1,0:T(8,128)(2,1)S(1)} %get-tuple-element.42.b), channel_id=1, source_target_pairs={{0,4},{1,33},{2,6},{3,35},{4,0},{5,37},{6,2},{7,39},{8,12},{9,41},... | collective-permute-start | bytes 196616 | tf_op jit(solution)/shard_map/ppermute | solution.py:246
  6.3 7.1 %collective-permute-start.3 = (bf16[128,256]{1,0:T(8,128)(2,1)S(1)}, bf16[128,256]{1,0:T(8,128)(2,1)S(1)}, u32[]{:S(2)}, u32[]{:S(2)}) collective-permute-start(bf16[128,256]{1,0:T(8,128)(2,1)S(1)} %get-tuple-element.38.refs_0_.a), channel_id=1, source_target_pairs={{0,6},{1,33},{2,4},{3,35},{4,2},{5,37},{6,0},{7,39},{8,14},{9,41},... | collective-permute-start | bytes 196616 | tf_op jit(solution)/shard_map/ppermute | solution.py:246
  7.8 8.3 %collective-permute-start.1 = (bf16[128,256]{1,0:T(8,128)(2,1)S(1)}, bf16[128,256]{1,0:T(8,128)(2,1)S(1)}, u32[]{:S(2)}, u32[]{:S(2)}) collective-permute-start(bf16[128,256]{1,0:T(8,128)(2,1)S(1)} %get-tuple-element.38.refs_0_.a), channel_id=1, source_target_pairs={{0,2},{2,0},{4,6},{6,4},{8,10},{10,8},{12,14},{14,12},{16,18},{18,... | collective-permute-start | bytes 196616 | tf_op jit(solution)/shard_map/ppermute | solution.py:246
  16.1 8.7 %collective-permute-start.4 = (bf16[512,256]{1,0:T(8,128)(2,1)S(1)}, bf16[512,256]{1,0:T(8,128)(2,1)S(1)}, u32[]{:S(2)}, u32[]{:S(2)}) collective-permute-start(bf16[512,256]{1,0:T(8,128)(2,1)S(1)} %shard_map.114.refs_0_), channel_id=1, source_target_pairs={{0,16},{1,129},{2,18},{3,131},{4,20},{5,133},{6,22},{7,135},{8,24}... | collective-permute-start | bytes 786440 | tf_op jit(solution)/shard_map/ppermute | solution.py:246
  19.4 7.9 %collective-permute-start.5 = (bf16[512,256]{1,0:T(8,128)(2,1)S(1)}, bf16[512,256]{1,0:T(8,128)(2,1)S(1)}, u32[]{:S(2)}, u32[]{:S(2)}) collective-permute-start(bf16[512,256]{1,0:T(8,128)(2,1)S(1)} %shard_map.114.refs_0_), channel_id=1, source_target_pairs={{0,8},{1,65},{2,10},{3,67},{4,12},{5,69},{6,14},{7,71},{8,0},{9,73... | collective-permute-start | bytes 786440 | tf_op jit(solution)/shard_map/ppermute | solution.py:246
  20.1 7.8 %collective-permute-start.6 = (bf16[512,256]{1,0:T(8,128)(2,1)S(1)}, bf16[512,256]{1,0:T(8,128)(2,1)S(1)}, u32[]{:S(2)}, u32[]{:S(2)}) collective-permute-start(bf16[512,256]{1,0:T(8,128)(2,1)S(1)} %shard_map.114.refs_0_), channel_id=1, source_target_pairs={{0,24},{1,193},{2,26},{3,195},{4,28},{5,197},{6,30},{7,199},{8,16}... | collective-permute-start | bytes 786440 | tf_op jit(solution)/shard_map/ppermute | solution.py:246
  20.5 7.6 %collective-permute-start.7 = (bf16[512,256]{1,0:T(8,128)(2,1)S(1)}, bf16[512,256]{1,0:T(8,128)(2,1)S(1)}, u32[]{:S(2)}, u32[]{:S(2)}) collective-permute-start(bf16[512,256]{1,0:T(8,128)(2,1)S(1)} %shard_map.114.refs_0_), channel_id=1, source_target_pairs={{0,1},{1,0},{2,3},{3,2},{4,5},{5,4},{6,7},{7,6},{8,9},{9,8},{10,11... | collective-permute-start | bytes 786440 | tf_op jit(solution)/shard_map/ppermute | solution.py:235
  24.9 3.2 %collective-permute-start.8 = (bf16[512,256]{1,0:T(8,128)(2,1)S(1)}, bf16[512,256]{1,0:T(8,128)(2,1)S(1)}, u32[]{:S(2)}, u32[]{:S(2)}) collective-permute-start(bf16[512,256]{1,0:T(8,128)(2,1)S(1)} %shard_map.116.refs_1_), channel_id=1, source_target_pairs={{0,1},{1,0},{2,3},{3,2},{4,5},{5,4},{6,7},{7,6},{8,9},{9,8},{10,11... | collective-permute-start | bytes 786440 | tf_op jit(solution)/shard_map/ppermute | solution.py:235
  27.3 1.7 %collective-permute-start.9 = (bf16[512,256]{1,0:T(8,128)(2,1)S(1)}, bf16[512,256]{1,0:T(8,128)(2,1)S(1)}, u32[]{:S(2)}, u32[]{:S(2)}) collective-permute-start(bf16[512,256]{1,0:T(8,128)(2,1)S(1)} %shard_map.117.refs_2_), channel_id=1, source_target_pairs={{0,1},{1,0},{2,3},{3,2},{4,5},{5,4},{6,7},{7,6},{8,9},{9,8},{10,11... | collective-permute-start | bytes 786440 | tf_op jit(solution)/shard_map/ppermute | solution.py:235
  27.9 1.6 %collective-permute-start.10 = (bf16[512,256]{1,0:T(8,128)(2,1)S(1)}, bf16[512,256]{1,0:T(8,128)(2,1)S(1)}, u32[]{:S(2)}, u32[]{:S(2)}) collective-permute-start(bf16[512,256]{1,0:T(8,128)(2,1)S(1)} %shard_map.118.refs_3_), channel_id=1, source_target_pairs={{0,1},{1,0},{2,3},{3,2},{4,5},{5,4},{6,7},{7,6},{8,9},{9,8},{10,11... | collective-permute-start | bytes 786440 | tf_op jit(solution)/shard_map/ppermute | solution.py:235
  29.5 25.7 %copy-start = (f32[128,256]{1,0:T(8,128)S(1)}, f32[128,256]{1,0:T(8,128)}, u32[]{:S(2)}) copy-start(f32[128,256]{1,0:T(8,128)} %refs_2_.1) | copy-start | bytes 393220
  29.5 25.7 %copy-start.2 = (f32[128]{0:T(128)S(1)}, f32[128]{0:T(128)}, u32[]{:S(2)}) copy-start(f32[128]{0:T(128)} %param.15) | copy-start | bytes 1540
  29.5 26.6 %copy-start.1 = (f32[64,256]{1,0:T(8,128)S(1)}, f32[64,256]{1,0:T(8,128)}, u32[]{:S(2)}) copy-start(f32[64,256]{1,0:T(8,128)} %refs_4_.1) | copy-start | bytes 196612
  29.5 26.6 %copy-start.3 = (f32[64]{0:T(128)S(1)}, f32[64]{0:T(128)}, u32[]{:S(2)}) copy-start(f32[64]{0:T(128)} %param.13) | copy-start | bytes 772
  34.1 4.5 %collective-permute-start.11 = (bf16[1024,256]{1,0:T(8,128)(2,1)S(1)}, bf16[1024,256]{1,0:T(8,128)(2,1)S(1)}, u32[]{:S(2)}, u32[]{:S(2)}) collective-permute-start(bf16[1024,256]{1,0:T(8,128)(2,1)S(1)} %get-tuple-element.47), channel_id=1, source_target_pairs={{0,1},{1,0},{2,3},{3,2},{4,5},{5,4},{6,7},{7,6},{8,9},{9,8},{10,11... | collective-permute-start | bytes 1572872 | tf_op jit(solution)/shard_map/ppermute | solution.py:235
  34.4 8.1 %collective-permute-start.18 = (bf16[256,256]{1,0:T(8,128)(2,1)S(1)}, bf16[256,256]{1,0:T(8,128)(2,1)S(1)}, u32[]{:S(2)}, u32[]{:S(2)}) collective-permute-start(bf16[256,256]{1,0:T(8,128)(2,1)S(1)} %get-tuple-element.59), channel_id=1, source_target_pairs={{0,128},{32,160},{64,192},{96,224},{128,0},{160,32},{192,64},{224,... | collective-permute-start | bytes 393224 | tf_op jit(solution)/shard_map/ppermute | solution.py:235
  36.4 8.9 %collective-permute-start.19 = (bf16[256,256]{1,0:T(8,128)(2,1)S(1)}, bf16[256,256]{1,0:T(8,128)(2,1)S(1)}, u32[]{:S(2)}, u32[]{:S(2)}) collective-permute-start(bf16[256,256]{1,0:T(8,128)(2,1)S(1)} %get-tuple-element.60), channel_id=1, source_target_pairs={{0,64},{32,96},{64,0},{96,32},{128,192},{160,224},{192,128},{224,1... | collective-permute-start | bytes 393224 | tf_op jit(solution)/shard_map/ppermute | solution.py:235
  37.8 7.4 %collective-permute-start.20 = (bf16[256,256]{1,0:T(8,128)(2,1)S(1)}, bf16[256,256]{1,0:T(8,128)(2,1)S(1)}, u32[]{:S(2)}, u32[]{:S(2)}) collective-permute-start(bf16[256,256]{1,0:T(8,128)(2,1)S(1)} %get-tuple-element.61), channel_id=1, source_target_pairs={{0,192},{32,224},{64,128},{96,160},{128,64},{160,96},{192,0},{224,... | collective-permute-start | bytes 393224 | tf_op jit(solution)/shard_map/ppermute | solution.py:235
  38.6 9.8 %collective-permute-start.12 = (bf16[256,256]{1,0:T(8,128)(2,1)S(1)}, bf16[256,256]{1,0:T(8,128)(2,1)S(1)}, u32[]{:S(2)}, u32[]{:S(2)}) collective-permute-start(bf16[256,256]{1,0:T(8,128)(2,1)S(1)} %get-tuple-element.49), channel_id=1, source_target_pairs={{0,16},{1,17},{2,18},{3,19},{4,20},{5,21},{6,22},{7,23},{8,24},{9,... | collective-permute-start | bytes 393224 | tf_op jit(solution)/shard_map/ppermute | solution.py:235
  41.9 6.6 %collective-permute-start.13 = (bf16[256,256]{1,0:T(8,128)(2,1)S(1)}, bf16[256,256]{1,0:T(8,128)(2,1)S(1)}, u32[]{:S(2)}, u32[]{:S(2)}) collective-permute-start(bf16[256,256]{1,0:T(8,128)(2,1)S(1)} %get-tuple-element.50), channel_id=1, source_target_pairs={{0,8},{1,9},{2,10},{3,11},{4,12},{5,13},{6,14},{7,15},{8,0},{9,1},... | collective-permute-start | bytes 393224 | tf_op jit(solution)/shard_map/ppermute | solution.py:235
  42.5 6.2 %collective-permute-start.14 = (bf16[256,256]{1,0:T(8,128)(2,1)S(1)}, bf16[256,256]{1,0:T(8,128)(2,1)S(1)}, u32[]{:S(2)}, u32[]{:S(2)}) collective-permute-start(bf16[256,256]{1,0:T(8,128)(2,1)S(1)} %get-tuple-element.51), channel_id=1, source_target_pairs={{0,24},{1,25},{2,26},{3,27},{4,28},{5,29},{6,30},{7,31},{8,16},{9,... | collective-permute-start | bytes 393224 | tf_op jit(solution)/shard_map/ppermute | solution.py:235
  45.3 9.9 %collective-permute-start.21 = (bf16[128,256]{1,0:T(8,128)(2,1)S(1)}, bf16[128,256]{1,0:T(8,128)(2,1)S(1)}, u32[]{:S(2)}, u32[]{:S(2)}) collective-permute-start(bf16[128,256]{1,0:T(8,128)(2,1)S(1)} %get-tuple-element.63), channel_id=1, source_target_pairs={{0,32},{32,0},{64,96},{96,64},{128,160},{160,128},{192,224},{224,1... | collective-permute-start | bytes 196616 | tf_op jit(solution)/shard_map/ppermute | solution.py:235
  48.8 7.3 %collective-permute-start.15 = (bf16[64,256]{1,0:T(8,128)(2,1)S(1)}, bf16[64,256]{1,0:T(8,128)(2,1)S(1)}, u32[]{:S(2)}, u32[]{:S(2)}) collective-permute-start(bf16[64,256]{1,0:T(8,128)(2,1)S(1)} %get-tuple-element.53), channel_id=1, source_target_pairs={{0,4},{1,5},{2,6},{3,7},{4,0},{5,1},{6,2},{7,3},{8,12},{9,13},{10,... | collective-permute-start | bytes 98312 | tf_op jit(solution)/shard_map/ppermute | solution.py:235
  49.8 6.3 %collective-permute-start.16 = (bf16[64,256]{1,0:T(8,128)(2,1)S(1)}, bf16[64,256]{1,0:T(8,128)(2,1)S(1)}, u32[]{:S(2)}, u32[]{:S(2)}) collective-permute-start(bf16[64,256]{1,0:T(8,128)(2,1)S(1)} %get-tuple-element.54), channel_id=1, source_target_pairs={{0,6},{1,7},{2,4},{3,5},{4,2},{5,3},{6,0},{7,1},{8,14},{9,15},{10,... | collective-permute-start | bytes 98312 | tf_op jit(solution)/shard_map/ppermute | solution.py:235
  51.9 4.2 %collective-permute-start.17 = (bf16[64,256]{1,0:T(8,128)(2,1)S(1)}, bf16[64,256]{1,0:T(8,128)(2,1)S(1)}, u32[]{:S(2)}, u32[]{:S(2)}) collective-permute-start(bf16[64,256]{1,0:T(8,128)(2,1)S(1)} %get-tuple-element.55), channel_id=1, source_target_pairs={{0,2},{1,3},{2,0},{3,1},{4,6},{5,7},{6,4},{7,5},{8,10},{9,11},{10,... | collective-permute-start | bytes 98312 | tf_op jit(solution)/shard_map/ppermute | solution.py:235

commit v5 on v4

--- a/solution.py
+++ b/solution.py
@@ -264,7 +264,7 @@
     mine = list(call(third_kernel, [block(512)], (token, a, b, *near)))
     mine = mine + [hop(mine[0], 8 * k, 2 * k) for k in (2, 1, 3)]
     weight_b, base_b, token = slope_parts(FIRST, 16 - FIRST, *margs, after=(mine[0],))
-    mine = mine[0:1] + [tie(x, token) for x in mine[1:]]
+    mine = [tie(x, token) for x in mine]
     got = [col_swap(x, 1) for x in mine]
 
     row_own, row_other, col_own, *col_send = call(

time: 57.3 us -> 57.3 us (level)
    pallas_call x14 -> x15, Pallas kernels: 13.6 us -> 13.6 us  [call(): pl.pallas_call(kernel, in_specs=in_specs or [VM] * len(ins), out_specs=[V...]
  transfers between devices with their start and end apart: 22 -> 22, of which waited for: 8 -> 8; matrix products, arithmetic and copies ran while one was open for 0% -> 0% of each run, Pallas kernels for 12% -> 13%
where the time goes in v5:
time: 57.3 us; the launch traced here: 57 us
  starting transfers between devices  31.3 us (55%)
  Pallas kernels  13.6 us (24%)
  waiting for transfers between devices  10.7 us (19%)
  between operations  1.42 us (2%)
    ppermute x16, starting transfers between devices, swap(): return lax.ppermute(x, axis, [(i, i ^ flip) for i in range(size)])  19.8 us
    pallas_call x15, Pallas kernels, call(): pl.pallas_call(kernel, in_specs=in_specs or [VM] * len(ins), out_specs=[V...  13.6 us
    ppermute x6, starting transfers between devices, hop(): return lax.ppermute(x, ('row', 'col'), pairs)  11.5 us
    ppermute x16, waiting for transfers between devices, swap(): return lax.ppermute(x, axis, [(i, i ^ flip) for i in range(size)])  5.88 us
    ppermute x6, waiting for transfers between devices, hop(): return lax.ppermute(x, ('row', 'col'), pairs)  4.81 us
  transfers between devices with their start and end apart: 22, of which 8 were waited for; matrix products, arithmetic and copies ran while one was open for 0% of the time, Pallas kernels for 13%

profile of v5, /device:TPU:2, one launch (start us, length us, event | category | flops | bytes accessed | tf_op | source)
XLA Modules:
  0.0 57.0 jit_solution(12629735275237189468)
XLA Ops:
  0.6 1.0 %shard_map.111 = (bf16[64,256]{1,0:T(8,128)(2,1)S(1)}, bf16[128,256]{1,0:T(8,128)(2,1)S(1)}, bf16[128,256]{1,0:T(8,128)(2,1)S(1)}) custom-call(f32[64,256]{1,0:T(8,128)} %refs_4_.1, f32[128,256]{1,0:T(8,128)} %refs_2_.1), custom_call_target="tpu_custom_call" | custom-call | tf_op jit(solution)/shard_map/pallas_call | solution.py:18
  1.6 0.1 collective-permute-start
  1.7 1.2 %collective-permute-done.got = bf16[128,256]{1,0:T(8,128)(2,1)S(1)} collective-permute-done((bf16[128,256]{1,0:T(8,128)(2,1)S(1)}, bf16[128,256]{1,0:T(8,128)(2,1)S(1)}, u32[]{:S(2)}, u32[]{:S(2)}) %collective-permute-start) | collective-permute-done | bytes 65568 | tf_op jit(solution)/shard_map/ppermute | solution.py:235
  3.0 3.4 %collective-permute-start.2 = (bf16[128,256]{1,0:T(8,128)(2,1)S(1)}, bf16[128,256]{1,0:T(8,128)(2,1)S(1)}, u32[]{:S(2)}, u32[]{:S(2)}) collective-permute-start(bf16[128,256]{1,0:T(8,128)(2,1)S(1)} %get-tuple-element.42.b), channel_id=1, source_target_pairs={{0,4},{1,33},{2,6},{3,35},{4,0},{5,37},{6,2},{7,39},{8,12},{9,41},... | collective-permute-start | bytes 196616 | tf_op jit(solution)/shard_map/ppermute | solution.py:246
  6.3 1.5 %collective-permute-start.3 = (bf16[128,256]{1,0:T(8,128)(2,1)S(1)}, bf16[128,256]{1,0:T(8,128)(2,1)S(1)}, u32[]{:S(2)}, u32[]{:S(2)}) collective-permute-start(bf16[128,256]{1,0:T(8,128)(2,1)S(1)} %get-tuple-element.38.refs_0_.a), channel_id=1, source_target_pairs={{0,6},{1,33},{2,4},{3,35},{4,2},{5,37},{6,0},{7,39},{8,14},{9,41},... | collective-permute-start | bytes 196616 | tf_op jit(solution)/shard_map/ppermute | solution.py:246
  7.8 2.4 %collective-permute-start.1 = (bf16[128,256]{1,0:T(8,128)(2,1)S(1)}, bf16[128,256]{1,0:T(8,128)(2,1)S(1)}, u32[]{:S(2)}, u32[]{:S(2)}) collective-permute-start(bf16[128,256]{1,0:T(8,128)(2,1)S(1)} %get-tuple-element.38.refs_0_.a), channel_id=1, source_target_pairs={{0,2},{2,0},{4,6},{6,4},{8,10},{10,8},{12,14},{14,12},{16,18},{18,... | collective-permute-start | bytes 196616 | tf_op jit(solution)/shard_map/ppermute | solution.py:246
  10.8 2.5 %shard_map.113 = (f32[768,1024]{1,0:T(8,128)S(1)}, f32[768,1024]{1,0:T(8,128)S(1)}, f32[8,128]{1,0:T(8,128)S(1)}) custom-call(f32[1]{0:T(128)S(6)} %copy.12.log_total, s32[16,128]{1,0:T(8,128)} %bitcast.8, s32[8,128]{1,0:T(8,128)} %bitcast.10, s32[2048,1024]{1,0:T(8,128)} %counts.3, bf16[128,256]{1,0:T(8,128)(2,1)S(1)} %get-tuple-element.38.refs_0_.a), custom_call_target="tpu_custom_call" | custom-call | bytes 7864320 | tf_op jit(solution)/shard_map/pallas_call | solution.py:18
  13.3 0.1 collective-permute-done.3.g3
  13.5 2.6 %collective-permute-done.1.g1 = bf16[128,256]{1,0:T(8,128)(2,1)S(1)} collective-permute-done((bf16[128,256]{1,0:T(8,128)(2,1)S(1)}, bf16[128,256]{1,0:T(8,128)(2,1)S(1)}, u32[]{:S(2)}, u32[]{:S(2)}) %collective-permute-start.1) | collective-permute-done | bytes 65568 | tf_op jit(solution)/shard_map/ppermute | solution.py:246
  16.1 3.3 %collective-permute-start.4 = (bf16[512,256]{1,0:T(8,128)(2,1)S(1)}, bf16[512,256]{1,0:T(8,128)(2,1)S(1)}, u32[]{:S(2)}, u32[]{:S(2)}) collective-permute-start(bf16[512,256]{1,0:T(8,128)(2,1)S(1)} %shard_map.114.refs_0_.x), channel_id=1, source_target_pairs={{0,16},{1,129},{2,18},{3,131},{4,20},{5,133},{6,22},{7,135},{8,24}... | collective-permute-start | bytes 786440 | tf_op jit(solution)/shard_map/ppermute | solution.py:246
  19.4 0.7 %collective-permute-start.5 = (bf16[512,256]{1,0:T(8,128)(2,1)S(1)}, bf16[512,256]{1,0:T(8,128)(2,1)S(1)}, u32[]{:S(2)}, u32[]{:S(2)}) collective-permute-start(bf16[512,256]{1,0:T(8,128)(2,1)S(1)} %shard_map.114.refs_0_.x), channel_id=1, source_target_pairs={{0,8},{1,65},{2,10},{3,67},{4,12},{5,69},{6,14},{7,71},{8,0},{9,73... | collective-permute-start | bytes 786440 | tf_op jit(solution)/shard_map/ppermute | solution.py:246
  20.1 0.4 collective-permute-start.6
  20.5 3.5 %shard_map.115 = (f32[1280,1024]{1,0:T(8,128)S(1)}, f32[1280,1024]{1,0:T(8,128)S(1)}, f32[8,128]{1,0:T(8,128)S(1)}) custom-call(f32[1]{0:T(128)S(6)} %copy.12.log_total, s32[16,128]{1,0:T(8,128)} %bitcast.9, s32[8,128]{1,0:T(8,128)} %bitcast.11, s32[2048,1024]{1,0:T(8,128)} %counts.3, bf16[512,256]{1,0:T(8,128)(2,1)S(1)} %shard_map.114.refs_0_.x), custom_call_target="tpu_custom_call" | custom-call | bytes 13107200 | tf_op jit(solution)/shard_map/pallas_call | solution.py:18
  24.0 1.0 %collective-permute-start.7 = (bf16[512,256]{1,0:T(8,128)(2,1)S(1)}, bf16[512,256]{1,0:T(8,128)(2,1)S(1)}, u32[]{:S(2)}, u32[]{:S(2)}) collective-permute-start(bf16[512,256]{1,0:T(8,128)(2,1)S(1)} %shard_map.116.refs_0_), channel_id=1, source_target_pairs={{0,1},{1,0},{2,3},{3,2},{4,5},{5,4},{6,7},{7,6},{8,9},{9,8},{10,11... | collective-permute-start | bytes 786440 | tf_op jit(solution)/shard_map/ppermute | solution.py:235
  24.9 0.0 collective-permute-done.4.x
  25.0 0.3 collective-permute-start.8
  25.2 2.0 %collective-permute-done.5.x = bf16[512,256]{1,0:T(8,128)(2,1)S(1)} collective-permute-done((bf16[512,256]{1,0:T(8,128)(2,1)S(1)}, bf16[512,256]{1,0:T(8,128)(2,1)S(1)}, u32[]{:S(2)}, u32[]{:S(2)}) %collective-permute-start.5) | collective-permute-done | bytes 262176 | tf_op jit(solution)/shard_map/ppermute | solution.py:246
  27.3 0.6 %collective-permute-start.9 = (bf16[512,256]{1,0:T(8,128)(2,1)S(1)}, bf16[512,256]{1,0:T(8,128)(2,1)S(1)}, u32[]{:S(2)}, u32[]{:S(2)}) collective-permute-start(bf16[512,256]{1,0:T(8,128)(2,1)S(1)} %shard_map.118.refs_2_), channel_id=1, source_target_pairs={{0,1},{1,0},{2,3},{3,2},{4,5},{5,4},{6,7},{7,6},{8,9},{9,8},{10,11... | collective-permute-start | bytes 786440 | tf_op jit(solution)/shard_map/ppermute | solution.py:235
  27.9 0.0 collective-permute-done.6.x
  27.9 0.1 collective-permute-start.10
  28.0 0.0 collective-permute-done.7.refs_4_
  28.0 0.0 collective-permute-done.8.refs_5_
  28.0 1.0 %collective-permute-done.9.refs_6_ = bf16[512,256]{1,0:T(8,128)(2,1)S(1)} collective-permute-done((bf16[512,256]{1,0:T(8,128)(2,1)S(1)}, bf16[512,256]{1,0:T(8,128)(2,1)S(1)}, u32[]{:S(2)}, u32[]{:S(2)}) %collective-permute-start.9) | collective-permute-done | bytes 262176 | tf_op jit(solution)/shard_map/ppermute | solution.py:235
  29.0 0.5 collective-permute-done.10.refs_7_
  29.5 4.6 %shard_map.120 = (f32[1024,256]{1,0:T(8,128)S(1)}, bf16[1024,256]{1,0:T(8,128)(2,1)S(1)}, f32[256,256]{1,0:T(8,128)S(1)}, bf16[256,256]{1,0:T(8,128)(2,1)S(1)}, ...) custom-call(f32[768,1024]{1,0:T(8,128)S(1)} %get-tuple-element.39.weight_a, ...), custom_call_target="tpu_custom_call" | custom-call | flops 3221225472 | bytes 16777216 | tf_op jit(solution)/shard_map/pallas_call | solution.py:18
  34.1 0.3 collective-permute-start.11
  34.4 1.9 %collective-permute-start.18 = (bf16[256,256]{1,0:T(8,128)(2,1)S(1)}, bf16[256,256]{1,0:T(8,128)(2,1)S(1)}, u32[]{:S(2)}, u32[]{:S(2)}) collective-permute-start(bf16[256,256]{1,0:T(8,128)(2,1)S(1)} %get-tuple-element.59), channel_id=1, source_target_pairs={{0,128},{32,160},{64,192},{96,224},{128,0},{160,32},{192,64},{224,... | collective-permute-start | bytes 393224 | tf_op jit(solution)/shard_map/ppermute | solution.py:235
  36.4 1.4 %collective-permute-start.19 = (bf16[256,256]{1,0:T(8,128)(2,1)S(1)}, bf16[256,256]{1,0:T(8,128)(2,1)S(1)}, u32[]{:S(2)}, u32[]{:S(2)}) collective-permute-start(bf16[256,256]{1,0:T(8,128)(2,1)S(1)} %get-tuple-element.60), channel_id=1, source_target_pairs={{0,64},{32,96},{64,0},{96,32},{128,192},{160,224},{192,128},{224,1... | collective-permute-start | bytes 393224 | tf_op jit(solution)/shard_map/ppermute | solution.py:235
  37.8 0.8 %collective-permute-start.20 = (bf16[256,256]{1,0:T(8,128)(2,1)S(1)}, bf16[256,256]{1,0:T(8,128)(2,1)S(1)}, u32[]{:S(2)}, u32[]{:S(2)}) collective-permute-start(bf16[256,256]{1,0:T(8,128)(2,1)S(1)} %get-tuple-element.61), channel_id=1, source_target_pairs={{0,192},{32,224},{64,128},{96,160},{128,64},{160,96},{192,0},{224,... | collective-permute-start | bytes 393224 | tf_op jit(solution)/shard_map/ppermute | solution.py:235
  38.6 0.0 collective-permute-done.11.refs_1_
  38.6 0.1 shard_map.121
  38.6 3.2 %collective-permute-start.12 = (bf16[256,256]{1,0:T(8,128)(2,1)S(1)}, bf16[256,256]{1,0:T(8,128)(2,1)S(1)}, u32[]{:S(2)}, u32[]{:S(2)}) collective-permute-start(bf16[256,256]{1,0:T(8,128)(2,1)S(1)} %get-tuple-element.49), channel_id=1, source_target_pairs={{0,16},{1,17},{2,18},{3,19},{4,20},{5,21},{6,22},{7,23},{8,24},{9,... | collective-permute-start | bytes 393224 | tf_op jit(solution)/shard_map/ppermute | solution.py:235
  41.9 0.7 %collective-permute-start.13 = (bf16[256,256]{1,0:T(8,128)(2,1)S(1)}, bf16[256,256]{1,0:T(8,128)(2,1)S(1)}, u32[]{:S(2)}, u32[]{:S(2)}) collective-permute-start(bf16[256,256]{1,0:T(8,128)(2,1)S(1)} %get-tuple-element.50), channel_id=1, source_target_pairs={{0,8},{1,9},{2,10},{3,11},{4,12},{5,13},{6,14},{7,15},{8,0},{9,1},... | collective-permute-start | bytes 393224 | tf_op jit(solution)/shard_map/ppermute | solution.py:235
  42.5 0.0 collective-permute-done.18.refs_1_
  42.5 2.7 %collective-permute-start.14 = (bf16[256,256]{1,0:T(8,128)(2,1)S(1)}, bf16[256,256]{1,0:T(8,128)(2,1)S(1)}, u32[]{:S(2)}, u32[]{:S(2)}) collective-permute-start(bf16[256,256]{1,0:T(8,128)(2,1)S(1)} %get-tuple-element.51), channel_id=1, source_target_pairs={{0,24},{1,25},{2,26},{3,27},{4,28},{5,29},{6,30},{7,31},{8,16},{9,... | collective-permute-start | bytes 393224 | tf_op jit(solution)/shard_map/ppermute | solution.py:235
  45.2 0.0 collective-permute-done.19.refs_2_
  45.2 0.0 collective-permute-done.20.refs_3_
  45.2 0.1 shard_map.124
  45.3 3.2 %collective-permute-start.21 = (bf16[128,256]{1,0:T(8,128)(2,1)S(1)}, bf16[128,256]{1,0:T(8,128)(2,1)S(1)}, u32[]{:S(2)}, u32[]{:S(2)}) collective-permute-start(bf16[128,256]{1,0:T(8,128)(2,1)S(1)} %get-tuple-element.63), channel_id=1, source_target_pairs={{0,32},{32,0},{64,96},{96,64},{128,160},{160,128},{192,224},{224,1... | collective-permute-start | bytes 196616 | tf_op jit(solution)/shard_map/ppermute | solution.py:235
  48.5 0.0 collective-permute-done.12.refs_1_
  48.5 0.2 collective-permute-done.14.refs_3_
  48.7 0.1 shard_map.122
  48.8 1.0 %collective-permute-start.15 = (bf16[64,256]{1,0:T(8,128)(2,1)S(1)}, bf16[64,256]{1,0:T(8,128)(2,1)S(1)}, u32[]{:S(2)}, u32[]{:S(2)}) collective-permute-start(bf16[64,256]{1,0:T(8,128)(2,1)S(1)} %get-tuple-element.53), channel_id=1, source_target_pairs={{0,4},{1,5},{2,6},{3,7},{4,0},{5,1},{6,2},{7,3},{8,12},{9,13},{10,... | collective-permute-start | bytes 98312 | tf_op jit(solution)/shard_map/ppermute | solution.py:235
  49.8 2.1 %collective-permute-start.16 = (bf16[64,256]{1,0:T(8,128)(2,1)S(1)}, bf16[64,256]{1,0:T(8,128)(2,1)S(1)}, u32[]{:S(2)}, u32[]{:S(2)}) collective-permute-start(bf16[64,256]{1,0:T(8,128)(2,1)S(1)} %get-tuple-element.54), channel_id=1, source_target_pairs={{0,6},{1,7},{2,4},{3,5},{4,2},{5,3},{6,0},{7,1},{8,14},{9,15},{10,... | collective-permute-start | bytes 98312 | tf_op jit(solution)/shard_map/ppermute | solution.py:235
  51.9 0.4 collective-permute-start.17
  52.4 2.9 %collective-permute-done.21.refs_1_ = bf16[128,256]{1,0:T(8,128)(2,1)S(1)} collective-permute-done((bf16[128,256]{1,0:T(8,128)(2,1)S(1)}, bf16[128,256]{1,0:T(8,128)(2,1)S(1)}, u32[]{:S(2)}, u32[]{:S(2)}) %collective-permute-start.21) | collective-permute-done | bytes 65568 | tf_op jit(solution)/shard_map/ppermute | solution.py:235
  55.2 0.9 %shard_map.125 = (f32[128,256]{1,0:T(8,128)}, f32[1,128]{1,0:T(1,128)}) custom-call(f32[128,256]{1,0:T(8,128)S(1)} %get-tuple-element.62.refs_0_, bf16[128,256]{1,0:T(8,128)(2,1)S(1)} %collective-permute-done.21.refs_1_, f32[128,256]{1,0:T(8,128)S(1)} %copy-done, f32[1,128]{1,0:T(1,128)S(1)} %bitcast.6), custom_call_target="tpu_custom_call" | custom-call | tf_op jit(solution)/shard_map/pallas_call | solution.py:18
  56.1 0.9 %shard_map.123 = (f32[64,256]{1,0:T(8,128)}, f32[1,64]{1,0:T(1,128)}) custom-call(f32[64,256]{1,0:T(8,128)S(1)} %get-tuple-element.52.refs_0_, bf16[64,256]{1,0:T(8,128)(2,1)S(1)} %collective-permute-done.15.refs_1_, bf16[64,256]{1,0:T(8,128)(2,1)S(1)} %collective-permute-done.16.refs_2_, bf16[64,256]{1,0:T(8,128)(2,1)S(1)} %collective-permute-done.17.refs_3_, ...), custom_call_target="tpu_custom_call" | custom-call | tf_op jit(solution)/shard_map/pallas_call | solution.py:18
  (19 shorter events, 0.1 us)
Async XLA Ops:
  1.6 1.3 %collective-permute-start = (bf16[128,256]{1,0:T(8,128)(2,1)S(1)}, bf16[128,256]{1,0:T(8,128)(2,1)S(1)}, u32[]{:S(2)}, u32[]{:S(2)}) collective-permute-start(bf16[128,256]{1,0:T(8,128)(2,1)S(1)} %get-tuple-element.37), channel_id=1, source_target_pairs={{0,1},{1,0},{2,3},{3,2},{4,5},{5,4},{6,7},{7,6},{8,9},{9,8},{10,11... | collective-permute-start | bytes 196616 | tf_op jit(solution)/shard_map/ppermute | solution.py:235
  3.0 10.3 %collective-permute-start.2 = (bf16[128,256]{1,0:T(8,128)(2,1)S(1)}, bf16[128,256]{1,0:T(8,128)(2,1)S(1)}, u32[]{:S(2)}, u32[]{:S(2)}) collective-permute-start(bf16[128,256]{1,0:T(8,128)(2,1)S(1)} %get-tuple-element.42.b), channel_id=1, source_target_pairs={{0,4},{1,33},{2,6},{3,35},{4,0},{5,37},{6,2},{7,39},{8,12},{9,41},... | collective-permute-start | bytes 196616 | tf_op jit(solution)/shard_map/ppermute | solution.py:246
  6.3 7.1 %collective-permute-start.3 = (bf16[128,256]{1,0:T(8,128)(2,1)S(1)}, bf16[128,256]{1,0:T(8,128)(2,1)S(1)}, u32[]{:S(2)}, u32[]{:S(2)}) collective-permute-start(bf16[128,256]{1,0:T(8,128)(2,1)S(1)} %get-tuple-element.38.refs_0_.a), channel_id=1, source_target_pairs={{0,6},{1,33},{2,4},{3,35},{4,2},{5,37},{6,0},{7,39},{8,14},{9,41},... | collective-permute-start | bytes 196616 | tf_op jit(solution)/shard_map/ppermute | solution.py:246
  7.8 8.3 %collective-permute-start.1 = (bf16[128,256]{1,0:T(8,128)(2,1)S(1)}, bf16[128,256]{1,0:T(8,128)(2,1)S(1)}, u32[]{:S(2)}, u32[]{:S(2)}) collective-permute-start(bf16[128,256]{1,0:T(8,128)(2,1)S(1)} %get-tuple-element.38.refs_0_.a), channel_id=1, source_target_pairs={{0,2},{2,0},{4,6},{6,4},{8,10},{10,8},{12,14},{14,12},{16,18},{18,... | collective-permute-start | bytes 196616 | tf_op jit(solution)/shard_map/ppermute | solution.py:246
  16.1 8.8 %collective-permute-start.4 = (bf16[512,256]{1,0:T(8,128)(2,1)S(1)}, bf16[512,256]{1,0:T(8,128)(2,1)S(1)}, u32[]{:S(2)}, u32[]{:S(2)}) collective-permute-start(bf16[512,256]{1,0:T(8,128)(2,1)S(1)} %shard_map.114.refs_0_.x), channel_id=1, source_target_pairs={{0,16},{1,129},{2,18},{3,131},{4,20},{5,133},{6,22},{7,135},{8,24}... | collective-permute-start | bytes 786440 | tf_op jit(solution)/shard_map/ppermute | solution.py:246
  19.4 7.9 %collective-permute-start.5 = (bf16[512,256]{1,0:T(8,128)(2,1)S(1)}, bf16[512,256]{1,0:T(8,128)(2,1)S(1)}, u32[]{:S(2)}, u32[]{:S(2)}) collective-permute-start(bf16[512,256]{1,0:T(8,128)(2,1)S(1)} %shard_map.114.refs_0_.x), channel_id=1, source_target_pairs={{0,8},{1,65},{2,10},{3,67},{4,12},{5,69},{6,14},{7,71},{8,0},{9,73... | collective-permute-start | bytes 786440 | tf_op jit(solution)/shard_map/ppermute | solution.py:246
  20.1 7.8 %collective-permute-start.6 = (bf16[512,256]{1,0:T(8,128)(2,1)S(1)}, bf16[512,256]{1,0:T(8,128)(2,1)S(1)}, u32[]{:S(2)}, u32[]{:S(2)}) collective-permute-start(bf16[512,256]{1,0:T(8,128)(2,1)S(1)} %shard_map.114.refs_0_.x), channel_id=1, source_target_pairs={{0,24},{1,193},{2,26},{3,195},{4,28},{5,197},{6,30},{7,199},{8,16}... | collective-permute-start | bytes 786440 | tf_op jit(solution)/shard_map/ppermute | solution.py:246
  24.0 4.1 %collective-permute-start.7 = (bf16[512,256]{1,0:T(8,128)(2,1)S(1)}, bf16[512,256]{1,0:T(8,128)(2,1)S(1)}, u32[]{:S(2)}, u32[]{:S(2)}) collective-permute-start(bf16[512,256]{1,0:T(8,128)(2,1)S(1)} %shard_map.116.refs_0_), channel_id=1, source_target_pairs={{0,1},{1,0},{2,3},{3,2},{4,5},{5,4},{6,7},{7,6},{8,9},{9,8},{10,11... | collective-permute-start | bytes 786440 | tf_op jit(solution)/shard_map/ppermute | solution.py:235
  25.0 3.1 %collective-permute-start.8 = (bf16[512,256]{1,0:T(8,128)(2,1)S(1)}, bf16[512,256]{1,0:T(8,128)(2,1)S(1)}, u32[]{:S(2)}, u32[]{:S(2)}) collective-permute-start(bf16[512,256]{1,0:T(8,128)(2,1)S(1)} %shard_map.117.refs_1_), channel_id=1, source_target_pairs={{0,1},{1,0},{2,3},{3,2},{4,5},{5,4},{6,7},{7,6},{8,9},{9,8},{10,11... | collective-permute-start | bytes 786440 | tf_op jit(solution)/shard_map/ppermute | solution.py:235
  27.3 1.7 %collective-permute-start.9 = (bf16[512,256]{1,0:T(8,128)(2,1)S(1)}, bf16[512,256]{1,0:T(8,128)(2,1)S(1)}, u32[]{:S(2)}, u32[]{:S(2)}) collective-permute-start(bf16[512,256]{1,0:T(8,128)(2,1)S(1)} %shard_map.118.refs_2_), channel_id=1, source_target_pairs={{0,1},{1,0},{2,3},{3,2},{4,5},{5,4},{6,7},{7,6},{8,9},{9,8},{10,11... | collective-permute-start | bytes 786440 | tf_op jit(solution)/shard_map/ppermute | solution.py:235
  27.9 1.6 %collective-permute-start.10 = (bf16[512,256]{1,0:T(8,128)(2,1)S(1)}, bf16[512,256]{1,0:T(8,128)(2,1)S(1)}, u32[]{:S(2)}, u32[]{:S(2)}) collective-permute-start(bf16[512,256]{1,0:T(8,128)(2,1)S(1)} %shard_map.119.refs_3_), channel_id=1, source_target_pairs={{0,1},{1,0},{2,3},{3,2},{4,5},{5,4},{6,7},{7,6},{8,9},{9,8},{10,11... | collective-permute-start | bytes 786440 | tf_op jit(solution)/shard_map/ppermute | solution.py:235
  29.5 25.7 %copy-start = (f32[128,256]{1,0:T(8,128)S(1)}, f32[128,256]{1,0:T(8,128)}, u32[]{:S(2)}) copy-start(f32[128,256]{1,0:T(8,128)} %refs_2_.1) | copy-start | bytes 393220
  29.5 25.7 %copy-start.2 = (f32[128]{0:T(128)S(1)}, f32[128]{0:T(128)}, u32[]{:S(2)}) copy-start(f32[128]{0:T(128)} %param.15) | copy-start | bytes 1540
  29.5 26.6 %copy-start.1 = (f32[64,256]{1,0:T(8,128)S(1)}, f32[64,256]{1,0:T(8,128)}, u32[]{:S(2)}) copy-start(f32[64,256]{1,0:T(8,128)} %refs_4_.1) | copy-start | bytes 196612
  29.5 26.6 %copy-start.3 = (f32[64]{0:T(128)S(1)}, f32[64]{0:T(128)}, u32[]{:S(2)}) copy-start(f32[64]{0:T(128)} %param.13) | copy-start | bytes 772
  34.1 4.5 %collective-permute-start.11 = (bf16[1024,256]{1,0:T(8,128)(2,1)S(1)}, bf16[1024,256]{1,0:T(8,128)(2,1)S(1)}, u32[]{:S(2)}, u32[]{:S(2)}) collective-permute-start(bf16[1024,256]{1,0:T(8,128)(2,1)S(1)} %get-tuple-element.47), channel_id=1, source_target_pairs={{0,1},{1,0},{2,3},{3,2},{4,5},{5,4},{6,7},{7,6},{8,9},{9,8},{10,11... | collective-permute-start | bytes 1572872 | tf_op jit(solution)/shard_map/ppermute | solution.py:235
  34.4 8.1 %collective-permute-start.18 = (bf16[256,256]{1,0:T(8,128)(2,1)S(1)}, bf16[256,256]{1,0:T(8,128)(2,1)S(1)}, u32[]{:S(2)}, u32[]{:S(2)}) collective-permute-start(bf16[256,256]{1,0:T(8,128)(2,1)S(1)} %get-tuple-element.59), channel_id=1, source_target_pairs={{0,128},{32,160},{64,192},{96,224},{128,0},{160,32},{192,64},{224,... | collective-permute-start | bytes 393224 | tf_op jit(solution)/shard_map/ppermute | solution.py:235
  36.4 8.9 %collective-permute-start.19 = (bf16[256,256]{1,0:T(8,128)(2,1)S(1)}, bf16[256,256]{1,0:T(8,128)(2,1)S(1)}, u32[]{:S(2)}, u32[]{:S(2)}) collective-permute-start(bf16[256,256]{1,0:T(8,128)(2,1)S(1)} %get-tuple-element.60), channel_id=1, source_target_pairs={{0,64},{32,96},{64,0},{96,32},{128,192},{160,224},{192,128},{224,1... | collective-permute-start | bytes 393224 | tf_op jit(solution)/shard_map/ppermute | solution.py:235
  37.8 7.4 %collective-permute-start.20 = (bf16[256,256]{1,0:T(8,128)(2,1)S(1)}, bf16[256,256]{1,0:T(8,128)(2,1)S(1)}, u32[]{:S(2)}, u32[]{:S(2)}) collective-permute-start(bf16[256,256]{1,0:T(8,128)(2,1)S(1)} %get-tuple-element.61), channel_id=1, source_target_pairs={{0,192},{32,224},{64,128},{96,160},{128,64},{160,96},{192,0},{224,... | collective-permute-start | bytes 393224 | tf_op jit(solution)/shard_map/ppermute | solution.py:235
  38.6 9.8 %collective-permute-start.12 = (bf16[256,256]{1,0:T(8,128)(2,1)S(1)}, bf16[256,256]{1,0:T(8,128)(2,1)S(1)}, u32[]{:S(2)}, u32[]{:S(2)}) collective-permute-start(bf16[256,256]{1,0:T(8,128)(2,1)S(1)} %get-tuple-element.49), channel_id=1, source_target_pairs={{0,16},{1,17},{2,18},{3,19},{4,20},{5,21},{6,22},{7,23},{8,24},{9,... | collective-permute-start | bytes 393224 | tf_op jit(solution)/shard_map/ppermute | solution.py:235
  41.9 6.6 %collective-permute-start.13 = (bf16[256,256]{1,0:T(8,128)(2,1)S(1)}, bf16[256,256]{1,0:T(8,128)(2,1)S(1)}, u32[]{:S(2)}, u32[]{:S(2)}) collective-permute-start(bf16[256,256]{1,0:T(8,128)(2,1)S(1)} %get-tuple-element.50), channel_id=1, source_target_pairs={{0,8},{1,9},{2,10},{3,11},{4,12},{5,13},{6,14},{7,15},{8,0},{9,1},... | collective-permute-start | bytes 393224 | tf_op jit(solution)/shard_map/ppermute | solution.py:235
  42.5 6.2 %collective-permute-start.14 = (bf16[256,256]{1,0:T(8,128)(2,1)S(1)}, bf16[256,256]{1,0:T(8,128)(2,1)S(1)}, u32[]{:S(2)}, u32[]{:S(2)}) collective-permute-start(bf16[256,256]{1,0:T(8,128)(2,1)S(1)} %get-tuple-element.51), channel_id=1, source_target_pairs={{0,24},{1,25},{2,26},{3,27},{4,28},{5,29},{6,30},{7,31},{8,16},{9,... | collective-permute-start | bytes 393224 | tf_op jit(solution)/shard_map/ppermute | solution.py:235
  45.3 9.9 %collective-permute-start.21 = (bf16[128,256]{1,0:T(8,128)(2,1)S(1)}, bf16[128,256]{1,0:T(8,128)(2,1)S(1)}, u32[]{:S(2)}, u32[]{:S(2)}) collective-permute-start(bf16[128,256]{1,0:T(8,128)(2,1)S(1)} %get-tuple-element.63), channel_id=1, source_target_pairs={{0,32},{32,0},{64,96},{96,64},{128,160},{160,128},{192,224},{224,1... | collective-permute-start | bytes 196616 | tf_op jit(solution)/shard_map/ppermute | solution.py:235
  48.8 7.3 %collective-permute-start.15 = (bf16[64,256]{1,0:T(8,128)(2,1)S(1)}, bf16[64,256]{1,0:T(8,128)(2,1)S(1)}, u32[]{:S(2)}, u32[]{:S(2)}) collective-permute-start(bf16[64,256]{1,0:T(8,128)(2,1)S(1)} %get-tuple-element.53), channel_id=1, source_target_pairs={{0,4},{1,5},{2,6},{3,7},{4,0},{5,1},{6,2},{7,3},{8,12},{9,13},{10,... | collective-permute-start | bytes 98312 | tf_op jit(solution)/shard_map/ppermute | solution.py:235
  49.8 6.3 %collective-permute-start.16 = (bf16[64,256]{1,0:T(8,128)(2,1)S(1)}, bf16[64,256]{1,0:T(8,128)(2,1)S(1)}, u32[]{:S(2)}, u32[]{:S(2)}) collective-permute-start(bf16[64,256]{1,0:T(8,128)(2,1)S(1)} %get-tuple-element.54), channel_id=1, source_target_pairs={{0,6},{1,7},{2,4},{3,5},{4,2},{5,3},{6,0},{7,1},{8,14},{9,15},{10,... | collective-permute-start | bytes 98312 | tf_op jit(solution)/shard_map/ppermute | solution.py:235
  51.9 4.2 %collective-permute-start.17 = (bf16[64,256]{1,0:T(8,128)(2,1)S(1)}, bf16[64,256]{1,0:T(8,128)(2,1)S(1)}, u32[]{:S(2)}, u32[]{:S(2)}) collective-permute-start(bf16[64,256]{1,0:T(8,128)(2,1)S(1)} %get-tuple-element.55), channel_id=1, source_target_pairs={{0,2},{1,3},{2,0},{3,1},{4,6},{5,7},{6,4},{7,5},{8,10},{9,11},{10,... | collective-permute-start | bytes 98312 | tf_op jit(solution)/shard_map/ppermute | solution.py:235
